TPU v7x, 128 devices: a whole 4x4x4 slice. The times are simulated.
128 devices in a mesh: dp: 2 (over core), ctx: 64 (over x, y, z).
Axes of the slice: x: 4, y: 4, z: 4, core: 2. Of those that a mesh axis runs over, the one named last changes fastest.
Arguments:
- tokens: bfloat16 [2, 8192, 640], P('dp', 'ctx'), may hold values from -16 to 16
- doc_lengths: int32 [2, 8], P('dp'), may hold values from 1 to 4160, as said below
- block_order: int32 [128], replicated, may hold values from 0 to 127, as said below
- attn_norm: bfloat16 [640], P(('dp', 'ctx')), may hold values from 0.25 to 1.75
- query_weight: bfloat16 [640, 1024], P(('dp', 'ctx')), may hold values from -0.25 to 0.25
- key_weight: bfloat16 [640, 256], P(('dp', 'ctx')), may hold values from -0.25 to 0.25
- value_weight: bfloat16 [640, 256], P(('dp', 'ctx')), may hold values from -0.25 to 0.25
- query_gain: bfloat16 [256], P(('dp', 'ctx')), may hold values from 0.25 to 1.75
- key_gain: bfloat16 [256], P(('dp', 'ctx')), may hold values from 0.25 to 1.75
- output_weight: bfloat16 [1024, 640], P(('dp', 'ctx')), may hold values from -0.1875 to 0.1875
- attn_post_norm: bfloat16 [640], P(('dp', 'ctx')), may hold values from 0.25 to 1.75
- ffn_norm: bfloat16 [640], P(('dp', 'ctx')), may hold values from 0.25 to 1.75
- gate_weight: bfloat16 [640, 2048], P(('dp', 'ctx')), may hold values from -0.25 to 0.25
- up_weight: bfloat16 [640, 2048], P(('dp', 'ctx')), may hold values from -0.25 to 0.25
- down_weight: bfloat16 [2048, 640], P(('dp', 'ctx')), may hold values from -0.125 to 0.125
- ffn_post_norm: bfloat16 [640], P(('dp', 'ctx')), may hold values from 0.25 to 1.75
- out_cot: bfloat16 [2, 8192, 640], P('dp', 'ctx'), may hold values from -6 to 6
Outputs:
- block_out: bfloat16 [2, 8192, 640], P('dp', 'ctx')
- tokens_grad: bfloat16 [2, 8192, 640], P('dp', 'ctx')
- attn_norm_grad: float32 [640], P(('dp', 'ctx'))
- query_grad: float32 [640, 1024], P(('dp', 'ctx'))
- key_grad: float32 [640, 256], P(('dp', 'ctx'))
- value_grad: float32 [640, 256], P(('dp', 'ctx'))
- query_gain_grad: float32 [256], P(('dp', 'ctx'))
- key_gain_grad: float32 [256], P(('dp', 'ctx'))
- output_grad: float32 [1024, 640], P(('dp', 'ctx'))
- attn_post_norm_grad: float32 [640], P(('dp', 'ctx'))
- ffn_norm_grad: float32 [640], P(('dp', 'ctx'))
- gate_grad: float32 [640, 2048], P(('dp', 'ctx'))
- up_grad: float32 [640, 2048], P(('dp', 'ctx'))
- down_grad: float32 [2048, 640], P(('dp', 'ctx'))
- ffn_post_norm_grad: float32 [640], P(('dp', 'ctx'))
Inputs may be any that keep to these rules, and one draw needn't show every extreme that they name: `doc_lengths`: in each row the lengths are positive and sum to 8192; the longest, 4160, is the row's first or last document. `block_order`: A permutation of the 128 block numbers; entries 2c and 2c + 1, the blocks that index c of ctx holds, sum to 127.
All inputs are finite; a program needn't handle non-finite values.
Results may differ from a plain program's by a relative error of at most 0.029.
Values may be sent and summed in bfloat16 or wider, within the bound.
A program may use at most 128 MiB of HBM per device.

v0:
```python
import jax
import jax.numpy as jnp
from jax import lax
from jax.sharding import PartitionSpec as P

EPSILON = 1e-06
ROPE_BASE = 1000000.0
MASKED = -1e30


def rms_scale(values, weights):
    return values * lax.rsqrt(jnp.mean(values * values, axis=-1, keepdims=True) + EPSILON) * weights


def rope_turn(vectors, places):
    halfway = vectors.shape[-1] // 2
    steps_up = jnp.arange(halfway, dtype=jnp.float32)
    frequency = ROPE_BASE ** (-2.0 * steps_up / vectors.shape[-1])
    angles = places.astype(jnp.float32)[:, None] * frequency[None, :]
    angles = jnp.concatenate([angles, angles], axis=-1)
    if vectors.ndim == 3:
        angles = angles[:, None, :]
    turned = jnp.concatenate([-vectors[..., halfway:], vectors[..., :halfway]], axis=-1)
    return vectors * jnp.cos(angles) + turned * jnp.sin(angles)


def pick_block(row_count):
    for candidate in (512, 256, 128):
        return candidate
    return row_count


def place_tables(lengths, block_order, seq_len, block_len):
    rows_all = jnp.arange(seq_len, dtype=jnp.int32)
    block_of = rows_all // block_len
    numbers = jnp.arange(block_order.shape[0], dtype=jnp.int32)
    picked = jnp.sum(
        jnp.where(block_of[:, None] == numbers[None, :], block_order[None, :], 0), axis=1
    )
    seq_place = picked * block_len + rows_all % block_len
    starts = jnp.cumsum(lengths) - lengths
    segment = jnp.sum((starts[None, 1:] <= seq_place[:, None]).astype(jnp.int32), axis=1)
    doc_numbers = jnp.arange(lengths.shape[0], dtype=jnp.int32)
    doc_start = jnp.sum(
        jnp.where(segment[:, None] == doc_numbers[None, :], starts[None, :], 0), axis=1
    )
    return (seq_place, segment, seq_place - doc_start)


def norm_back(values, weights, incoming):
    unused, pull = jax.vjp(rms_scale, values, weights)
    return pull(incoming)


def on_device(
    tokens,
    doc_lengths,
    block_order,
    attn_norm,
    query_weight,
    key_weight,
    value_weight,
    query_gain,
    key_gain,
    output_weight,
    attn_post_norm,
    ffn_norm,
    gate_weight,
    up_weight,
    down_weight,
    ffn_post_norm,
    out_cot,
):
    gathered = (
        lax.all_gather(attn_norm, ("dp", "ctx"), axis=0, tiled=True),
        lax.all_gather(query_weight, ("dp", "ctx"), axis=0, tiled=True),
        lax.all_gather(key_weight, ("dp", "ctx"), axis=0, tiled=True),
        lax.all_gather(value_weight, ("dp", "ctx"), axis=0, tiled=True),
        lax.all_gather(query_gain, ("dp", "ctx"), axis=0, tiled=True),
        lax.all_gather(key_gain, ("dp", "ctx"), axis=0, tiled=True),
        lax.all_gather(output_weight, ("dp", "ctx"), axis=0, tiled=True),
        lax.all_gather(attn_post_norm, ("dp", "ctx"), axis=0, tiled=True),
        lax.all_gather(ffn_norm, ("dp", "ctx"), axis=0, tiled=True),
        lax.all_gather(gate_weight, ("dp", "ctx"), axis=0, tiled=True),
        lax.all_gather(up_weight, ("dp", "ctx"), axis=0, tiled=True),
        lax.all_gather(down_weight, ("dp", "ctx"), axis=0, tiled=True),
        lax.all_gather(ffn_post_norm, ("dp", "ctx"), axis=0, tiled=True),
    )
    (
        gain_attn,
        w_query,
        w_key,
        w_value,
        gain_query,
        gain_key,
        w_output,
        gain_post_attn,
        gain_ffn,
        w_gate,
        w_up,
        w_down,
        gain_post_ffn,
    ) = gathered
    gain_attn = gain_attn.astype(jnp.float32)
    gain_query = gain_query.astype(jnp.float32)
    gain_key = gain_key.astype(jnp.float32)
    gain_post_attn = gain_post_attn.astype(jnp.float32)
    gain_ffn = gain_ffn.astype(jnp.float32)
    gain_post_ffn = gain_post_ffn.astype(jnp.float32)
    local_rows = tokens.shape[1]
    head_size = w_key.shape[1]
    heads_count = w_query.shape[1] // head_size
    seq_len = local_rows * lax.axis_size("ctx")
    block_len = local_rows // 2
    score_scale = float(head_size) ** (-0.5)
    seq_place, segment, position = place_tables(doc_lengths[0], block_order, seq_len, block_len)
    first_row = lax.axis_index("ctx") * local_rows
    my_place = lax.dynamic_slice_in_dim(seq_place, first_row, local_rows)
    my_segment = lax.dynamic_slice_in_dim(segment, first_row, local_rows)
    my_position = lax.dynamic_slice_in_dim(position, first_row, local_rows)

    def head_side(raw_values, gain_values):
        return rope_turn(rms_scale(raw_values, gain_values), my_position)

    inputs = tokens[0].astype(jnp.float32)
    normed = rms_scale(inputs, gain_attn).astype(jnp.bfloat16)
    query_raw = jnp.dot(normed, w_query, preferred_element_type=jnp.float32).reshape(
        local_rows, heads_count, head_size
    )
    key_raw = jnp.dot(normed, w_key, preferred_element_type=jnp.float32)
    value_raw = jnp.dot(normed, w_value, preferred_element_type=jnp.float32)
    query_rot = head_side(query_raw, gain_query).astype(jnp.bfloat16)
    key_rot = head_side(key_raw, gain_key).astype(jnp.bfloat16)
    key_value = jnp.concatenate([key_rot, value_raw.astype(jnp.bfloat16)], axis=1)
    all_kv = lax.all_gather(key_value, "ctx", axis=0, tiled=True)

    def block_scores(key_start, row_count):
        kv_block = lax.dynamic_slice_in_dim(all_kv, key_start, row_count)
        keys_part = kv_block[:, :head_size]
        values_part = kv_block[:, head_size:]
        raw_scores = (
            jnp.einsum("ihd,jd->hij", query_rot, keys_part, preferred_element_type=jnp.float32)
            * score_scale
        )
        key_place = lax.dynamic_slice_in_dim(seq_place, key_start, row_count)
        key_segment = lax.dynamic_slice_in_dim(segment, key_start, row_count)
        allowed = (key_segment[None, :] == my_segment[:, None]) & (
            key_place[None, :] <= my_place[:, None]
        )
        return (jnp.where(allowed[None], raw_scores, MASKED), keys_part, values_part)

    span_rows = pick_block(seq_len)
    block_steps = jnp.arange(seq_len // span_rows, dtype=jnp.int32)

    def total_step(carry, step_index):
        run_max, run_sum = carry
        scores, unused, unused_values = block_scores(step_index * span_rows, span_rows)
        new_max = jnp.maximum(run_max, jnp.max(scores, axis=2))
        run_sum = run_sum * jnp.exp(run_max - new_max) + jnp.sum(
            jnp.exp(scores - new_max[..., None]), axis=2
        )
        return ((new_max, run_sum), None)

    start_max = jnp.full((heads_count, local_rows), MASKED, jnp.float32)
    (run_max, run_sum), unused = lax.scan(
        total_step, (start_max, jnp.zeros_like(start_max)), block_steps
    )
    log_total = run_max + jnp.log(run_sum)
    zero_heads = jnp.zeros((local_rows, heads_count, head_size), jnp.float32)

    def value_step(carry, step_index):
        total, exact = carry
        scores, unused, values_part = block_scores(step_index * span_rows, span_rows)
        attn_probs = jnp.exp(scores - log_total[..., None])
        total = total + jnp.einsum(
            "hij,jd->ihd",
            attn_probs.astype(jnp.bfloat16),
            values_part,
            preferred_element_type=jnp.float32,
        )
        exact = exact + jnp.einsum(
            "hij,jd->ihd",
            attn_probs,
            values_part.astype(jnp.float32),
            precision=lax.Precision.HIGHEST,
        )
        return ((total, exact), None)

    (attn_sum, attn_exact), unused = lax.scan(value_step, (zero_heads, zero_heads), block_steps)
    attn_low = attn_sum.reshape(local_rows, heads_count * head_size).astype(jnp.bfloat16)
    proj_out = jnp.dot(attn_low, w_output, preferred_element_type=jnp.float32)
    middle = inputs + rms_scale(proj_out, gain_post_attn)
    ffn_in = rms_scale(middle, gain_ffn).astype(jnp.bfloat16)
    gate = jnp.dot(ffn_in, w_gate, preferred_element_type=jnp.float32)
    upper = jnp.dot(ffn_in, w_up, preferred_element_type=jnp.float32)

    def geglu(gate_in, upper_in):
        return jax.nn.gelu(gate_in, approximate=True) * upper_in

    hidden = geglu(gate, upper).astype(jnp.bfloat16)
    ffn_out = jnp.dot(hidden, w_down, preferred_element_type=jnp.float32)
    block_out = (middle + rms_scale(ffn_out, gain_post_ffn)).astype(jnp.bfloat16)
    grad_out = out_cot[0].astype(jnp.float32)
    grad_ffn_out, post_ffn_term = norm_back(ffn_out, gain_post_ffn, grad_out)
    ffn_out_low = grad_ffn_out.astype(jnp.bfloat16)
    down_term = jnp.einsum("tf,td->fd", hidden, ffn_out_low, preferred_element_type=jnp.float32)
    grad_hidden = jnp.einsum("td,fd->tf", ffn_out_low, w_down, preferred_element_type=jnp.float32)
    unused, pull_geglu = jax.vjp(geglu, gate, upper)
    grad_gate, grad_upper = pull_geglu(grad_hidden)
    grad_gate = grad_gate.astype(jnp.bfloat16)
    grad_upper = grad_upper.astype(jnp.bfloat16)
    gate_term = jnp.einsum("td,tf->df", ffn_in, grad_gate, preferred_element_type=jnp.float32)
    upper_term = jnp.einsum("td,tf->df", ffn_in, grad_upper, preferred_element_type=jnp.float32)
    grad_ffn_in = jnp.einsum(
        "tf,df->td", grad_gate, w_gate, preferred_element_type=jnp.float32
    ) + jnp.einsum("tf,df->td", grad_upper, w_up, preferred_element_type=jnp.float32)
    grad_middle_norm, ffn_norm_term = norm_back(middle, gain_ffn, grad_ffn_in)
    grad_middle = grad_out + grad_middle_norm
    grad_proj, post_attn_term = norm_back(proj_out, gain_post_attn, grad_middle)
    proj_low = grad_proj.astype(jnp.bfloat16)
    out_term = jnp.einsum("tq,td->qd", attn_low, proj_low, preferred_element_type=jnp.float32)
    grad_attn = jnp.einsum("td,qd->tq", proj_low, w_output, preferred_element_type=jnp.float32)
    grad_attn = grad_attn.astype(jnp.bfloat16).reshape(local_rows, heads_count, head_size)
    row_dot = jnp.transpose(jnp.sum(grad_attn.astype(jnp.float32) * attn_exact, axis=2))

    def key_block(key_start, row_count):
        scores, keys_part, values_part = block_scores(key_start, row_count)
        attn_probs = jnp.exp(scores - log_total[..., None])
        grad_probs = jnp.einsum(
            "ihd,jd->hij", grad_attn, values_part, preferred_element_type=jnp.float32
        )
        grad_scores = (attn_probs * (grad_probs - row_dot[..., None])).astype(jnp.bfloat16)
        return (attn_probs, grad_scores, keys_part)

    def kv_terms(attn_probs, grad_scores):
        key_term = (
            jnp.einsum("hij,ihd->jd", grad_scores, query_rot, preferred_element_type=jnp.float32)
            * score_scale
        )
        value_term = jnp.einsum(
            "hij,ihd->jd",
            attn_probs.astype(jnp.bfloat16),
            grad_attn,
            preferred_element_type=jnp.float32,
        )
        return jnp.concatenate([key_term, value_term], axis=1)

    def grad_step(total, step_index):
        attn_probs, grad_scores, keys_part = key_block(step_index * span_rows, span_rows)
        total = (
            total
            + jnp.einsum("hij,jd->ihd", grad_scores, keys_part, preferred_element_type=jnp.float32)
            * score_scale
        )
        return (total, kv_terms(attn_probs, grad_scores))

    grad_query_rot, kv_pieces = lax.scan(grad_step, zero_heads, block_steps)
    kv_grad = lax.psum_scatter(
        kv_pieces.reshape(seq_len, 2 * head_size), "ctx", scatter_dimension=0, tiled=True
    )
    unused, pull_query = jax.vjp(head_side, query_raw, gain_query)
    grad_query_raw, query_gain_term = pull_query(grad_query_rot)
    unused, pull_key = jax.vjp(head_side, key_raw, gain_key)
    grad_key_raw, key_gain_term = pull_key(kv_grad[:, :head_size])
    query_low = grad_query_raw.reshape(local_rows, heads_count * head_size).astype(jnp.bfloat16)
    key_low = grad_key_raw.astype(jnp.bfloat16)
    value_low = kv_grad[:, head_size:].astype(jnp.bfloat16)
    query_term = jnp.einsum("td,tq->dq", normed, query_low, preferred_element_type=jnp.float32)
    key_term = jnp.einsum("td,tq->dq", normed, key_low, preferred_element_type=jnp.float32)
    value_term = jnp.einsum("td,tq->dq", normed, value_low, preferred_element_type=jnp.float32)
    grad_normed = (
        jnp.einsum("tq,dq->td", query_low, w_query, preferred_element_type=jnp.float32)
        + jnp.einsum("tq,dq->td", key_low, w_key, preferred_element_type=jnp.float32)
        + jnp.einsum("tq,dq->td", value_low, w_value, preferred_element_type=jnp.float32)
    )
    grad_inputs, attn_norm_term = norm_back(inputs, gain_attn, grad_normed)
    tokens_grad = (grad_middle + grad_inputs).astype(jnp.bfloat16)
    sums = tuple(
        (
            lax.psum_scatter(attn_norm_term, ("dp", "ctx"), scatter_dimension=0, tiled=True),
            lax.psum_scatter(query_term, ("dp", "ctx"), scatter_dimension=0, tiled=True),
            lax.psum_scatter(key_term, ("dp", "ctx"), scatter_dimension=0, tiled=True),
            lax.psum_scatter(value_term, ("dp", "ctx"), scatter_dimension=0, tiled=True),
            lax.psum_scatter(query_gain_term, ("dp", "ctx"), scatter_dimension=0, tiled=True),
            lax.psum_scatter(key_gain_term, ("dp", "ctx"), scatter_dimension=0, tiled=True),
            lax.psum_scatter(out_term, ("dp", "ctx"), scatter_dimension=0, tiled=True),
            lax.psum_scatter(post_attn_term, ("dp", "ctx"), scatter_dimension=0, tiled=True),
            lax.psum_scatter(ffn_norm_term, ("dp", "ctx"), scatter_dimension=0, tiled=True),
            lax.psum_scatter(gate_term, ("dp", "ctx"), scatter_dimension=0, tiled=True),
            lax.psum_scatter(upper_term, ("dp", "ctx"), scatter_dimension=0, tiled=True),
            lax.psum_scatter(down_term, ("dp", "ctx"), scatter_dimension=0, tiled=True),
            lax.psum_scatter(post_ffn_term, ("dp", "ctx"), scatter_dimension=0, tiled=True),
        )
    )
    return (block_out[None], tokens_grad[None]) + sums


def solution(mesh):
    placed = (
        P("dp", "ctx", None),
        P("dp", None),
        P(),
        P(("dp", "ctx")),
        P(("dp", "ctx"), None),
        P(("dp", "ctx"), None),
        P(("dp", "ctx"), None),
        P(("dp", "ctx")),
        P(("dp", "ctx")),
        P(("dp", "ctx"), None),
        P(("dp", "ctx")),
        P(("dp", "ctx")),
        P(("dp", "ctx"), None),
        P(("dp", "ctx"), None),
        P(("dp", "ctx"), None),
        P(("dp", "ctx")),
        P("dp", "ctx", None),
    )
    return jax.shard_map(
        on_device,
        mesh=mesh,
        in_specs=placed,
        out_specs=(
            P("dp", "ctx", None),
            P("dp", "ctx", None),
            P(("dp", "ctx")),
            P(("dp", "ctx"), None),
            P(("dp", "ctx"), None),
            P(("dp", "ctx"), None),
            P(("dp", "ctx")),
            P(("dp", "ctx")),
            P(("dp", "ctx"), None),
            P(("dp", "ctx")),
            P(("dp", "ctx")),
            P(("dp", "ctx"), None),
            P(("dp", "ctx"), None),
            P(("dp", "ctx"), None),
            P(("dp", "ctx")),
        ),
        check_vma=False,
    )
```

profile of v0, /device:TPU:0, one launch (start us, length us, event | category | flops | bytes accessed | tf_op | source)
XLA Modules:
  0.0 2455.0 jit_solution(18210376181095498545)
XLA Ops:
  9.5 321.8 %all-gather.1 = bf16[128,5,256]{2,1,0:T(8,128)(2,1)S(1)} all-gather(bf16[1,5,256]{2,1,0:T(8,128)(2,1)} %bitcast.265), channel_id=1, replica_groups=mesh['dp'=2,'ctx'=64] {'dp','ctx'}, dimensions={0}, use_global_device_ids=true | all-gather | bytes 330240 | tf_op jit(solution)/shard_map/all_gather | solution.py:78
  336.5 62.4 %all-reduce.24 = (bf16[640]{0:T(1024)(128)(2,1)S(1)}, bf16[256]{0:T(256)(128)(2,1)S(1)}, bf16[256]{0:T(256)(128)(2,1)S(1)}, bf16[640]{0:T(1024)(128)(2,1)S(1)}, ...) all-reduce(bf16[640]{0:T(1024)(128)(2,1)S(1)} %dynamic-update-slice, ...), channel_id=1, replica_groups=mesh['dp'=2,'ctx'=64] {'dp','ctx'}, use_global_device_ids=true, to_apply=%add.4 | all-reduce | flops 3072 | bytes 12288
  398.9 315.4 %all-gather = bf16[128,5,256]{2,1,0:T(8,128)(2,1)S(1)} all-gather(bf16[1,5,256]{2,1,0:T(8,128)(2,1)} %bitcast.266), channel_id=1, replica_groups=mesh['dp'=2,'ctx'=64] {'dp','ctx'}, dimensions={0}, use_global_device_ids=true | all-gather | bytes 330240 | tf_op jit(solution)/shard_map/all_gather | solution.py:77
  714.9 2.6 select_reduce_fusion
  718.0 1.5 convert_reduce_fusion
  727.5 2.6 reshape.489
  730.2 1.5 copy.95
  731.7 1.9 multiply_reduce_fusion.3
  735.5 5.6 reshape.491
  741.1 5.6 reshape.493
  746.7 50.3 %all-gather.12.cloned.1.call-done = bf16[8192,512]{1,0:T(8,128)(2,1)} async-done(((bf16[128,512]{1,0:T(8,128)(2,1)}), bf16[8192,512]{1,0:T(8,128)(2,1)}) %all-gather.12.cloned.1.call-update) | async-done | bytes 8388624 | tf_op jit(solution)/shard_map/all_gather | solution.py:135
  797.0 72.1 %while.39 = (s32[]{:T(128)}, f32[4,128]{1,0:T(4,128)S(1)}, f32[4,128]{1,0:T(4,128)S(1)}, s32[16]{0:T(128)S(1)}, s32[8192]{0:T(1024)}, /*index=5*/s32[128]{0:T(12...) while((s32[]{:T(128)}, f32[4,128]{1,0:T(4,128)S(1)}, ...), condition=%wide.region_10.11_spmd.clone, body=%wide.region_7.10_spmd.clone.sunk | while | flops 135727616 | bytes 2792670 | solution.py:165
  869.7 120.1 %while.40 = (s32[]{:T(128)}, f32[128,4,256]{0,2,1:T(8,128)S(1)}, f32[128,4,256]{0,2,1:T(8,128)S(1)}, s32[16]{0:T(128)S(1)}, bf16[8192,512]{1,0:T(8,128)(2,1)}, /...) while((s32[]{:T(128)}, f32[128,4,256]{0,2,1:T(8,128)S(1)}, ...), condition=%wide.region_12.13_spmd.clone, body=%wide.region_11.12_spmd.clone.sunk | while | flops 1075511296 | bytes 6438154 | solution.py:189
  875.4 1.8 fusion.174
  882.9 1.8 fusion.174
  890.4 1.8 fusion.174
  897.9 1.8 fusion.174
  905.4 1.8 fusion.174
  912.9 1.8 fusion.174
  920.5 1.8 fusion.174
  928.0 1.8 fusion.174
  935.5 1.8 fusion.174
  943.0 1.8 fusion.174
  950.5 1.8 fusion.174
  958.0 1.8 fusion.174
  965.5 1.8 fusion.174
  973.0 1.8 fusion.174
  980.5 1.8 fusion.174
  988.0 1.8 fusion.174
  990.7 2.0 multiply_reduce_fusion.10
  996.8 1.9 multiply_convert_fusion.1
  998.7 2.7 multiply_reduce_fusion.8
  1001.5 1.7 fusion.55
  1003.2 1.8 fusion.51
  1007.8 1.6 multiply_reduce_fusion.4
  1013.1 155.9 %while.41 = (s32[]{:T(128)}, f32[128,4,256]{0,2,1:T(8,128)S(1)}, f32[16,512,512]{2,1,0:T(8,128)}, s32[16]{0:T(128)}, bf16[8192,512]{1,0:T(8,128)(2,1)}, /*index=...) while((s32[]{:T(128)}, f32[128,4,256]{0,2,1:T(8,128)S(1)}, ...), condition=%wide.region_21.22_spmd.clone, body=%wide.region_20.21_spmd.clone.sunk | while | flops 673906688 | bytes 15090969 | solution.py:257
  1171.0 2.0 fusion.99
  1173.0 2.2 fusion.60
  1175.2 3.2 fusion.100
  1178.4 3.3 fusion.101
  1181.7 375.8 %reduce-scatter.3.cloned.1.call-done = f32[128,512]{1,0:T(8,128)} async-done(((f32[8192,512]{1,0:T(8,128)}), f32[128,512]{1,0:T(8,128)}) %reduce-scatter.3.cloned.1.call-update) | async-done | bytes 262160 | tf_op jit(solution)/shard_map/reduce_scatter | solution.py:258
  1561.4 2.1 fusion.77
  1564.6 3.4 fusion.102
  1570.6 63.4 %all-reduce.22 = (f32[640]{0:T(1024)S(1)}, f32[256]{0:T(256)S(1)}, f32[256]{0:T(256)S(1)}, f32[640]{0:T(1024)S(1)}, f32[640]{0:T(1024)S(1)}, /*index=5*/f32[640]{0:T(1024)S(1)}) all-reduce(f32[640]{0:T(1024)S(1)} %get-tuple-element.371, f32[256]{0:T(256)S(1)} %get-tuple-element.363, ...), channel_id=3, replica_groups=mesh['dp'=2,'ctx'=64] {'dp','ctx'}, use_global_device_ids=true, to_apply=%region_27.28.clone | all-reduce | flops 3072 | bytes 24576
  1638.3 142.3 %all-reduce.27.cloned.1.call-done = (f32[640,1024]{1,0:T(8,128)}, f32[640,256]{1,0:T(8,128)}, f32[640,256]{1,0:T(8,128)}, f32[1024,640]{1,0:T(8,128)}, f32[640,2048]{1,0:T(8,128)}, /*index=5*/f32[640,2048]{1,0:T(8,128)}) async-done(((f32[640,1024]{1,0:T(8,128)}, f32[640,256]{1,0:T(8,128)}, f32[640,256]{1,0:T(8,128)}, f32[1024,640]{1,0:T(8,128)}, f32[640,2048]{1,0:T(8,128)}, ...) | async-done | bytes 17039376
  1786.1 1.5 constant_dynamic-slice_fusion.1
  1787.6 1.5 constant_dynamic-slice_fusion
  1789.1 659.3 %reduce-scatter.5.cloned.1.call-done = f32[16,640]{1,0:T(8,128)} async-done(((f32[2048,640]{1,0:T(8,128)}), f32[16,640]{1,0:T(8,128)}) %reduce-scatter.5.cloned.1.call-update) | async-done | bytes 40976 | tf_op jit(solution)/shard_map/reduce_scatter | solution.py:291
  (704 shorter events, 334.1 us)
Async XLA Ops:
  7.2 707.4 %copy-start.72 = (s32[1,8]{1,0:T(1,128)S(1)}, s32[1,8]{1,0:T(1,128)}, u32[]{:S(2)}) copy-start(s32[1,8]{1,0:T(1,128)} %param.24) | copy-start | bytes 100
  7.2 707.7 %copy-start.65 = (s32[128]{0:T(128)S(1)}, s32[128]{0:T(128)}, u32[]{:S(2)}) copy-start(s32[128]{0:T(128)} %param.25) | copy-start | bytes 1540
  7.2 714.1 %copy-start.9 = (bf16[1,128,640]{2,1,0:T(8,128)(2,1)S(1)}, bf16[1,128,640]{2,1,0:T(8,128)(2,1)}, u32[]{:S(2)}) copy-start(bf16[1,128,640]{2,1,0:T(8,128)(2,1)} %param.23) | copy-start | bytes 491524
  7.2 720.3 %all-gather.18.cloned.1.call-start = ((), (), s32[]{:S(2)}) async-start(), calls=%async_computation.7 | async-start | bytes 2113536 | tf_op jit(solution)/shard_map/all_gather | solution.py:76
  7.9 727.5 %all-gather.20.cloned.1.call-start = ((), (), s32[]{:S(2)}) async-start(), calls=%async_computation.8 | async-start | bytes 4227072 | tf_op jit(solution)/shard_map/all_gather | solution.py:84
  8.7 732.4 %all-gather.22.cloned.1.call-start = ((), (), s32[]{:S(2)}) async-start(), calls=%async_computation.9 | async-start | bytes 4227072 | tf_op jit(solution)/shard_map/all_gather | solution.py:85
  9.4 787.6 %all-gather.12.cloned.1.call-start = ((), (), s32[]{:S(2)}) async-start(), calls=%async_computation.2 | async-start | bytes 8519680 | tf_op jit(solution)/shard_map/all_gather | solution.py:135
  331.4 394.1 %copy-start.35 = (bf16[640,256]{1,0:T(8,128)(2,1)}, bf16[640,256]{1,0:T(8,128)(2,1)S(1)}, u32[]{:S(2)}) copy-start(bf16[640,256]{1,0:T(8,128)(2,1)S(1)} %reshape.487) | copy-start | bytes 983044
  714.5 10.9 copy-start.33
  714.5 15.6 copy-start.52
  721.4 10.3 copy-start.48
  722.0 4.3 copy-start.59
  723.1 10.8 copy-start.37
  723.1 10.8 copy-start.39
  724.1 265.8 %all-gather.14.cloned.1.call-start = ((), (), s32[]{:S(2)}) async-start(), calls=%async_computation.3 | async-start | bytes 1320960 | tf_op jit(solution)/shard_map/all_gather | solution.py:81
  724.7 274.1 %all-gather.16.cloned.1.call-start = ((), (), s32[]{:S(2)}) async-start(), calls=%async_computation.4 | async-start | bytes 2641920 | tf_op jit(solution)/shard_map/all_gather | solution.py:86
  725.2 832.3 %reduce-scatter.3.cloned.1.call-start = ((), (), s32[]{:S(2)}) async-start(), calls=%async_computation.5 | async-start | bytes 17039360 | tf_op jit(solution)/shard_map/reduce_scatter | solution.py:258
  726.3 7.6 copy-start.54
  730.2 3.7 copy-start.7
  733.7 7.4 copy-start.50
  733.7 7.4 copy-start.46
  989.9 5.3 copy-start.1
  992.7 4.1 copy-start
  998.7 4.4 copy-start.12
  998.7 6.2 copy-start.18
  998.7 6.2 copy-start.21
  998.7 6.2 copy-start.42
  1006.3 3.0 copy-start.24
  1006.3 3.0 copy-start.26
  1007.7 2.5 copy-start.69
  1007.8 4.1 copy-start.14
  1009.4 3.2 copy-start.4
  1009.4 3.7 copy-start.10
  1169.1 611.5 %all-reduce.27.cloned.1.call-start = ((), (), s32[]{:S(2)}) async-start(), calls=%async_computation.10 | async-start | bytes 34078720
  1170.4 2.6 copy-start.49
  1171.0 4.2 copy-start.27
  1175.2 3.2 copy-start.25
  1178.4 380.5 %copy-start.29 = (f32[128,256]{1,0:T(8,128)S(1)}, f32[128,256]{1,0:T(8,128)}, u32[]{:S(2)}) copy-start(f32[128,256]{1,0:T(8,128)} %copy-done.28) | copy-start | bytes 393220
  1178.4 380.5 %copy-start.53 = (f32[256]{0:T(256)S(1)}, f32[256]{0:T(256)}, u32[]{:S(2)}) copy-start(f32[256]{0:T(256)} %copy-done.52) | copy-start | bytes 3076
  1178.4 380.5 %copy-start.60 = (f32[128]{0:T(128)S(1)}, f32[128]{0:T(128)}, u32[]{:S(2)}) copy-start(f32[128]{0:T(128)} %copy-done.59) | copy-start | bytes 1540
  1178.4 381.7 %copy-start.74 = (f32[128]{0:T(128)S(1)}, f32[128]{0:T(128)}, u32[]{:S(2)}) copy-start(f32[128]{0:T(128)} %copy-done.73) | copy-start | bytes 1540
  1563.6 884.9 %reduce-scatter.5.cloned.1.call-start = ((), (), s32[]{:S(2)}) async-start(), calls=%async_computation.6 | async-start | bytes 5283840 | tf_op jit(solution)/shard_map/reduce_scatter | solution.py:291
  1568.1 2.1 copy-start.36
  1568.1 2.5 copy-start.56
  1568.1 2.5 copy-start.57
  1568.1 2.5 copy-start.58
  1568.1 69.4 %copy-start.67 = (f32[128]{0:T(128)S(1)}, f32[128]{0:T(128)}, u32[]{:S(2)}) copy-start(f32[128]{0:T(128)} %copy-done.66) | copy-start | bytes 1540
  1568.1 69.4 %copy-start.20 = (f32[128,640]{1,0:T(8,128)S(1)}, f32[128,640]{1,0:T(8,128)}, u32[]{:S(2)}) copy-start(f32[128,640]{1,0:T(8,128)} %copy-done.19) | copy-start | bytes 983044
  (36 other events, 39.0 us)
Sparse Core Ops, SparseCore 0:
  11.0 67.6 all-gather.17
  81.9 64.3 all-gather.19
  149.5 64.4 all-gather.21
  724.2 72.7 all-gather.11
  799.7 63.4 all-gather.13
  866.2 63.1 all-gather.15
  1169.2 388.3 reduce-scatter.2
  1563.9 216.6 all-reduce.26
  1783.6 664.8 reduce-scatter.4
where the time goes:
time: 2460 us
  waiting for transfers between devices  1230 us (50%)
  blocking collectives  763 us (31%)
  matrix products  199 us (8%)
  local copies, waits for them, and re-layouts  179 us (7%)
  loops' own time  34.2 us (1%)
  other arithmetic  33.6 us (1%)
    reduce_scatter x1, waiting for transfers between devices, on_device(): lax.psum_scatter(down_term, ('dp', 'ctx'), scatter_dimension=0, tiled=True)  659 us
    reduce_scatter x1, waiting for transfers between devices, on_device(): lax.psum_scatter(kv_pieces.reshape(seq_len, 2 * head_size), 'ctx', scatte...  376 us
    all_gather x1, blocking collectives, on_device(): lax.all_gather(value_weight, ('dp', 'ctx'), axis=0, tiled=True)  322 us
    all_gather x1, blocking collectives, on_device(): lax.all_gather(key_weight, ('dp', 'ctx'), axis=0, tiled=True)  315 us
    unnamed x10, waiting for transfers between devices  145 us
    unnamed x2, blocking collectives  126 us
    dot_general x48, matrix products, block_scores(): jnp.einsum('ihd,jd->hij', query_rot, keys_part, preferred_element_type=jn...  63.4 us
    all_gather x1, waiting for transfers between devices, on_device(): all_kv = lax.all_gather(key_value, 'ctx', axis=0, tiled=True)  50.3 us
  transfers between devices with their start and end apart: 9, of which 4 were waited for; matrix products, arithmetic and copies ran while one was open for 10% of the time, Pallas kernels for 0%

commit v1 on v0

v1 whole, which is shorter than its diff:
```python
import functools

import jax
import jax.numpy as jnp
from jax import lax
from jax.experimental import pallas as pl
from jax.experimental.pallas import tpu as pltpu
from jax.sharding import PartitionSpec as P

EPSILON = 1e-06
ROPE_BASE = 1000000.0
MESH = pl.DeviceIdType.MESH
F32 = jnp.float32
BF16 = jnp.bfloat16
MIB = 2**20

X, Y, Z = 0, 1, 2
ORDERS = ((Z, Y, X), (X, Z, Y), (Y, X, Z))
KV_ROWS = ((0, 80), (80, 80), (160, 96))
HEADS = 4
HEAD = 256
SCALE = HEAD**-0.5
LOG2E = 1.4426950408889634


def place():
    chip = lax.axis_index("ctx")
    return (chip // 16, (chip // 4) % 4, chip % 4)


def shifted(value, step):
    return lax.rem(value + step + 4, 4)


def peer(axis, step):
    spot = list(place())
    spot[axis] = shifted(spot[axis], step)
    return (lax.axis_index("dp"), spot[0] * 16 + spot[1] * 4 + spot[2])


def other_core():
    return (1 - lax.axis_index("dp"), lax.axis_index("ctx"))


def greet():
    barrier = pltpu.get_barrier_semaphore()
    for axis in (X, Y, Z):
        for step in (1, 2, 3):
            pl.semaphore_signal(barrier, inc=1, device_id=peer(axis, step), device_id_type=MESH)
    pl.semaphore_signal(barrier, inc=1, device_id=other_core(), device_id_type=MESH)
    pl.semaphore_wait(barrier, 10)


class Links:
    def __init__(self, send, recv):
        self.send, self.recv, self.used, self.sent = send, recv, 0, []

    def copy(self, number, src, dst, device):
        return pltpu.make_async_remote_copy(
            src_ref=src,
            dst_ref=dst,
            send_sem=self.send.at[number],
            recv_sem=self.recv.at[number],
            device_id=device,
            device_id_type=MESH,
        )

    def start(self, src, dst, device):
        number = self.used
        self.used += 1
        copy = self.copy(number, src, dst, device)
        copy.start()
        self.sent.append(copy)
        return number

    def ring(self, axis, src_of, dst_of):
        mine = place()[axis]
        numbers = [
            self.start(src_of(step), dst_of(step, mine), peer(axis, step)) for step in (1, 2, 3)
        ]

        def wait(step):
            self.copy(
                numbers[step - 1],
                src_of(step),
                dst_of(step, shifted(mine, -step)),
                peer(axis, step),
            ).wait_recv()

        return wait

    def across(self, src, dst_of):
        mine = lax.axis_index("dp")
        number = self.start(src, dst_of(mine), other_core())

        def wait():
            self.copy(number, src, dst_of(1 - mine), other_core()).wait_recv()

        return wait

    def close(self):
        for copy in self.sent:
            copy.wait_send()


def all_steps(wait):
    for step in (1, 2, 3):
        wait(step)


VMEM = pl.BlockSpec(memory_space=pltpu.VMEM)
SMEM = pl.BlockSpec(memory_space=pltpu.SMEM)
ANY = pl.BlockSpec(memory_space=pl.ANY)


def link_call(kernel, number, semaphores, outs, ins, in_specs, out_specs, scratch=(), local=0):
    return pl.pallas_call(
        kernel,
        out_shape=[jax.ShapeDtypeStruct(shape, kind) for shape, kind in outs],
        in_specs=in_specs,
        out_specs=out_specs,
        scratch_shapes=[pltpu.VMEM(shape, kind) for shape, kind in scratch]
        + [pltpu.SemaphoreType.DMA((semaphores,)), pltpu.SemaphoreType.DMA((semaphores,))]
        + ([pltpu.SemaphoreType.DMA((local,))] if local else []),
        compiler_params=pltpu.CompilerParams(
            collective_id=number, has_side_effects=True, vmem_limit_bytes=60 * MIB
        ),
    )(*ins)


def early_kernel(a_ref, b_ref, c_ref, kvg_ref, pa_ref, pb_ref, pc_ref, u0_ref, u1_ref, send, recv):
    links = Links(send, recv)
    core = lax.axis_index("dp")
    spot = place()
    planes = (pa_ref, pb_ref, pc_ref)
    for part, own in enumerate((a_ref, b_ref, c_ref)):
        first, second, _ = ORDERS[part]
        planes[part][spot[second], spot[first]] = own[...]
    x, y, z = spot
    u0_ref[core, x, y, z] = kvg_ref[0:16]
    u1_ref[core, y, z, x] = kvg_ref[16:32]
    greet()

    def small(axis, unit, index_of):
        ref = (u0_ref, u1_ref)[unit]
        return links.ring(
            axis, lambda step: ref.at[index_of(spot[axis])], lambda step, at: ref.at[index_of(at)]
        )

    w0 = small(Z, 0, lambda at: (core, x, y, at))
    w1 = small(X, 1, lambda at: (core, y, z, at))
    waits = []
    for part in range(3):
        first, second, _ = ORDERS[part]
        ref, row = planes[part], spot[second]
        waits.append(
            links.ring(
                first,
                lambda step, ref=ref, row=row, first=first: ref.at[row, spot[first]],
                lambda step, at, ref=ref, row=row: ref.at[row, at],
            )
        )
    all_steps(w0)
    w0 = small(Y, 0, lambda at: (core, x, at))
    all_steps(w1)
    w1 = small(Z, 1, lambda at: (core, y, at))
    seconds = []
    for part in range(3):
        all_steps(waits[part])
        second = ORDERS[part][1]
        ref = planes[part]
        seconds.append(
            links.ring(
                second,
                lambda step, ref=ref, second=second: ref.at[spot[second]],
                lambda step, at, ref=ref: ref.at[at],
            )
        )
    all_steps(w0)
    w0 = small(X, 0, lambda at: (core, at))
    all_steps(w1)
    w1 = small(Y, 1, lambda at: (core, at))
    all_steps(w0)
    c0 = links.across(u0_ref.at[core], lambda at: u0_ref.at[at])
    all_steps(w1)
    c1 = links.across(u1_ref.at[core], lambda at: u1_ref.at[at])
    for wait in seconds:
        all_steps(wait)
    c0()
    c1()
    links.close()


def early(a, b, c, kvg):
    outs = [
        ((4, 4) + a.shape, BF16),
        ((4, 4) + b.shape, BF16),
        ((4, 4) + c.shape, BF16),
        ((2, 4, 4, 4, 16, 128), BF16),
        ((2, 4, 4, 4, 16, 128), BF16),
    ]
    return link_call(early_kernel, 1, 40, outs, (a, b, c, kvg), [VMEM] * 4, [VMEM] * 5)


def of_plane(ref, axis, at, *rest):
    index = [slice(None)] * 3
    index[axis] = at
    return ref.at[(*index, *rest)]


def chip_of(spot, axis, step):
    spot = list(spot)
    spot[axis] = shifted(spot[axis], step)
    return spot[0] * 16 + spot[1] * 4 + spot[2]


WEIGHTS = ((0, False), (0, False), (1, False), (1, False), (2, True))


def weight_plane(ref, part, by_chip, core, at):
    if by_chip:
        return of_plane(ref.at[core], ORDERS[part][2], at)
    return ref.at[core, at]


def plane_loop(part, body):
    first, second, last = ORDERS[part]

    def step(number, unused):
        spot = [None] * 3
        spot[first], spot[second], spot[last] = number % 4, number // 4, place()[last]
        body(spot, number // 4, number % 4)
        return unused

    lax.fori_loop(0, 16, step, 0)


def gather_kernel(*refs):
    b_ref, kv_ref, gp, op, up, qp, dp = refs[:7]
    s_ref, extra_ref, gw, ow, uw, qw, dw = refs[7:14]
    f1, g, sel, special, rsp = (refs[14 + 3 * i : 17 + 3 * i] for i in range(5))
    send, recv, local = refs[29:]
    links = Links(send, recv)
    core = lax.axis_index("dp")
    spot = place()
    me = lax.axis_index("ctx")
    weights = tuple(zip((gp, op, up, qp, dp), (gw, ow, uw, qw, dw), WEIGHTS))
    greet()
    waits = []
    for part, (row, rows) in enumerate(KV_ROWS):
        first = ORDERS[part][0]
        own = kv_ref.at[:, pl.ds(row, rows)]
        waits.append(
            links.ring(
                first,
                lambda step, own=own: own,
                lambda step, at, ref=f1[part]: ref.at[at],
            )
        )
    own_copies = []
    weight_waits = []
    for number, (plane, whole, (part, by_chip)) in enumerate(weights):
        last = ORDERS[part][2]

        def landing(core, at, whole=whole, part=part, by_chip=by_chip):
            return weight_plane(whole, part, by_chip, core, at)

        copy = pltpu.make_async_copy(plane, landing(core, spot[last]), local.at[number])
        copy.start()
        own_copies.append(copy)
        wait = links.ring(
            last,
            lambda step, plane=plane: plane,
            lambda step, at, landing=landing: landing(core, at),
        )
        over = links.across(plane, lambda at, landing=landing, last=last: landing(at, spot[last]))
        weight_waits.append((wait, landing, last, over))

    seconds = []
    for part, (row, rows) in enumerate(KV_ROWS):
        first, second, _ = ORDERS[part]
        f1[part][spot[first]] = kv_ref[:, row : row + rows]
        all_steps(waits[part])
        mine = spot[second]
        total = f1[part][0, 2].astype(F32)
        for at in range(4):
            g[part][mine, 2 * at] = f1[part][at, 0]
            g[part][mine, 2 * at + 1] = f1[part][at, 1]
            if at:
                total += f1[part][at, 2].astype(F32)
        g[part][mine, 8] = total.astype(BF16)
        seconds.append(
            links.ring(
                second,
                lambda step, ref=g[part], mine=mine: ref.at[mine],
                lambda step, at, ref=g[part]: ref.at[at],
            )
        )
    thirds = []
    for part, (row, rows) in enumerate(KV_ROWS):
        first, second, last = ORDERS[part]
        all_steps(seconds[part])

        def choose(at, i2, i1, part=part, row=row, rows=rows, last=last):
            low = g[part][i2, 2 * i1]
            high = g[part][i2, 2 * i1 + 1]
            source = b_ref[chip_of(at, last, 0)]
            plane = [at[axis] for axis in (X, Y, Z) if axis != last]
            s_ref[at[0], at[1], at[2], pl.ds(row, rows)] = jnp.where(
                source <= b_ref[me], low, high
            )
            for step in (1, 2, 3):
                target = b_ref[chip_of(spot, last, step)]
                sel[part][step - 1, plane[0], plane[1]] = jnp.where(source < target, low, high)

        plane_loop(part, choose)
        total = g[part][0, 8].astype(F32)
        for at in range(1, 4):
            total += g[part][at, 8].astype(F32)
        special[part][...] = total.astype(BF16)
        wait = links.ring(
            last,
            lambda step, part=part: sel[part].at[step - 1],
            lambda step, at, row=row, rows=rows, last=last: of_plane(
                s_ref, last, at, pl.ds(row, rows)
            ),
        )
        wait_special = links.ring(
            last,
            lambda step, part=part: special[part],
            lambda step, at, part=part: rsp[part].at[at],
        )
        thirds.append((wait, wait_special))
    overs = []
    for wait, landing, last, over in weight_waits:
        for step in (1, 3, 2):
            wait(step)
            at = shifted(spot[last], -step)
            overs.append(
                links.across(
                    landing(core, at), lambda at_core, landing=landing, at=at: landing(at_core, at)
                )
            )
        overs.append(over)
    extra_ref[0] = kv_ref[1]
    for part, (row, rows) in enumerate(KV_ROWS):
        last = ORDERS[part][2]
        wait, wait_special = thirds[part]
        all_steps(wait_special)
        rsp[part][spot[last]] = special[part][...]
        total = rsp[part][0].astype(F32)
        for at in range(1, 4):
            total += rsp[part][at].astype(F32)
        extra_ref[1, row : row + rows] = total.astype(BF16)
        all_steps(wait)
    for wait in overs:
        wait()
    for copy in own_copies:
        copy.wait()
    links.close()


def gather(b_all, kv3, planes):
    outs = [((4, 4, 4, 256, 128), BF16), ((2, 256, 128), BF16)]
    for plane, (part, by_chip) in zip(planes, WEIGHTS):
        shape = (2, 4, 4, 4, plane.shape[2], plane.shape[3]) if by_chip else (2, 4) + plane.shape
        outs.append((shape, BF16))
    scratch = []
    for shape in ((4, 3), (4, 9), (3, 4, 4), (), (4,)):
        for _, rows in KV_ROWS:
            scratch.append((shape + (rows, 128), BF16))
    return link_call(
        gather_kernel,
        2,
        80,
        outs,
        (b_all, kv3, *planes),
        [SMEM, VMEM] + [ANY] * 5,
        [VMEM, VMEM] + [ANY] * 5,
        scratch,
        local=5,
    )


def slots_kv(block):
    count = block.shape[0] * 64
    quarters = [block[:, 64 * i : 64 * i + 64].reshape(count, 128) for i in range(4)]
    return (
        jnp.concatenate(quarters[:2], axis=1),
        jnp.concatenate(quarters[2:], axis=1),
    )


CHUNK = 8
EXTRA = 64 * 64
KEYS = 66 * 64


def dot_nt(left, right):
    return lax.dot_general(left, right, (((1,), (1,)), ((), ())), preferred_element_type=F32)


def dot_tn(left, right):
    return lax.dot_general(left, right, (((0,), (0,)), ((), ())), preferred_element_type=F32)


def attend_kernel(q_ref, s_ref, x_ref, place_ref, start_ref, kplace_ref, o_ref, lse_ref):
    q = q_ref[...]
    latest = place_ref[...]
    earliest = start_ref[...]
    o_ref[...] = jnp.zeros_like(o_ref)
    lse_ref[...] = jnp.zeros_like(lse_ref)

    def chunk(block, key_place):
        keys, values = slots_kv(block)
        scores = dot_nt(q, keys)
        allowed = (key_place <= latest) & (key_place >= earliest)
        weights = jnp.where(allowed, jnp.exp2(scores * (SCALE * LOG2E)), 0.0)
        lse_ref[...] += jnp.sum(weights, axis=1, keepdims=True)
        o_ref[...] += jnp.dot(weights.astype(BF16), values, preferred_element_type=F32)

    def step(number, unused):
        at = pl.multiple_of(number * CHUNK * 64, CHUNK * 64)
        chunk(s_ref[pl.ds(number * CHUNK, CHUNK)], kplace_ref[:, pl.ds(at, CHUNK * 64)])
        return unused

    lax.fori_loop(0, 64 // CHUNK, step, 0)
    chunk(x_ref[...], kplace_ref[:, EXTRA:KEYS])
    total = lse_ref[...]
    o_ref[...] = o_ref[...] / total
    lse_ref[...] = jnp.log2(total)


def attend(query, slots, extra, latest, earliest, key_place):
    rows = query.shape[0]
    return pl.pallas_call(
        attend_kernel,
        out_shape=[
            jax.ShapeDtypeStruct((rows, HEAD), F32),
            jax.ShapeDtypeStruct((rows, 1), F32),
        ],
        compiler_params=pltpu.CompilerParams(vmem_limit_bytes=60 * MIB),
    )(query, slots, extra, latest[:, None], earliest[:, None], key_place[None, :])


def attend_back_kernel(
    q_ref, go_ref, s_ref, x_ref, place_ref, start_ref, kplace_ref, lse_ref, dot_ref, gq_ref, gs_ref, gx_ref
):
    q = q_ref[...]
    grad_out = go_ref[...]
    latest = place_ref[...]
    earliest = start_ref[...]
    lse = lse_ref[...]
    row_dot = dot_ref[...]
    gq_ref[...] = jnp.zeros_like(gq_ref)

    def chunk(block, key_place):
        keys, values = slots_kv(block)
        scores = dot_nt(keys, q)
        allowed = (key_place <= latest) & (key_place >= earliest)
        probs = jnp.where(allowed, jnp.exp2(scores * (SCALE * LOG2E) - lse), 0.0)
        grad_probs = dot_nt(values, grad_out)
        grad_scores = (probs * (grad_probs - row_dot)).astype(BF16)
        grad_values = jnp.dot(probs.astype(BF16), grad_out, preferred_element_type=F32).astype(BF16)
        grad_keys = (jnp.dot(grad_scores, q, preferred_element_type=F32) * SCALE).astype(BF16)
        gq_ref[...] += dot_tn(grad_scores, keys) * SCALE
        shape = (block.shape[0], 64, 128)
        return [
            grad[:, at : at + 128].reshape(shape)
            for grad in (grad_keys, grad_values)
            for at in (0, 128)
        ]

    def step(number, unused):
        at = pl.multiple_of(number * CHUNK * 64, CHUNK * 64)
        slots = pl.ds(number * CHUNK, CHUNK)
        parts = chunk(s_ref[slots], kplace_ref[pl.ds(at, CHUNK * 64)])
        for quarter, part in enumerate(parts):
            gs_ref[slots, 64 * quarter : 64 * quarter + 64] = part
        return unused

    lax.fori_loop(0, 64 // CHUNK, step, 0)
    for quarter, part in enumerate(chunk(x_ref[...], kplace_ref[EXTRA:KEYS])):
        gx_ref[:, 64 * quarter : 64 * quarter + 64] = part


def attend_back(query, grad_out, slots, extra, latest, earliest, key_place, lse, row_dot):
    return pl.pallas_call(
        attend_back_kernel,
        out_shape=[
            jax.ShapeDtypeStruct(query.shape, F32),
            jax.ShapeDtypeStruct(slots.shape, BF16),
            jax.ShapeDtypeStruct(extra.shape, BF16),
        ],
        compiler_params=pltpu.CompilerParams(vmem_limit_bytes=60 * MIB),
    )(
        query,
        grad_out,
        slots,
        extra,
        latest[None, :],
        earliest[None, :],
        key_place[:, None],
        lse[None, :],
        row_dot[None, :],
    )


def add_all(refs_values):
    total = refs_values[0].astype(F32)
    for value in refs_values[1:]:
        total += value.astype(F32)
    return total


def by_rows(rows, size, body):
    def step(number, unused):
        body(pl.ds(pl.multiple_of(number * size, size), size))
        return unused

    lax.fori_loop(0, rows // size, step, 0)


def scatter_kernel(*refs):
    b_ref, gs_ref, gx_ref = refs[:3]
    grads = refs[3:8]
    kv_out = refs[8]
    outs = refs[9:14]
    halves = refs[14:19]
    sums = refs[19:24]
    landed = refs[24:29]
    rb, rsp, acc, r2, h, r1 = (refs[29 + 3 * i : 32 + 3 * i] for i in range(6))
    send, recv, local = refs[47:]
    links = Links(send, recv)
    core = lax.axis_index("dp")
    spot = place()
    me = lax.axis_index("ctx")
    greet()

    overs = []
    for number, (grad, half, total) in enumerate(zip(grads, halves, sums)):
        overs.append(links.across(grad.at[1 - core], lambda at, half=half: half))
        copy = pltpu.make_async_copy(grad.at[core], total, local.at[number])
        copy.start()

    thirds = []
    for part, (row, rows) in enumerate(KV_ROWS):
        last = ORDERS[part][2]
        wait = links.ring(
            last,
            lambda step, row=row, rows=rows, last=last: of_plane(
                gs_ref, last, shifted(spot[last], step), pl.ds(row, rows)
            ),
            lambda step, at, part=part: rb[part].at[step - 1],
        )
        wait_special = links.ring(
            last,
            lambda step, row=row, rows=rows: gx_ref.at[1, pl.ds(row, rows)],
            lambda step, at, part=part: rsp[part].at[step - 1],
        )
        thirds.append((wait, wait_special))

    weight_waits = []
    for number, (total, half, over, land) in enumerate(zip(sums, halves, overs, landed)):
        part, by_chip = WEIGHTS[number]
        last = ORDERS[part][2]
        pltpu.make_async_copy(grads[number].at[core], total, local.at[number]).wait()
        over()
        if by_chip:

            def add(at, total=total, half=half):
                for z in range(4):
                    index = (at // 4, at % 4, z)
                    total[index] = (total[index].astype(F32) + half[index].astype(F32)).astype(BF16)

            def step16(at, unused, add=add):
                add(at)
                return unused

            lax.fori_loop(0, 16, step16, 0)
        else:
            for at in range(4):

                def add(rows, at=at, total=total, half=half):
                    total[at, rows] = (
                        total[at, rows].astype(F32) + half[at, rows].astype(F32)
                    ).astype(BF16)

                by_rows(total.shape[1], 16, add)
        weight_waits.append(
            links.ring(
                last,
                lambda step, total=total, last=last, by_chip=by_chip: (
                    of_plane(total, last, shifted(spot[last], step))
                    if by_chip
                    else total.at[shifted(spot[last], step)]
                ),
                lambda step, at, land=land: land.at[step - 1],
            )
        )

    seconds = []
    for part, (row, rows) in enumerate(KV_ROWS):
        first, second, last = ORDERS[part]
        wait, wait_special = thirds[part]
        all_steps(wait)
        all_steps(wait_special)
        special = add_all(
            [gx_ref[1, row : row + rows]] + [rsp[part][step] for step in range(3)]
        ).astype(BF16)
        for at in range(4):
            acc[part][at, 8] = special

        def collect(at, i2, i1, part=part, row=row, rows=rows, last=last):
            chip = chip_of(at, last, 0)
            source = b_ref[chip]
            plane = [at[axis] for axis in (X, Y, Z) if axis != last]
            own = gs_ref[at[0], at[1], at[2], pl.ds(row, rows)].astype(F32)
            none = jnp.zeros_like(own)
            take_low = source <= b_ref[me]
            low = jnp.where(take_low, own, none)
            high = jnp.where(take_low, none, own)
            high += jnp.where(chip == me, gx_ref[0, pl.ds(row, rows)].astype(F32), none)
            for step in (1, 2, 3):
                sender = b_ref[chip_of(spot, last, -step)]
                came = rb[part][step - 1, plane[0], plane[1]].astype(F32)
                low += jnp.where(source < sender, came, none)
                high += jnp.where(source < sender, none, came)
            acc[part][i2, 2 * i1] = low.astype(BF16)
            acc[part][i2, 2 * i1 + 1] = high.astype(BF16)

        plane_loop(part, collect)
        seconds.append(
            links.ring(
                second,
                lambda step, part=part, second=second: acc[part].at[shifted(spot[second], step)],
                lambda step, at, part=part: r2[part].at[step - 1],
            )
        )
    firsts = []
    for part, (row, rows) in enumerate(KV_ROWS):
        first, second, last = ORDERS[part]
        all_steps(seconds[part])

        def pick(index, part=part, second=second):
            return add_all(
                [acc[part][spot[second], index]] + [r2[part][step, index] for step in range(3)]
            ).astype(BF16)

        special = pick(8)
        for at in range(4):
            h[part][at, 0] = pick(2 * at)
            h[part][at, 1] = pick(2 * at + 1)
            h[part][at, 2] = special
        firsts.append(
            links.ring(
                first,
                lambda step, part=part, first=first: h[part].at[shifted(spot[first], step)],
                lambda step, at, part=part: r1[part].at[step - 1],
            )
        )
    for number, (total, land, out) in enumerate(zip(sums, landed, outs)):
        part, by_chip = WEIGHTS[number]
        last = ORDERS[part][2]
        all_steps(weight_waits[number])
        if by_chip:

            def add(at, unused, total=total, land=land, out=out, last=last):
                i, j = at // 4, at % 4
                out[i, j] = add_all(
                    [total[i, j, spot[last]]] + [land[step, i, j] for step in range(3)]
                ).astype(BF16)
                return unused

            lax.fori_loop(0, 16, add, 0)
        else:

            def add(rows, total=total, land=land, out=out, last=last):
                out[rows] = add_all(
                    [total[spot[last], rows]] + [land[step, rows] for step in range(3)]
                ).astype(BF16)

            by_rows(out.shape[0], 16, add)
    for part, (row, rows) in enumerate(KV_ROWS):
        first = ORDERS[part][0]
        all_steps(firsts[part])
        for index in range(3):
            kv_out[index, row : row + rows] = add_all(
                [h[part][spot[first], index]] + [r1[part][step, index] for step in range(3)]
            )
    links.close()


def scatter(b_all, grad_slots, grad_extra, grads):
    outs = [((3, 256, 128), F32)]
    halves, landed = [], []
    for grad, (part, by_chip) in zip(grads, WEIGHTS):
        plane = grad.shape[3:] if by_chip else grad.shape[2:]
        if by_chip:
            plane = grad.shape[2:4] + grad.shape[4:]
        outs.append((plane, BF16))
        halves.append((grad.shape[1:], BF16))
        landed.append(((3,) + plane, BF16))
    scratch = halves + halves + landed
    for shape in ((3, 4, 4), (3,), (4, 9), (3, 9), (4, 3), (3, 3)):
        for _, rows in KV_ROWS:
            scratch.append((shape + (rows, 128), BF16))
    return link_call(
        scatter_kernel,
        3,
        80,
        outs,
        (b_all, grad_slots, grad_extra, *grads),
        [SMEM, VMEM, VMEM] + [ANY] * 5,
        [VMEM] * 6,
        scratch,
        local=5,
    )


def late_kernel(*refs):
    flats = refs[:3]
    kvg_ref = refs[3]
    outs = refs[4:7]
    kvg_out = refs[7]
    r2, h, r1 = (refs[8 + 3 * i : 11 + 3 * i] for i in range(3))
    half, k3, k2, k1 = refs[17:21]
    l3, l2, l1 = refs[21:24]
    send, recv = refs[24:]
    links = Links(send, recv)
    core = lax.axis_index("dp")
    spot = place()
    greet()
    over = links.across(kvg_ref.at[1 - core], lambda at: half)
    seconds = []
    for part in range(3):
        second = ORDERS[part][1]
        seconds.append(
            links.ring(
                second,
                lambda step, part=part, second=second: flats[part].at[shifted(spot[second], step)],
                lambda step, at, part=part: r2[part].at[step - 1],
            )
        )
    over()

    def add(at, unused):
        i, j = at // 4, at % 4
        for k in range(4):
            k3[i, j, k] = (
                kvg_ref[core, i, j, k].astype(F32) + half[i, j, k].astype(F32)
            ).astype(BF16)
        return unused

    lax.fori_loop(0, 16, add, 0)
    w3 = links.ring(
        X, lambda step: k3.at[shifted(spot[X], step)], lambda step, at: l3.at[step - 1]
    )
    firsts = []

    def weights(part):
        first, second, _ = ORDERS[part]
        all_steps(seconds[part])
        for at in range(4):
            h[part][at] = add_all(
                [flats[part][spot[second], at]] + [r2[part][step, at] for step in range(3)]
            ).astype(BF16)
        firsts.append(
            links.ring(
                first,
                lambda step, part=part, first=first: h[part].at[shifted(spot[first], step)],
                lambda step, at, part=part: r1[part].at[step - 1],
            )
        )

    weights(0)
    all_steps(w3)
    for i in range(4):
        for j in range(4):
            k2[i, j] = add_all([k3[spot[X], i, j]] + [l3[step, i, j] for step in range(3)]).astype(
                BF16
            )
    w2 = links.ring(
        Y, lambda step: k2.at[shifted(spot[Y], step)], lambda step, at: l2.at[step - 1]
    )
    weights(1)
    weights(2)
    all_steps(w2)
    for i in range(4):
        k1[i] = add_all([k2[spot[Y], i]] + [l2[step, i] for step in range(3)]).astype(BF16)
    w1 = links.ring(
        Z, lambda step: k1.at[shifted(spot[Z], step)], lambda step, at: l1.at[step - 1]
    )
    for part in range(3):
        first = ORDERS[part][0]
        all_steps(firsts[part])
        outs[part][...] = add_all(
            [h[part][spot[first]]] + [r1[part][step] for step in range(3)]
        )
    all_steps(w1)
    kvg_out[...] = add_all([k1[spot[Z]]] + [l1[step] for step in range(3)])
    links.close()


def late(flats, kvg):
    outs = [(flat.shape[2:], F32) for flat in flats] + [((32, 128), F32)]
    scratch = []
    for shape in ((3, 4), (4,), (3,)):
        for flat in flats:
            scratch.append((shape + flat.shape[2:], BF16))
    for shape in ((4, 4, 4), (4, 4, 4), (4, 4), (4,), (3, 4, 4), (3, 4), (3,)):
        scratch.append((shape + (32, 128), BF16))
    return link_call(
        late_kernel, 4, 40, outs, (*flats, kvg), [VMEM] * 4, [VMEM] * 4, scratch
    )


def rms_scale(values, weights):
    return values * lax.rsqrt(jnp.mean(values * values, axis=-1, keepdims=True) + EPSILON) * weights


def rope_turn(vectors, cos, sin):
    halfway = vectors.shape[-1] // 2
    if vectors.ndim == 3:
        cos, sin = cos[:, None, :], sin[:, None, :]
    turned = jnp.concatenate([-vectors[..., halfway:], vectors[..., :halfway]], axis=-1)
    return vectors * cos + turned * sin


def norm_back(values, weights, incoming):
    unused, pull = jax.vjp(rms_scale, values, weights)
    return pull(incoming)


def dot32(left, right):
    return jnp.dot(left, right, preferred_element_type=F32)


def pack_rows(rows, to):
    return jnp.concatenate([rows, jnp.zeros((to - rows.shape[0], 128), rows.dtype)], axis=0)


def on_device(
    tokens,
    doc_lengths,
    block_order,
    attn_norm,
    query_weight,
    key_weight,
    value_weight,
    query_gain,
    key_gain,
    output_weight,
    attn_post_norm,
    ffn_norm,
    gate_weight,
    up_weight,
    down_weight,
    ffn_post_norm,
    out_cot,
):
    me = lax.axis_index("ctx")
    flat = lambda weight: weight.reshape(-1, 128)
    gains = jnp.concatenate(
        [attn_norm, attn_post_norm, ffn_norm, ffn_post_norm, query_gain, key_gain]
    )
    gains = jnp.concatenate([gains, jnp.zeros((104,), BF16)])[None]
    kvg = pack_rows(
        jnp.concatenate([flat(jnp.concatenate([key_weight, value_weight], axis=1)), gains]), 32
    )
    part_a = pack_rows(jnp.concatenate([flat(gate_weight), flat(output_weight)]), 128)
    part_b = pack_rows(jnp.concatenate([flat(up_weight), flat(query_weight)]), 128)
    part_c = flat(down_weight)
    pa, pb, pc, u0, u1 = early(part_a, part_b, part_c, kvg)
    whole = jnp.concatenate([u0, jnp.transpose(u1, (0, 3, 1, 2, 4, 5))], axis=4)
    whole = whole.reshape(128, 32, 128)
    w_kv = whole[:, :20].reshape(640, 512)
    gains = whole[:, 20].astype(F32)
    gain_attn, gain_post_attn, gain_ffn, gain_post_ffn = (
        gains[:, 5 * i : 5 * i + 5].reshape(640) for i in range(4)
    )
    gain_query, gain_key = (gains[:, 20 + 2 * i : 22 + 2 * i].reshape(256) for i in range(2))

    pairs = block_order.reshape(64, 2)
    b_all = jnp.min(pairs, axis=1)
    b_me = lax.dynamic_index_in_dim(b_all, me, keepdims=False)
    flip = lax.dynamic_index_in_dim(pairs, me, keepdims=False)[0] != b_me

    def low_first(rows):
        return jnp.where(flip, jnp.concatenate([rows[64:], rows[:64]]), rows)

    ramp = jnp.arange(64, dtype=jnp.int32)
    my_place = jnp.concatenate([b_me * 64 + ramp, (127 - b_me) * 64 + ramp])
    lengths = doc_lengths[0]
    starts = jnp.cumsum(lengths) - lengths
    my_start = jnp.max(
        jnp.where(starts[None, :] <= my_place[:, None], starts[None, :], 0), axis=1
    )
    my_position = my_place - my_start
    slot_block = jnp.where(b_all <= b_me, b_all, 127 - b_all)
    slot_block = jnp.concatenate([slot_block, jnp.stack([127 - b_me, jnp.where(b_me == 63, 1000, 63)])])
    key_place = (slot_block[:, None] * 64 + ramp[None, :]).reshape(KEYS)

    frequency = ROPE_BASE ** (-2.0 * jnp.arange(128, dtype=F32) / 256)
    angles = my_position.astype(F32)[:, None] * frequency[None, :]
    angles = jnp.concatenate([angles, angles], axis=-1)
    cos, sin = jnp.cos(angles), jnp.sin(angles)

    def head_side(raw_values, gain_values):
        return rope_turn(rms_scale(raw_values, gain_values), cos, sin)

    inputs = low_first(tokens[0]).astype(F32)
    normed = rms_scale(inputs, gain_attn).astype(BF16)
    kv_raw = dot32(normed, w_kv)
    key_raw, value_raw = kv_raw[:, :HEAD], kv_raw[:, HEAD:]
    key_rot = head_side(key_raw, gain_key).astype(BF16)
    kv = jnp.concatenate([key_rot, value_raw.astype(BF16)], axis=1)
    kv = jnp.transpose(kv.reshape(2, 64, 4, 128), (0, 2, 1, 3)).reshape(2, 256, 128)
    kv3 = jnp.concatenate([kv, jnp.where(b_me == 63, kv[:1], jnp.zeros_like(kv[:1]))])

    pa = pa.reshape(16, 128, 128)
    pb = pb.reshape(16, 128, 128)
    planes = (
        pa[:, :80].reshape(80, 2048),
        pa[:, 80:120].reshape(128, 640),
        pb[:, :80].reshape(80, 2048),
        pb[:, 80:120].reshape(80, 1024),
        pc.reshape(4, 4, 16, 640),
    )
    slots, extra, w_gate, w_output, w_up, w_query, w_down = gather(b_all, kv3, planes)
    slots = slots.reshape(64, 256, 128)
    w_gate = w_gate.reshape(640, 2048)
    w_output = w_output.reshape(1024, 640)
    w_up = w_up.reshape(640, 2048)
    w_query = w_query.reshape(640, 1024)
    w_down = w_down.reshape(2048, 640)

    k = jnp.arange(640, dtype=jnp.int32)
    at_core, at_y, at_z, at_x, at_row = k // 320, (k // 80) % 4, (k // 20) % 4, (k // 5) % 4, k % 5
    turn = (((at_core * 4 + at_x) * 4 + at_y) * 4 + at_z) * 5 + at_row
    turning = (k[:, None] == turn[None, :]).astype(BF16)

    def turned(values):
        return dot32(values, turning).astype(BF16)

    def unturned(values):
        return dot_nt(values.astype(BF16), turning)

    normed_b = turned(normed)
    query_raw = dot32(normed_b, w_query).reshape(128, HEADS, HEAD)
    query_rot = head_side(query_raw, gain_query).astype(BF16)

    def to_rows(values):
        return jnp.transpose(values.reshape(2, 64, HEADS, HEAD), (0, 2, 1, 3)).reshape(512, HEAD)

    def from_rows(rows):
        return jnp.transpose(rows.reshape(2, HEADS, 64, HEAD), (0, 2, 1, 3)).reshape(
            128, HEADS, HEAD
        )

    def row_numbers(numbers):
        return jnp.broadcast_to(numbers.reshape(2, 1, 64), (2, HEADS, 64)).reshape(512)

    query_rows = to_rows(query_rot)
    latest, earliest = row_numbers(my_place), row_numbers(my_start)
    attn_rows, lse = attend(query_rows, slots, extra, latest, earliest, key_place)
    attn_low = from_rows(attn_rows).reshape(128, HEADS * HEAD).astype(BF16)
    proj_out = dot32(attn_low, w_output)
    middle = inputs + rms_scale(proj_out, gain_post_attn)
    ffn_in = rms_scale(middle, gain_ffn).astype(BF16)
    ffn_in_b = turned(ffn_in)
    gate = dot32(ffn_in, w_gate)
    upper = dot32(ffn_in_b, w_up)

    def geglu(gate_in, upper_in):
        return jax.nn.gelu(gate_in, approximate=True) * upper_in

    hidden = geglu(gate, upper).astype(BF16)
    ffn_out = dot32(hidden, w_down)
    block_out = (middle + rms_scale(ffn_out, gain_post_ffn)).astype(BF16)
    grad_out = low_first(out_cot[0]).astype(F32)
    grad_ffn_out, post_ffn_term = norm_back(ffn_out, gain_post_ffn, grad_out)
    ffn_out_low = grad_ffn_out.astype(BF16)
    down_term = dot_tn(hidden, ffn_out_low).astype(BF16)
    grad_hidden = dot_nt(ffn_out_low, w_down)
    unused, pull_geglu = jax.vjp(geglu, gate, upper)
    grad_gate, grad_upper = pull_geglu(grad_hidden)
    grad_gate = grad_gate.astype(BF16)
    grad_upper = grad_upper.astype(BF16)
    gate_term = dot_tn(ffn_in, grad_gate).astype(BF16)
    upper_term = dot_tn(ffn_in_b, grad_upper).astype(BF16)
    grad_ffn_in = dot_nt(grad_gate, w_gate) + unturned(dot_nt(grad_upper, w_up))
    grad_middle_norm, ffn_norm_term = norm_back(middle, gain_ffn, grad_ffn_in)
    grad_middle = grad_out + grad_middle_norm
    grad_proj, post_attn_term = norm_back(proj_out, gain_post_attn, grad_middle)
    proj_low = grad_proj.astype(BF16)
    out_term = dot_tn(attn_low, proj_low).astype(BF16)
    grad_attn = to_rows(dot_nt(proj_low, w_output).astype(BF16))
    row_dot = jnp.sum(grad_attn.astype(F32) * attn_rows, axis=1)

    grad_query_rows, grad_slots, grad_extra = attend_back(
        query_rows, grad_attn, slots, extra, latest, earliest, key_place, lse[:, 0], row_dot
    )
    unused, pull_query = jax.vjp(head_side, query_raw, gain_query)
    grad_query_raw, query_gain_term = pull_query(from_rows(grad_query_rows))
    query_low = grad_query_raw.reshape(128, HEADS * HEAD).astype(BF16)
    query_term = dot_tn(normed_b, query_low).astype(BF16)

    grads = (
        gate_term.reshape(2, 4, 80, 2048),
        out_term.reshape(2, 4, 128, 640),
        upper_term.reshape(2, 4, 80, 2048),
        query_term.reshape(2, 4, 80, 1024),
        down_term.reshape(2, 4, 4, 4, 16, 640),
    )
    kv_sum, *planes = scatter(b_all, grad_slots.reshape(4, 4, 4, 256, 128), grad_extra, grads)
    low_sum = kv_sum[0] + jnp.where(b_me == 63, kv_sum[2], jnp.zeros_like(kv_sum[2]))
    kv_grad = jnp.stack([low_sum, kv_sum[1]]).reshape(2, 4, 64, 128)
    kv_grad = jnp.transpose(kv_grad, (0, 2, 1, 3)).reshape(128, 512)
    unused, pull_key = jax.vjp(head_side, key_raw, gain_key)
    grad_key_raw, key_gain_term = pull_key(kv_grad[:, :HEAD])
    kv_low = jnp.concatenate([grad_key_raw, kv_grad[:, HEAD:]], axis=1).astype(BF16)
    kv_term = dot_tn(normed, kv_low).astype(BF16)
    grad_normed = unturned(dot_nt(query_low, w_query)) + dot_nt(kv_low, w_kv)
    grad_inputs, attn_norm_term = norm_back(inputs, gain_attn, grad_normed)
    tokens_grad = (grad_middle + grad_inputs).astype(BF16)

    terms = [
        term.reshape(128, -1)
        for term in (
            attn_norm_term,
            post_attn_term,
            ffn_norm_term,
            post_ffn_term,
            query_gain_term,
            key_gain_term,
        )
    ]
    terms = jnp.concatenate(terms + [jnp.zeros((128, 104), F32)], axis=1).astype(BF16)
    kvg_term = jnp.concatenate(
        [kv_term.reshape(128, 20, 128), terms[:, None], jnp.zeros((128, 11, 128), BF16)], axis=1
    ).reshape(2, 4, 4, 4, 32, 128)
    gate_sum, out_sum, up_sum, query_sum, down_sum = planes
    blank = jnp.zeros((16, 8, 128), BF16)
    flats = (
        jnp.concatenate(
            [gate_sum.reshape(16, 80, 128), out_sum.reshape(16, 40, 128), blank], axis=1
        ).reshape(4, 4, 128, 128),
        jnp.concatenate(
            [up_sum.reshape(16, 80, 128), query_sum.reshape(16, 40, 128), blank], axis=1
        ).reshape(4, 4, 128, 128),
        down_sum.reshape(4, 4, 80, 128),
    )
    fa, fb, fc, fk = late(flats, kvg_term)
    kv_final = fk[:20].reshape(5, 512)
    gain_sums = fk[20]
    fives = [gain_sums[5 * i : 5 * i + 5] for i in range(4)]
    return (
        low_first(block_out)[None],
        low_first(tokens_grad)[None],
        fives[0],
        fb[80:120].reshape(5, 1024),
        kv_final[:, :HEAD],
        kv_final[:, HEAD:],
        gain_sums[20:22],
        gain_sums[22:24],
        fa[80:120].reshape(8, 640),
        fives[1],
        fives[2],
        fa[:80].reshape(5, 2048),
        fb[:80].reshape(5, 2048),
        fc.reshape(16, 640),
        fives[3],
    )


def solution(mesh):
    rows = P(("dp", "ctx"), None)
    vector = P(("dp", "ctx"))
    stream = P("dp", "ctx", None)
    return jax.shard_map(
        on_device,
        mesh=mesh,
        in_specs=(
            stream,
            P("dp", None),
            P(),
            vector,
            rows,
            rows,
            rows,
            vector,
            vector,
            rows,
            vector,
            vector,
            rows,
            rows,
            rows,
            vector,
            stream,
        ),
        out_specs=(
            stream,
            stream,
            vector,
            rows,
            rows,
            rows,
            vector,
            vector,
            rows,
            vector,
            vector,
            rows,
            rows,
            rows,
            vector,
        ),
        check_vma=False,
    )
```

time: 2460 us -> 308 us (0.13)
  waiting for transfers between devices: 1230 us -> 0 us
  blocking collectives: 763 us -> 0 us
  Pallas kernels: 0 us -> 195 us
  matrix products: 199 us -> 31.9 us
  local copies, waits for them, and re-layouts: 179 us -> 51.1 us
  loops' own time: 34.2 us -> 0 us
    reduce_scatter x2 -> x0, waiting for transfers between devices: 1040 us -> none  [the longest x1 659 us: on_device(): lax.psum_scatter(down_term, ('dp', 'ctx'), scatter_dimension=0, tiled=True)]
    all_gather x2 -> x0, blocking collectives: 637 us -> none  [the longest x1 322 us: on_device(): lax.all_gather(value_weight, ('dp', 'ctx'), axis=0, tiled=True)]
    pallas_call x0 -> x6, Pallas kernels: none -> 195 us  [the longest x4 173 us: link_call(): pl.pallas_call(kernel, out_shape=[jax.ShapeDtypeStruct(shape, kind) for s...]
    dot_general x165 -> x20, matrix products: 199 us -> 31.9 us  [the longest x6 13.3 us: dot_nt(): lax.dot_general(left, right, (((1,), (1,)), ((), ())), preferred_element_...]
    unnamed x10 -> x0, waiting for transfers between devices: 145 us -> none
    unnamed x2 -> x0, blocking collectives: 126 us -> none
    dynamic_slice x145 -> x2, local copies, waits for them, and re-layouts: 112 us -> 0.6 us  [the longest x1 0.59 us: on_device(): b_me = lax.dynamic_index_in_dim(b_all, me, keepdims=False)]
    all_gather x6 -> x0, waiting for transfers between devices: 50.4 us -> none  [the longest x1 50.3 us: on_device(): all_kv = lax.all_gather(key_value, 'ctx', axis=0, tiled=True)]
  transfers between devices with their start and end apart: 9 -> 0, of which waited for: 4 -> 0; matrix products, arithmetic and copies ran while one was open for 10% -> 0% of each run, Pallas kernels for 0% -> 0%
where the time goes in v1:
time: 308 us; the launch traced here: 307 us
  Pallas kernels  195 us (63%)
  local copies, waits for them, and re-layouts  51.1 us (17%)
  matrix products  31.9 us (10%)
  other arithmetic  24.3 us (8%)
  between operations  4.92 us (2%)
    pallas_call x4, Pallas kernels, link_call(): pl.pallas_call(kernel, out_shape=[jax.ShapeDtypeStruct(shape, kind) for s...  173 us
    dot_general x6, matrix products, dot_nt(): lax.dot_general(left, right, (((1,), (1,)), ((), ())), preferred_element_...  13.3 us
    pallas_call x1, Pallas kernels, attend_back(): pl.pallas_call(attend_back_kernel, out_shape=[jax.ShapeDtypeStruct(query....  13.1 us
    dot_general x6, matrix products, dot_tn(): lax.dot_general(left, right, (((0,), (0,)), ((), ())), preferred_element_...  10.7 us
    pallas_call x1, Pallas kernels, attend(): pl.pallas_call(attend_kernel, out_shape=[jax.ShapeDtypeStruct((rows, HEAD...  8.99 us
    dot_general x8, matrix products, dot32(): return jnp.dot(left, right, preferred_element_type=F32)  7.84 us

profile of v1, /device:TPU:0, one launch (start us, length us, event | category | flops | bytes accessed | tf_op | source)
XLA Modules:
  0.0 306.8 jit_solution(4101513443627776913)
XLA Ops:
  1.4 0.8 reshape.740
  3.0 0.8 reshape.738
  4.5 1.4 reshape.742.c_ref
  5.9 4.1 %concatenate.132 = bf16[128]{0:T(256)(128)(2,1)S(1)} concatenate(bf16[5]{0:T(256)(128)(2,1)} %param.20, bf16[5]{0:T(256)(128)(2,1)} %param.27, bf16[5]{0:T(256)(128)(2,1)} %param.28, bf16[5]{0:T(256)(128)(2,1)} %param.32, bf16[2]{0:T(256)(128)(2,1)} %param.24, bf16[2]{0:T(256)(128)(2,1)} %param.25, bf16[104]{0:T(256)(128)(2,1)S(1)} %broadcast_in_dim.52), dimensions={0} | concatenate | bytes 512 | tf_op jit(solution)/shard_map/concatenate | solution.py:867
  11.5 25.4 %shard_map.280 = (bf16[4,4,128,128]{3,2,1,0:T(8,128)(2,1)}, bf16[4,4,128,128]{3,2,1,0:T(8,128)(2,1)}, bf16[4,4,80,128]{3,2,1,0:T(8,128)(2,1)}, bf16[2,4,4,4,16,1...) custom-call(bf16[128,128]{1,0:T(8,128)(2,1)} %get-tuple-element.135.a_ref, ...), custom_call_target="tpu_custom_call" | custom-call | tf_op jit(solution)/shard_map/pallas_call | solution.py:117
  36.9 1.3 pad_maximum_fusion
  46.8 0.9 reshape.749.refs_2_
  47.7 0.8 reshape.750.refs_3_
  48.5 0.9 reshape.752.refs_4_
  50.2 1.0 reshape.754.refs_6_
  51.2 62.9 %shard_map.281 = (bf16[4,4,4,256,128]{4,3,2,1,0:T(8,128)(2,1)}, bf16[2,256,128]{2,1,0:T(8,128)(2,1)}, bf16[2,4,80,2048]{3,2,1,0:T(8,128)(2,1)}, bf16[2,4,128,640...) custom-call(s32[64]{0:T(128)} %copy-done.74, ...), custom_call_target="tpu_custom_call" | custom-call | tf_op jit(solution)/shard_map/pallas_call | solution.py:117
  114.1 1.7 copy.61
  119.1 0.9 broadcast_in_dim_reshape.12.place_ref
  120.1 0.9 broadcast_in_dim_reshape.13.start_ref
  122.5 9.0 %shard_map.282 = (f32[512,256]{1,0:T(8,128)}, f32[512,1]{1,0:T(8,128)}) custom-call(bf16[512,256]{1,0:T(8,128)(2,1)} %bitcast.169, bf16[64,256,128]{2,1,0:T(8,128)(2,1)} %bitcast.145, bf16[2,256,128]{2,1,0:T(8,128)(2,1)} %get-tuple-element.49.x_ref, s32[512,1]{1,0:T(8,128)} %broadcast_in_dim_reshape.12.place_ref, ...), custom_call_target="tpu_custom_call" | custom-call | tf_op jit(solution)/shard_map/pallas_call | solution.py:436
  131.5 1.2 convert_element_type.141
  135.4 2.5 fusion.99
  138.4 1.7 multiply_convert_fusion.1
  141.0 1.3 multiply_reduce_fusion.8
  143.3 1.6 mul.623
  145.0 1.1 slice_bitcast_fusion.1
  146.0 1.8 fusion.31
  148.5 1.2 fusion.32
  150.5 4.1 %multiply_convert_fusion = (bf16[128,2048]{1,0:T(8,128)(2,1)}, bf16[128,2048]{1,0:T(8,128)(2,1)S(1)}) fusion(f32[128,2048]{1,0:T(8,128)S(1)} %copy-done.10, f32[128,2048]{1,0:T(8,128)S(1)} %copy-done.34, bf16[128,640]{1,0:T(8,128)(2,1)S(1)} %get-tuple-element.97, bf16[2048,640]{1,0:T(8,128)(2,1)} %bitcast.164), kind=kOutput, calls=%fused_computation.29 | convolution fusion | flops 341835776 | bytes 5931008 | tf_op jit(solution)/shard_map/dot_general | solution.py:400
  154.6 1.7 fusion.100
  156.3 3.9 %multiply_reduce_fusion.4 = (bf16[640]{0:T(1024)(128)(2,1)}, f32[128]{0:T(128)}, f32[128,640]{1,0:T(8,128)}) fusion(f32[128,640]{1,0:T(8,128)S(1)} %get-tuple-element.86, f32[128]{0:T(128)} %copy-done.77, f32[640]{0:T(1024)S(1)} %mul.612, f32[128,640]{1,0:T(8,128)} %fusion.100, s32[640]{0:T(1024)} %copy-done.65, bf16[128,2048]{1,0:T(8,128)(2,1)} %get-tuple-element.89, ...), kind=kOutput, calls=%fused_computation.78 | convolution fusion | flops 441466112 | bytes 4136192 | tf_op jit(solution)/shard_map/dot_general | solution.py:400
  161.0 1.4 multiply_reduce_fusion.5
  163.1 1.1 fusion.33
  166.3 3.5 %add.357.kplace_ref = s32[4224,1]{1,0:T(8,128)} reshape(s32[66,64]{1,0:T(8,128)S(1)} %copy-done.45) | data formatting | bytes 33792 | tf_op jit(solution)/shard_map/add | solution.py:902
  171.3 13.1 %shard_map.283 = (f32[512,256]{1,0:T(8,128)}, bf16[64,256,128]{2,1,0:T(8,128)(2,1)}, bf16[2,256,128]{2,1,0:T(8,128)(2,1)}) custom-call(bf16[512,256]{1,0:T(8,128)(2,1)} %bitcast.170, bf16[512,256]{1,0:T(8,128)(2,1)} %bitcast.168, bf16[64,256,128]{2,1,0:T(8,128)(2,1)} %bitcast.146, bf16[2,256,128]{2,1,0:T(8,128)(2,1)} %get-tuple-element.49.x_ref, ...), custom_call_target="tpu_custom_call" | custom-call | tf_op jit(solution)/shard_map/pallas_call | solution.py:488
  184.5 2.3 convolution_convert_fusion.2
  186.8 1.6 convolution_convert_fusion.4
  188.4 2.4 convolution_convert_fusion.1
  192.4 1.6 convolution_convert_fusion.3
  194.0 2.4 convolution_convert_fusion
  196.4 59.7 %shard_map.284 = (f32[3,256,128]{2,1,0:T(8,128)}, bf16[80,2048]{1,0:T(8,128)(2,1)}, bf16[128,640]{1,0:T(8,128)(2,1)}, bf16[80,2048]{1,0:T(8,128)(2,1)}, bf16[80,...) custom-call(s32[64]{0:T(128)} %copy-done.74, bf16[4,4,4,256,128]{4,3,2,1,0:T(8,128)(2,1)} %bitcast.159, ...), custom_call_target="tpu_custom_call" | custom-call | tf_op jit(solution)/shard_map/pallas_call | solution.py:117
  256.1 1.1 select_add_fusion
  258.5 1.1 fusion.55
  259.7 2.0 fusion.29
  261.9 0.8 fusion.43
  263.3 1.3 maximum_maximum_fusion.2
  264.7 1.0 reshape.774.refs_2_
  267.1 1.6 concatenate.163
  269.7 1.5 maximum_maximum_fusion.refs_3_
  271.2 24.6 %shard_map.285 = (f32[128,128]{1,0:T(8,128)}, f32[128,128]{1,0:T(8,128)}, f32[80,128]{1,0:T(8,128)}, f32[32,128]{1,0:T(8,128)}) custom-call(bf16[4,4,128,128]{3,2,1,0:T(8,128)(2,1)} %get-tuple-element.133.refs_0_, bf16[4,4,128,128]{3,2,1,0:T(8,128)(2,1)} %get-tuple-element.132.refs_1_, bf16[4,4,80,128]{3,2,1,0:T(8,128)(2,1)} %reshape.774.refs_2_, ...), custom_call_target="tpu_custom_call" | custom-call | tf_op jit(solution)/shard_map/pallas_call | solution.py:117
  295.8 1.4 slice_bitcast_fusion.2
  299.9 1.3 slice_bitcast_fusion.5
  305.4 1.4 reshape.780
  (318 shorter events, 38.8 us)
Async XLA Ops:
  2.3 34.6 %copy-start.78 = (bf16[128]{0:T(256)(128)(2,1)}, bf16[128]{0:T(256)(128)(2,1)S(1)}, u32[]{:S(2)}) copy-start(bf16[128]{0:T(256)(128)(2,1)S(1)} %pad.66.clone) | copy-start | bytes 772
  10.8 26.1 %copy-start.80 = (bf16[32]{0:T(256)(128)(2,1)}, bf16[32]{0:T(256)(128)(2,1)S(1)}, u32[]{:S(2)}) copy-start(bf16[32]{0:T(256)(128)(2,1)S(1)} %pad.58.clone) | copy-start | bytes 196
  36.9 2.5 copy-start.82
  39.6 2.7 copy-start.74
  39.7 4.1 %copy-start.90 = (s32[1,8]{1,0:T(1,128)S(1)}, s32[1,8]{1,0:T(1,128)}, u32[]{:S(2)}) copy-start(s32[1,8]{1,0:T(1,128)} %param.18) | copy-start | bytes 100
  40.3 5.0 %copy-start.2 = (bf16[640,512]{1,0:T(8,128)(2,1)}, bf16[640,512]{1,0:T(8,128)(2,1)S(1)}, u32[]{:S(2)}) copy-start(bf16[640,512]{1,0:T(8,128)(2,1)S(1)} %reshape.745) | copy-start | bytes 1966084
  42.0 91.7 %copy-start.14 = (bf16[128,640]{1,0:T(8,128)(2,1)}, bf16[128,640]{1,0:T(8,128)(2,1)S(1)}, u32[]{:S(2)}) copy-start(bf16[128,640]{1,0:T(8,128)(2,1)S(1)} %get-tuple-element.88) | copy-start | bytes 491524
  42.0 73.9 %copy-start.72 = (f32[128]{0:T(128)}, f32[128]{0:T(128)S(1)}, u32[]{:S(2)}) copy-start(f32[128]{0:T(128)S(1)} %fusion.82) | copy-start | bytes 1540
  42.0 4.8 %copy-start.43 = (bf16[4,4,128,128]{3,2,1,0:T(8,128)(2,1)S(1)}, bf16[4,4,128,128]{3,2,1,0:T(8,128)(2,1)}, u32[]{:S(2)}) copy-start(bf16[4,4,128,128]{3,2,1,0:T(8,128)(2,1)} %get-tuple-element.44) | copy-start | bytes 1572868
  42.3 5.4 %copy-start.11 = (f32[128,512]{1,0:T(8,128)}, f32[128,512]{1,0:T(8,128)S(1)}, u32[]{:S(2)}) copy-start(f32[128,512]{1,0:T(8,128)S(1)} %fusion.39) | copy-start | bytes 786436
  44.5 3.2 %copy-start.59 = (f32[256]{0:T(256)}, f32[256]{0:T(256)S(1)}, u32[]{:S(2)}) copy-start(f32[256]{0:T(256)S(1)} %mul.581) | copy-start | bytes 3076
  44.6 3.9 %copy-start.83 = (f32[128]{0:T(128)}, f32[128]{0:T(128)S(1)}, u32[]{:S(2)}) copy-start(f32[128]{0:T(128)S(1)} %multiply_reduce_fusion.13) | copy-start | bytes 1540
  44.6 3.9 %copy-start.70 = (f32[128]{0:T(128)}, f32[128]{0:T(128)S(1)}, u32[]{:S(2)}) copy-start(f32[128]{0:T(128)S(1)} %fusion.83) | copy-start | bytes 1540
  44.7 3.8 %copy-start.42 = (bf16[4,4,128,128]{3,2,1,0:T(8,128)(2,1)S(1)}, bf16[4,4,128,128]{3,2,1,0:T(8,128)(2,1)}, u32[]{:S(2)}) copy-start(bf16[4,4,128,128]{3,2,1,0:T(8,128)(2,1)} %get-tuple-element.45) | copy-start | bytes 1572868
  45.3 72.9 %copy-start.30 = (f32[128,256]{1,0:T(8,128)}, f32[128,256]{1,0:T(8,128)S(1)}, u32[]{:S(2)}) copy-start(f32[128,256]{1,0:T(8,128)S(1)} %get-tuple-element.119) | copy-start | bytes 393220
  45.3 72.9 %copy-start.32 = (f32[128,256]{1,0:T(8,128)}, f32[128,256]{1,0:T(8,128)S(1)}, u32[]{:S(2)}) copy-start(f32[128,256]{1,0:T(8,128)S(1)} %get-tuple-element.121) | copy-start | bytes 393220
  46.1 4.1 %copy-start.48 = (bf16[4,4,80,128]{3,2,1,0:T(8,128)(2,1)S(1)}, bf16[4,4,80,128]{3,2,1,0:T(8,128)(2,1)}, u32[]{:S(2)}) copy-start(bf16[4,4,80,128]{3,2,1,0:T(8,128)(2,1)} %get-tuple-element.46) | copy-start | bytes 983044
  117.9 3.1 %copy-start.75 = (s32[64]{0:T(128)S(1)}, s32[64]{0:T(128)}, u32[]{:S(2)}) copy-start(s32[64]{0:T(128)} %copy-done.74) | copy-start | bytes 772
  119.1 12.4 %copy-start.55 = (s32[2,4,64]{2,1,0:T(4,128)}, s32[2,4,64]{2,1,0:T(4,128)S(1)}, u32[]{:S(2)}) copy-start(s32[2,4,64]{2,1,0:T(4,128)S(1)} %broadcast_in_dim.107) | copy-start | bytes 6148
  120.1 11.4 %copy-start.57 = (s32[2,4,64]{2,1,0:T(4,128)}, s32[2,4,64]{2,1,0:T(4,128)S(1)}, u32[]{:S(2)}) copy-start(s32[2,4,64]{2,1,0:T(4,128)S(1)} %broadcast_in_dim.109) | copy-start | bytes 6148
  121.8 9.7 %copy-start.44 = (s32[66,64]{1,0:T(8,128)}, s32[66,64]{1,0:T(8,128)S(1)}, u32[]{:S(2)}) copy-start(s32[66,64]{1,0:T(8,128)S(1)} %iota_add_fusion) | copy-start | bytes 50692
  134.9 3.0 copy-start.66
  135.1 3.3 %copy-start.26 = (bf16[128,640]{1,0:T(8,128)(2,1)}, bf16[128,640]{1,0:T(8,128)(2,1)S(1)}, u32[]{:S(2)}) copy-start(bf16[128,640]{1,0:T(8,128)(2,1)S(1)} %multiply_convert_fusion.2) | copy-start | bytes 491524
  135.4 3.0 copy-start
  138.4 2.6 copy-start.13
  145.0 5.5 %copy-start.10 = (f32[128,2048]{1,0:T(8,128)S(1)}, f32[128,2048]{1,0:T(8,128)}, u32[]{:S(2)}) copy-start(f32[128,2048]{1,0:T(8,128)} %copy-done.9) | copy-start | bytes 3145732
  145.0 5.5 %copy-start.34 = (f32[128,2048]{1,0:T(8,128)S(1)}, f32[128,2048]{1,0:T(8,128)}, u32[]{:S(2)}) copy-start(f32[128,2048]{1,0:T(8,128)} %get-tuple-element.141) | copy-start | bytes 3145732
  147.8 2.6 copy-start.28
  149.7 4.9 %copy-start.37 = (bf16[128,640]{1,0:T(8,128)(2,1)}, bf16[128,640]{1,0:T(8,128)(2,1)S(1)}, u32[]{:S(2)}) copy-start(bf16[128,640]{1,0:T(8,128)(2,1)S(1)} %get-tuple-element.97) | copy-start | bytes 491524
  150.5 4.1 %copy-start.1 = (bf16[2,4,80,2048]{3,2,1,0:T(8,128)(2,1)S(1)}, bf16[2,4,80,2048]{3,2,1,0:T(8,128)(2,1)}, u32[]{:S(2)}) copy-start(bf16[2,4,80,2048]{3,2,1,0:T(8,128)(2,1)} %get-tuple-element.52) | copy-start | bytes 7864324
  160.2 4.0 %copy-start.5 = (bf16[2,4,128,640]{3,2,1,0:T(8,128)(2,1)S(1)}, bf16[2,4,128,640]{3,2,1,0:T(8,128)(2,1)}, u32[]{:S(2)}) copy-start(bf16[2,4,128,640]{3,2,1,0:T(8,128)(2,1)} %get-tuple-element.51) | copy-start | bytes 3932164
  162.4 2.6 copy-start.56
  162.4 3.3 %copy-start.58 = (s32[2,4,64]{2,1,0:T(4,128)S(1)}, s32[2,4,64]{2,1,0:T(4,128)}, u32[]{:S(2)}) copy-start(s32[2,4,64]{2,1,0:T(4,128)} %copy-done.57) | copy-start | bytes 6148
  162.4 3.9 %copy-start.45 = (s32[66,64]{1,0:T(8,128)S(1)}, s32[66,64]{1,0:T(8,128)}, u32[]{:S(2)}) copy-start(s32[66,64]{1,0:T(8,128)} %copy-done.44) | copy-start | bytes 50692
  164.2 5.7 %copy-start.52 = (f32[512,1]{1,0:T(8,128)S(1)}, f32[512,1]{1,0:T(8,128)}, u32[]{:S(2)}) copy-start(f32[512,1]{1,0:T(8,128)} %get-tuple-element.55) | copy-start | bytes 6148
  164.8 5.8 %copy-start.20 = (f32[512,256]{1,0:T(8,128)S(1)}, f32[512,256]{1,0:T(8,128)}, u32[]{:S(2)}) copy-start(f32[512,256]{1,0:T(8,128)} %get-tuple-element.50) | copy-start | bytes 1572868
  165.0 6.3 %copy-start.18 = (bf16[2,64,4,256]{3,1,2,0:T(8,128)(2,1)}, bf16[2,64,4,256]{3,1,2,0:T(8,128)(2,1)S(1)}, u32[]{:S(2)}) copy-start(bf16[2,64,4,256]{3,1,2,0:T(8,128)(2,1)S(1)} %copy.66) | copy-start | bytes 786436
  171.3 13.1 %copy-start.22 = (bf16[128,2048]{1,0:T(8,128)(2,1)S(1)}, bf16[128,2048]{1,0:T(8,128)(2,1)}, u32[]{:S(2)}) copy-start(bf16[128,2048]{1,0:T(8,128)(2,1)} %copy-done.21) | copy-start | bytes 1572868
  171.3 13.1 %copy-start.27 = (bf16[128,640]{1,0:T(8,128)(2,1)S(1)}, bf16[128,640]{1,0:T(8,128)(2,1)}, u32[]{:S(2)}) copy-start(bf16[128,640]{1,0:T(8,128)(2,1)} %copy-done.26) | copy-start | bytes 491524
  184.5 4.0 %copy-start.19 = (bf16[128,2048]{1,0:T(8,128)(2,1)S(1)}, bf16[128,2048]{1,0:T(8,128)(2,1)}, u32[]{:S(2)}) copy-start(bf16[128,2048]{1,0:T(8,128)(2,1)} %get-tuple-element.89) | copy-start | bytes 1572868
  184.5 3.9 %copy-start.40 = (bf16[128,640]{1,0:T(8,128)(2,1)S(1)}, bf16[128,640]{1,0:T(8,128)(2,1)}, u32[]{:S(2)}) copy-start(bf16[128,640]{1,0:T(8,128)(2,1)} %copy-done.39) | copy-start | bytes 491524
  186.8 4.0 %copy-start.41 = (f32[512,256]{1,0:T(8,128)S(1)}, f32[512,256]{1,0:T(8,128)}, u32[]{:S(2)}) copy-start(f32[512,256]{1,0:T(8,128)} %get-tuple-element.56) | copy-start | bytes 1572868
  256.1 2.4 copy-start.3
  258.4 3.3 %copy-start.89 = (f32[128]{0:T(128)S(1)}, f32[128]{0:T(128)}, u32[]{:S(2)}) copy-start(f32[128]{0:T(128)} %copy-done.88) | copy-start | bytes 1540
  259.7 3.1 %copy-start.51 = (bf16[80,2048]{1,0:T(8,128)(2,1)S(1)}, bf16[80,2048]{1,0:T(8,128)(2,1)}, u32[]{:S(2)}) copy-start(bf16[80,2048]{1,0:T(8,128)(2,1)} %get-tuple-element.62) | copy-start | bytes 983044
  262.8 3.4 %copy-start.69 = (bf16[640]{0:T(1024)(128)(2,1)S(1)}, bf16[640]{0:T(1024)(128)(2,1)}, u32[]{:S(2)}) copy-start(bf16[640]{0:T(1024)(128)(2,1)} %get-tuple-element.71) | copy-start | bytes 3844
  263.0 3.4 %copy-start.68 = (bf16[640]{0:T(1024)(128)(2,1)S(1)}, bf16[640]{0:T(1024)(128)(2,1)}, u32[]{:S(2)}) copy-start(bf16[640]{0:T(1024)(128)(2,1)} %get-tuple-element.75) | copy-start | bytes 3844
  264.7 5.0 %copy-start.81 = (bf16[32]{0:T(256)(128)(2,1)S(1)}, bf16[32]{0:T(256)(128)(2,1)}, u32[]{:S(2)}) copy-start(bf16[32]{0:T(256)(128)(2,1)} %copy-done.80) | copy-start | bytes 196
  (43 other events, 66.6 us)

commit v2 on v0

v2 whole, which is shorter than its diff:
```python
from types import SimpleNamespace

import jax
import jax.numpy as jnp
import numpy as np
from jax import lax
from jax.experimental import pallas as pl
from jax.experimental.pallas import tpu as pltpu
from jax.sharding import PartitionSpec as P

EPSILON = 1e-06
ROPE_BASE = 1000000.0
MESH = pl.DeviceIdType.MESH
F32 = jnp.float32
BF16 = jnp.bfloat16
MIB = 2**20

X, Y, Z = 0, 1, 2
ORDERS = ((Z, Y, X), (X, Z, Y), (Y, X, Z))
UNITS = (
    ((0, 0), (0, 1), (0, 2), (0, 3), (3, 0))
    + ((1, 0), (1, 1), (1, 2), (1, 3), (3, 1))
    + ((2, 0), (2, 1), (2, 2), (2, 3), (3, 2), (3, 3))
)
KV_ROWS = ((0, 80), (80, 80), (160, 96))
HEADS = 4
HEAD = 256
SCALE = HEAD**-0.5
LOG2E = 1.4426950408889634


def place():
    chip = lax.axis_index("ctx")
    return (chip // 16, (chip // 4) % 4, chip % 4)


def shifted(value, step):
    return lax.rem(value + step + 4, 4)


def peer(axis, step):
    spot = list(place())
    spot[axis] = shifted(spot[axis], step)
    return (lax.axis_index("dp"), spot[0] * 16 + spot[1] * 4 + spot[2])


def other_core():
    return (1 - lax.axis_index("dp"), lax.axis_index("ctx"))


def greet():
    barrier = pltpu.get_barrier_semaphore()
    for axis in (X, Y, Z):
        for step in (1, 2, 3):
            pl.semaphore_signal(barrier, inc=1, device_id=peer(axis, step), device_id_type=MESH)
    pl.semaphore_signal(barrier, inc=1, device_id=other_core(), device_id_type=MESH)


def greeted():
    pl.semaphore_wait(pltpu.get_barrier_semaphore(), 10)


class Ring:
    def __init__(self, links, axis, source, landing):
        self.links, self.axis, self.source, self.landing = links, axis, source, landing
        self.numbers = [links.number() for _ in range(3)]

    def copy(self, step, sender):
        return self.links.copy(
            self.numbers[step - 1],
            self.source(step),
            self.landing(step, sender),
            peer(self.axis, step),
        )

    def start(self, step):
        self.links.start(self.copy(step, place()[self.axis]))

    def wait(self, step):
        self.copy(step, shifted(place()[self.axis], -step)).wait_recv()

    def wait_all(self):
        for step in (1, 2, 3):
            self.wait(step)

    def sent(self):
        for step in (1, 2, 3):
            self.links.sent(self.numbers[step - 1])


class Across:
    def __init__(self, links, source, landing):
        mine = lax.axis_index("dp")
        self.links, self.number = links, links.number()
        links.start(links.copy(self.number, source, landing(mine), other_core()))
        self.came = links.copy(self.number, source, landing(1 - mine), other_core())

    def wait(self):
        self.came.wait_recv()

    def sent(self):
        self.links.sent(self.number)


class Links:
    def __init__(self, send, recv):
        self.send, self.recv, self.used, self.open = send, recv, 0, {}

    def number(self):
        self.used += 1
        return self.used - 1

    def copy(self, number, source, landing, device):
        copy = pltpu.make_async_remote_copy(
            src_ref=source,
            dst_ref=landing,
            send_sem=self.send.at[number],
            recv_sem=self.recv.at[number],
            device_id=device,
            device_id_type=MESH,
        )
        self.latest = (number, copy)
        return copy

    def start(self, copy):
        copy.start()
        self.open[self.latest[0]] = copy

    def sent(self, number):
        self.open.pop(number).wait_send()

    def ring(self, axis, source, landing, begin=True):
        ring = Ring(self, axis, source, landing)
        if begin:
            for step in (1, 2, 3):
                ring.start(step)
        return ring

    def across(self, source, landing):
        return Across(self, source, landing)

    def close(self):
        for number in tuple(self.open):
            self.sent(number)


VMEM = pl.BlockSpec(memory_space=pltpu.VMEM)
SMEM = pl.BlockSpec(memory_space=pltpu.SMEM)


def hold(kind, *shape):
    return pltpu.VMEM(shape, kind)


def run(stage, numbers, ins, outs, scratch, number=None, copies=0):
    flat, shape = jax.tree.flatten(scratch, is_leaf=lambda leaf: not isinstance(leaf, (dict, list)))

    def kernel(*refs):
        count = len(numbers) + len(ins) + len(outs)
        named = dict(zip((*numbers, *ins, *outs), refs))
        named.update(jax.tree.unflatten(shape, refs[count : count + len(flat)]))
        r = SimpleNamespace(**named)
        if copies:
            r.links = Links(*refs[count + len(flat) :])
        stage(r)

    remote = dict(collective_id=number, has_side_effects=True) if copies else {}
    results = pl.pallas_call(
        kernel,
        out_shape=[jax.ShapeDtypeStruct(out.shape, out.dtype) for out in outs.values()],
        in_specs=[SMEM] * len(numbers) + [VMEM] * len(ins),
        out_specs=[VMEM] * len(outs),
        scratch_shapes=flat + [pltpu.SemaphoreType.DMA((copies,))] * (2 if copies else 0),
        compiler_params=pltpu.CompilerParams(vmem_limit_bytes=60 * MIB, **remote),
    )(*numbers.values(), *ins.values())
    return dict(zip(outs, results))


def dot32(left, right):
    return jnp.dot(left, right, preferred_element_type=F32)


def dot_nt(left, right):
    return lax.dot_general(left, right, (((1,), (1,)), ((), ())), preferred_element_type=F32)


def dot_tn(left, right):
    return lax.dot_general(left, right, (((0,), (0,)), ((), ())), preferred_element_type=F32)


def add_all(values):
    total = values[0].astype(F32)
    for value in values[1:]:
        total += value.astype(F32)
    return total


def loop(count, body):
    def step(number, unused):
        body(number)
        return unused

    lax.fori_loop(0, count, step, 0)


def my_low(r):
    chip = lax.axis_index("ctx")
    return jnp.minimum(r.block_order[2 * chip], r.block_order[2 * chip + 1])


def low_of(r, chip):
    return jnp.minimum(r.block_order[2 * chip], r.block_order[2 * chip + 1])


def low_first(r, rows):
    chip = lax.axis_index("ctx")
    flip = r.block_order[2 * chip] > r.block_order[2 * chip + 1]
    return jnp.where(flip, jnp.concatenate([rows[64:], rows[:64]], axis=0), rows)


def document_starts(r, places):
    start = jnp.zeros_like(places)
    at = 0
    for number in range(1, 8):
        at = at + r.doc_lengths[0, number - 1]
        start = jnp.where(places >= at, at, start)
    return start


def places_of(r, within, high):
    low = my_low(r)
    return jnp.where(high, 127 - low, low) * 64 + within


def number_table():
    table = np.zeros((8, 768), np.int32)
    k = np.arange(640)
    table[0, :640], table[1, :640] = k % 5, k // 5
    core, y, z, x, row = k // 320, (k // 80) % 4, (k // 20) % 4, (k // 5) % 4, k % 5
    table[2, :640] = (((core * 4 + x) * 4 + y) * 4 + z) * 5 + row
    k = np.arange(768)
    table[3] = np.where(k % 6 < 5, 5 * (k // 6) + k % 6, -1)
    table[4, :256], table[5, :256] = np.arange(256) % 2, np.arange(256) // 2
    return table


def one_hot(rows, numbers):
    shape = (rows, numbers.shape[1])
    return jnp.where(lax.broadcasted_iota(jnp.int32, shape, 0) == numbers, 1.0, 0.0).astype(BF16)


GAINS = ((0, 640, 5, 0), (640, 640, 5, 5), (1280, 640, 5, 10), (1920, 640, 5, 15))
GAINS += ((2560, 256, 2, 20), (2816, 256, 2, 22))
G_ATTN, G_POST_ATTN, G_FFN, G_POST_FFN, G_QUERY, G_KEY = range(6)


def gain_maps(r, number):
    _, columns, held, lane = GAINS[number]
    row = 0 if held == 5 else 4
    rest, owner = r.table[row : row + 1, :columns], r.table[row + 1 : row + 2, :columns]
    lanes = one_hot(128, rest + lane)
    owners = lax.broadcasted_iota(jnp.int32, (128, columns), 0) == owner
    return lanes, owners


def gain(r, number):
    at, columns, _, _ = GAINS[number]
    return r.gains[0:1, at : at + columns]


def rows_of(r, base, weight, count):
    tiles = weight.shape[1] // 128
    for tile in range(tiles):
        r.stage[pl.ds(base + tile, count, stride=tiles)] = weight[
            :, 128 * tile : 128 * tile + 128
        ].astype(F32)


def columns_of(r, base, count, tiles, tile):
    return r.stage[pl.ds(base + tile, count, stride=tiles)]


def pack(r):
    rows_of(r, 0, r.gate_weight, 5)
    rows_of(r, 80, r.output_weight, 8)
    rows_of(r, 128, r.up_weight, 5)
    rows_of(r, 208, r.query_weight, 5)
    rows_of(r, 256, r.down_weight, 16)
    for tile in range(4):
        weight = (r.key_weight, r.value_weight)[tile // 2]
        half = 128 * (tile % 2)
        r.stage[pl.ds(336 + tile, 5, stride=4)] = weight[:, half : half + 128].astype(F32)
    r.stage[356:357] = r.gain_row[...].astype(F32)
    spot = place()
    for part, ref in enumerate(r.p):
        first, second, _ = ORDERS[part]
        rows = ref.shape[2]
        ref[spot[second], spot[first]] = r.stage[128 * part : 128 * part + rows].astype(BF16)
    core = lax.axis_index("dp")
    x, y, z = spot
    r.u[0][core, x, y, z] = r.stage[336:352].astype(BF16)
    r.u[1][core, y, z, x] = r.stage[352:368].astype(BF16)


def tables(r):
    r.x[...] = low_first(r, r.tokens[0].astype(F32))
    rows = lax.broadcasted_iota(jnp.int32, (128, 1), 0)
    places = places_of(r, rows % 64, rows >= 64)
    position = (places - document_starts(r, places)).astype(F32)
    angles = position * r.frequency[...]
    r.cos[...] = jnp.cos(angles)
    r.sin[...] = jnp.sin(angles)
    r.turning[...] = one_hot(640, r.table[2:3, :640])
    r.sixes[...] = one_hot(640, r.table[3:4, :])


NEVER = -(1 << 20)


def key_tables(r):
    mine = my_low(r)

    def chunk(number, token):
        plane = number % 4
        row = 4 * token + number
        for slot in range(16):
            spot = [slot // 4, slot % 4]
            spot.insert(chunk_axis(token), plane)
            low = low_of(r, spot[0] * 16 + spot[1] * 4 + spot[2])
            chosen = jnp.where(low < mine, low, 127 - low) * 64
            for_low = jnp.where(low < mine, chosen, NEVER)
            for_high = jnp.where(low == mine, NEVER, chosen)
            r.key_base[row, slot : slot + 1] = jnp.full((1, 128), for_low, jnp.int32)
            r.key_base[16 + row, slot : slot + 1] = jnp.full((1, 128), for_high, jnp.int32)

    for token in range(4):
        loop(4, lambda number, token=token: chunk(number, token))

    def turn(row):
        r.key_rows[pl.ds(row, 1)] = jnp.transpose(key_column(r, row, (row // 4) % 4))[0:1]

    loop(32, turn)


def key_column(r, row, token):
    base = jnp.broadcast_to(r.key_base[row][:, None, :], (16, 16, 128)).reshape(256, 128)
    return base + (lax.broadcasted_iota(jnp.int32, (256, 128), 0) % 16 + 16 * token)


def early(r):
    links = r.links
    core = lax.axis_index("dp")
    spot = place()
    x, y, z = spot

    def small(axis, unit, index_of):
        ref = r.u[unit]
        ring = links.ring(
            axis, lambda step: ref.at[index_of(spot[axis])], lambda step, at: ref.at[index_of(at)]
        )
        held.append(ring)
        return ring

    held = []

    one = small(Z, 0, lambda at: (core, x, y, at))
    two = small(X, 1, lambda at: (core, y, z, at))
    rings = []
    for part, ref in enumerate(r.p):
        first, second, _ = ORDERS[part]
        row = spot[second]
        rings.append(
            links.ring(
                first,
                lambda step, ref=ref, row=row, first=first: ref.at[row, spot[first]],
                lambda step, at, ref=ref, row=row: ref.at[row, at],
            )
        )
    tables(r)
    one.wait_all()
    one = small(Y, 0, lambda at: (core, x, at))
    two.wait_all()
    two = small(Z, 1, lambda at: (core, y, at))
    for part, ref in enumerate(r.p):
        rings[part].wait_all()
        second = ORDERS[part][1]
        rings.append(
            links.ring(
                second,
                lambda step, ref=ref, second=second: ref.at[spot[second]],
                lambda step, at, ref=ref: ref.at[at],
            )
        )
    key_tables(r)
    one.wait_all()
    one = small(X, 0, lambda at: (core, at))
    two.wait_all()
    two = small(Y, 1, lambda at: (core, at))
    spreads = {}
    for part, weights in ((2, (DOWN,)), (0, (GATE, OUTPUT)), (1, (QUERY, UP))):
        rings[3 + part].wait_all()
        for number in weights:
            unpack(r, number)
            if number not in (GATE, UP):
                spreads[number] = Spread(r, number)
    one.wait_all()
    three = links.across(r.u[0].at[core], lambda at: r.u[0].at[at])
    two.wait_all()
    four = links.across(r.u[1].at[core], lambda at: r.u[1].at[at])
    three.wait()
    four.wait()
    return rings, held + [three, four], spreads


def device_loop(body):
    def one(number):
        core, x, y, z = number // 64, (number // 16) % 4, (number // 4) % 4, number % 4
        body(pl.multiple_of(number * 24, 8), (core, x, y, z), (core, y, z, x))

    loop(128, one)


def unpack_small(r):
    def one(row, i0, i1):
        r.stage[pl.ds(row, 16)] = r.u[0][i0].astype(F32)
        r.stage[pl.ds(row + 16, 8)] = r.u[1][i1].astype(F32)[:8]

    device_loop(one)
    for tile in range(4):
        r.w_kv[:, 128 * tile : 128 * tile + 128] = columns_of(r, 0, 768, 4, tile).astype(BF16)
    held = r.stage[pl.ds(20, 128, stride=24)].astype(BF16)
    for number, (at, columns, _, _) in enumerate(GAINS):
        lanes, owners = gain_maps(r, number)
        spread = jnp.where(owners, dot32(held, lanes), 0.0)
        r.gains[0:1, at : at + columns] = jnp.sum(spread, axis=0, keepdims=True)


WEIGHTS = ((0, 0, 80, False), (0, 80, 40, False), (1, 0, 80, False), (1, 80, 40, False), (2, 0, 80, True))
GATE, OUTPUT, UP, QUERY, DOWN = range(5)


def own_plane(r, number):
    part = WEIGHTS[number][0]
    return weight_plane(r.w[number], number, lax.axis_index("dp"), place()[ORDERS[part][2]])


def weight_plane(ref, number, core, at):
    part, _, _, by_chip = WEIGHTS[number]
    if by_chip:
        return of_plane(ref.at[core], ORDERS[part][2], at)
    return ref.at[core, at]


def plane_tiles(number):
    return ((80, 16), (128, 5), (80, 16), (80, 8), (256, 5))[number]


def unpack(r, number):
    part, first, rows, by_chip = WEIGHTS[number]
    count, tiles = plane_tiles(number)
    plane = own_plane(r, number)

    def one(chip):
        r.stage[pl.ds(pl.multiple_of(chip * rows, 8), rows)] = r.p[part][
            chip // 4, chip % 4, first : first + rows
        ].astype(F32)

    loop(16, one)
    for tile in range(tiles):
        piece = columns_of(r, 0, count, tiles, tile).astype(BF16)
        lanes = slice(128 * tile, 128 * tile + 128)
        if by_chip:
            plane[:, :, :, lanes] = piece.reshape(4, 4, 16, 128)
        else:
            plane[:, lanes] = piece


def inverse_rms(values):
    return lax.rsqrt(jnp.mean(values * values, axis=-1, keepdims=True) + EPSILON)


def rms_scale(values, weights):
    return values * inverse_rms(values) * weights


def norm_back(values, weights, incoming):
    inverse = inverse_rms(values)
    normal = values * inverse
    scaled = incoming * weights
    back = (scaled - normal * jnp.mean(scaled * normal, axis=-1, keepdims=True)) * inverse
    return back, jnp.sum(incoming * normal, axis=0, keepdims=True)


def rope(r, u):
    cos, sin = r.cos[...], r.sin[...]
    one, two = u[:, :128], u[:, 128:]
    return jnp.concatenate([one * cos - two * sin, two * cos + one * sin], axis=1)


def rope_back(r, e):
    cos, sin = r.cos[...], r.sin[...]
    one, two = e[:, :128], e[:, 128:]
    return jnp.concatenate([one * cos + two * sin, two * cos - one * sin], axis=1)


def turned(r, values):
    return dot32(values, r.turning[...]).astype(BF16)


def unturned(r, values):
    return dot_nt(values.astype(BF16), r.turning[...])


def keys_values(r):
    x = r.x[...]
    normed = rms_scale(x, gain(r, G_ATTN)).astype(BF16)
    r.normed[...] = normed
    r.normed_six[...] = dot32(normed, r.sixes[...]).astype(BF16)
    raw = dot32(r.normed_six[...], r.w_kv[...])
    r.key_raw[...] = raw[:, :HEAD]
    keys = rope(r, rms_scale(raw[:, :HEAD], gain(r, G_KEY)))
    both = jnp.concatenate([keys, raw[:, HEAD:]], axis=1).astype(BF16)
    for block in range(2):
        for unit, (token, lane) in enumerate(UNITS):
            row = 64 * block + 16 * token
            r.kv3[block, 16 * unit : 16 * unit + 16] = both[
                row : row + 16, 128 * lane : 128 * lane + 128
            ]
    own = r.kv3[0]
    r.kv3[2] = jnp.where(my_low(r) == 63, own, jnp.zeros_like(own))


def of_plane(ref, axis, at, *rest):
    index = [slice(None)] * 3
    index[axis] = at
    return ref.at[(*index, *rest)]


def chip_of(spot, axis, step):
    spot = list(spot)
    spot[axis] = shifted(spot[axis], step)
    return spot[0] * 16 + spot[1] * 4 + spot[2]


def plane_loop(part, body):
    first, second, last = ORDERS[part]

    def one(number):
        spot = [None] * 3
        spot[first], spot[second], spot[last] = number % 4, number // 4, place()[last]
        body(spot, number // 4, number % 4)

    loop(16, one)


class Spread:
    def __init__(self, r, number):
        self.links, self.axis = r.links, ORDERS[WEIGHTS[number][0]][2]
        self.at = lambda core, at: weight_plane(r.w[number], number, core, at)
        self.core, self.mine = lax.axis_index("dp"), place()[self.axis]
        self.ring = r.links.ring(
            self.axis,
            lambda step: self.at(self.core, self.mine),
            lambda step, at: self.at(self.core, at),
        )
        self.overs = []
        self.over(self.mine)

    def over(self, at):
        self.overs.append(
            self.links.across(self.at(self.core, at), lambda core: self.at(core, at))
        )

    def pass_on(self):
        for step in (1, 3, 2):
            self.ring.wait(step)
            self.over(shifted(self.mine, -step))

    def finish(self):
        for over in self.overs:
            over.wait()

    def free(self):
        self.ring.sent()
        for over in self.overs:
            over.sent()


def gather_first(r):
    rings = []
    for part, (row, rows) in enumerate(KV_ROWS):
        own = r.kv3.at[:, pl.ds(row, rows)]
        rings.append(
            r.links.ring(
                ORDERS[part][0],
                lambda step, own=own: own,
                lambda step, at, ref=r.f1[part]: ref.at[at],
            )
        )
    return rings


def gather_second(r, firsts):
    spot = place()
    rings = []
    for part, (row, rows) in enumerate(KV_ROWS):
        first, second, _ = ORDERS[part]
        f1, g2, mine = r.f1[part], r.g2[part], spot[second]
        f1[spot[first]] = r.kv3[:, row : row + rows]
        firsts[part].wait_all()
        for at in range(4):
            g2[mine, 2 * at] = f1[at, 0]
            g2[mine, 2 * at + 1] = f1[at, 1]
        g2[mine, 8] = add_all([f1[at, 2] for at in range(4)]).astype(BF16)
        rings.append(
            r.links.ring(
                second,
                lambda step, g2=g2, mine=mine: g2.at[mine],
                lambda step, at, g2=g2: g2.at[at],
            )
        )
    return rings


def gather_third(r, seconds):
    spot = place()
    low_me = my_low(r)
    rings, specials = [], []
    for part, (row, rows) in enumerate(KV_ROWS):
        first, second, last = ORDERS[part]
        g2, sel, sp, rsp = r.g2[part], r.sel[part], r.sp[part], r.rsp[part]
        seconds[part].wait_all()
        targets = [low_of(r, chip_of(spot, last, step)) for step in (1, 2, 3)]

        def choose(at, i2, i1, g2=g2, sel=sel, row=row, rows=rows, last=last, targets=targets):
            low = g2[i2, 2 * i1]
            high = g2[i2, 2 * i1 + 1]
            source = low_of(r, chip_of(at, last, 0))
            plane = [at[axis] for axis in (X, Y, Z) if axis != last]
            r.slots[at[0], at[1], at[2], pl.ds(row, rows)] = jnp.where(source < low_me, low, high)
            for step in (1, 2, 3):
                sel[step - 1, plane[0], plane[1]] = jnp.where(
                    source < targets[step - 1], low, high
                )

        plane_loop(part, choose)
        sp[...] = add_all([g2[at, 8] for at in range(4)]).astype(BF16)
        rings.append(
            r.links.ring(
                last,
                lambda step, sel=sel: sel.at[step - 1],
                lambda step, at, row=row, rows=rows, last=last: of_plane(
                    r.slots, last, at, pl.ds(row, rows)
                ),
            )
        )
        specials.append(
            r.links.ring(
                last, lambda step, sp=sp: sp, lambda step, at, rsp=rsp: rsp.at[at]
            )
        )
    r.extra[0:2] = r.kv3[0:2]
    return rings, specials


def gather_special(r, specials):
    spot = place()
    for part, (row, rows) in enumerate(KV_ROWS):
        rsp = r.rsp[part]
        specials[part].wait_all()
        rsp[spot[ORDERS[part][2]]] = r.sp[part][...]
        r.extra[2, row : row + rows] = add_all([rsp[at] for at in range(4)]).astype(BF16)


QUARTER = 1.0 / 16
POWER = QUARTER * 1.4426950408889634


def chunk_axis(token):
    return ORDERS[token][2] if token < 3 else X


def chunk_index(token, plane):
    index = [slice(None)] * 3
    index[chunk_axis(token)] = plane
    return tuple(index)


def unit_rows(token, lane):
    return pl.ds(16 * UNITS.index((token, lane)), 16)


def chunk_kv(r, token, plane):
    index = chunk_index(token, plane)
    quarters = [
        r.slots[(*index, unit_rows(token, lane))].reshape(256, 128) for lane in range(4)
    ]
    return jnp.concatenate(quarters[:2], axis=1), jnp.concatenate(quarters[2:], axis=1)


def extra_kv(r):
    quarters = [
        jnp.concatenate(
            [r.extra[block, unit_rows(token, lane)] for block in range(3) for token in range(4)],
            axis=0,
        )
        for lane in range(4)
    ]
    return jnp.concatenate(quarters[:2], axis=1), jnp.concatenate(quarters[2:], axis=1)


def extra_places(r, numbers):
    low = my_low(r)
    block = jnp.where(numbers < 64, low, jnp.where(numbers < 128, 127 - low, 63))
    gone = (numbers >= 128) & (low == 63)
    return jnp.where(gone, 1 << 20, block * 64 + numbers % 64)


def query_places(r, numbers):
    return places_of(r, numbers % 64, numbers >= 256)


def attention(r, thirds, specials, between):
    spot = place()
    numbers = lax.broadcasted_iota(jnp.int32, (512, 1), 0)
    latest = query_places(r, numbers)
    earliest = document_starts(r, latest)
    query = r.query[...]
    r.attn[...] = jnp.zeros_like(r.attn)
    r.total[...] = jnp.zeros_like(r.total)

    def add(weights, values):
        total = weights[:, :128]
        if weights.shape[1] == 256:
            total = total + weights[:, 128:]
            r.total[...] += total
        else:
            r.total[...] += total
            r.total[:, :64] += weights[:, 128:]
        r.attn[...] += dot32(weights.astype(BF16), values)

    def chunk(token, plane):
        keys, values = chunk_kv(r, token, plane)
        scores = dot_nt(query, keys)
        row = 4 * token + plane
        allowed = jnp.concatenate(
            [
                r.key_rows[pl.ds(row, 1)] >= earliest[:256],
                r.key_rows[pl.ds(16 + row, 1)] >= earliest[256:],
            ],
            axis=0,
        )
        add(jnp.where(allowed, jnp.exp2(scores * POWER), 0.0), values)

    for token in range(3):
        chunk(token, spot[chunk_axis(token)])
    between(0)
    for number, step in enumerate((1, 3, 2)):
        for token in range(3):
            thirds[token].wait(step)
            chunk(token, shifted(spot[chunk_axis(token)], -step))
        between(number + 1)
    for plane in range(4):
        chunk(3, plane)
    gather_special(r, specials)
    keys, values = extra_kv(r)
    scores = dot_nt(query, keys)
    places = extra_places(r, lax.broadcasted_iota(jnp.int32, (1, 192), 1))
    allowed = (places >= earliest) & (places <= latest)
    add(jnp.where(allowed, jnp.exp2(scores * POWER), 0.0), values)
    total = jnp.sum(r.total[...], axis=1, keepdims=True)
    r.attn[...] = r.attn[...] / total
    r.total[...] = jnp.broadcast_to(jnp.log2(total), (512, 128))


def attention_back(r, between):
    spot = place()
    numbers = lax.broadcasted_iota(jnp.int32, (1, 512), 1)
    latest = query_places(r, numbers)
    earliest = document_starts(r, latest)
    query, grad_out = r.query[...], r.grad_attn[...]
    log_total = jnp.transpose(r.total[...])[0:1]
    row_dot = jnp.transpose(r.dots[...])[0:1]
    r.grad_query[...] = jnp.zeros_like(r.grad_query)

    def grads_of(keys, values, allowed):
        scores = dot_nt(keys, query)
        probs = jnp.where(allowed, jnp.exp2(scores * POWER - log_total), 0.0)
        grad_probs = dot_nt(values, grad_out)
        grad_scores = (probs * (grad_probs - row_dot)).astype(BF16)
        grad_values = dot32(probs.astype(BF16), grad_out)
        grad_keys = dot32(grad_scores, query) * QUARTER
        r.grad_query[...] += dot_tn(grad_scores, keys)
        return jnp.concatenate([grad_keys, grad_values], axis=1).astype(BF16)

    def chunk(token, plane):
        keys, values = chunk_kv(r, token, plane)
        row = 4 * token + plane
        low, high = key_column(r, row, token), key_column(r, 16 + row, token)
        allowed = jnp.concatenate([low, low, high, high], axis=1) >= earliest
        grads = grads_of(keys, values, allowed)
        index = chunk_index(token, plane)
        for lane in range(4):
            r.slots[(*index, unit_rows(token, lane))] = grads[
                :, 128 * lane : 128 * lane + 128
            ].reshape(4, 4, 16, 128)

    for plane in range(4):
        chunk(3, plane)
    between(0)
    rings, specials = scatter_third(r)
    for number, step in enumerate((1, 3, 2)):
        for token in range(3):
            chunk(token, shifted(spot[chunk_axis(token)], step))
            rings[token].start(step)
        between(number + 1)
    keys, values = extra_kv(r)
    places = extra_places(r, lax.broadcasted_iota(jnp.int32, (192, 1), 0))
    grads = grads_of(keys, values, (places >= earliest) & (places <= latest))
    for block in range(3):
        for unit, (token, lane) in enumerate(UNITS):
            row = 64 * block + 16 * token
            r.grad_extra[block, 16 * unit : 16 * unit + 16] = grads[
                row : row + 16, 128 * lane : 128 * lane + 128
            ]
    for ring in specials:
        for step in (1, 2, 3):
            ring.start(step)
    for token in range(3):
        chunk(token, spot[chunk_axis(token)])
    return rings, specials


GELU = 0.7978845608028654


def head_rows(block, head):
    start = 256 * block + 64 * head
    return slice(start, start + 64)


def queries(r):
    r.normed_b[...] = turned(r, r.normed[...])
    r.query_raw[...] = dot32(r.normed_b[...], r.w[QUERY][...].reshape(640, 1024))
    for head in range(HEADS):
        raw = r.query_raw[:, HEAD * head : HEAD * head + HEAD]
        rotated = rope(r, rms_scale(raw, gain(r, G_QUERY))).astype(BF16)
        for block in range(2):
            r.query[head_rows(block, head)] = rotated[64 * block : 64 * block + 64]


def gelu_parts(gate):
    inner = jnp.tanh(GELU * (gate + 0.044715 * gate * gate * gate))
    return 0.5 * gate * (1.0 + inner), inner


def columns(weight, at, width):
    rows = 8 * weight.shape[2]
    return weight[:, :, :, at : at + width].reshape(rows, width)


def down_rows(ref, number):
    return ref.at[number // 2, pl.ds(2 * (number % 2), 2)]


def feed_forward(r, spreads):
    spreads[OUTPUT].finish()
    for block in range(2):
        for head in range(HEADS):
            r.attn_low[64 * block : 64 * block + 64, HEAD * head : HEAD * head + HEAD] = r.attn[
                head_rows(block, head)
            ].astype(BF16)
    r.proj[...] = dot32(r.attn_low[...], r.w[OUTPUT][...].reshape(1024, 640))
    r.mid[...] = r.x[...] + rms_scale(r.proj[...], gain(r, G_POST_ATTN))
    r.ffn_in[...] = rms_scale(r.mid[...], gain(r, G_FFN)).astype(BF16)
    r.ffn_in_b[...] = turned(r, r.ffn_in[...])
    spreads[GATE].finish()
    spreads[UP].finish()
    for number in range(4):
        at = slice(512 * number, 512 * number + 512)
        gate = dot32(r.ffn_in[...], columns(r.w[GATE], 512 * number, 512))
        up = dot32(r.ffn_in_b[...], columns(r.w[UP], 512 * number, 512))
        r.gate[:, at] = gate
        r.up[:, at] = up
        r.hidden[:, at] = (gelu_parts(gate)[0] * up).astype(BF16)
    spreads[DOWN].finish()
    r.ffn_out[...] = dot32(r.hidden[...], r.w[DOWN][...].reshape(2048, 640))
    out = r.mid[...] + rms_scale(r.ffn_out[...], gain(r, G_POST_FFN))
    r.block_out[...] = low_first(r, out.astype(BF16))


def note_gain(r, number, term):
    at, count, _, _ = GAINS[number]
    r.gain_sums[0:1, at : at + count] = term


def feed_forward_back(r, spreads):
    for number in (GATE, OUTPUT, UP, DOWN):
        spreads[number].free()
    grad_out = low_first(r, r.out_cot[0].astype(F32))
    grad_ffn_out, term = norm_back(r.ffn_out[...], gain(r, G_POST_FFN), grad_out)
    note_gain(r, G_POST_FFN, term)
    low_grad = grad_ffn_out.astype(BF16)
    r.low_grad[...] = low_grad
    grad_in = jnp.zeros((128, 640), F32)
    grad_in_b = jnp.zeros((128, 640), F32)
    for number in range(4):
        at = slice(512 * number, 512 * number + 512)
        down = down_rows(r.w[DOWN], number)
        grad_hidden = dot_nt(low_grad, down[...].reshape(512, 640))
        down[...] = (
            dot_tn(r.hidden[:, at], low_grad).astype(BF16).reshape(2, 4, 4, 16, 640)
        )
        gate, up = r.gate[:, at], r.up[:, at]
        activated, inner = gelu_parts(gate)
        slope = 0.5 * (1.0 + inner) + 0.5 * gate * (1.0 - inner * inner) * GELU * (
            1.0 + 3 * 0.044715 * gate * gate
        )
        grad_gate = (grad_hidden * up * slope).astype(BF16)
        grad_up = (grad_hidden * activated).astype(BF16)
        grad_in += dot_nt(grad_gate, columns(r.w[GATE], 512 * number, 512))
        grad_in_b += dot_nt(grad_up, columns(r.w[UP], 512 * number, 512))
        term = dot_tn(r.ffn_in[...], grad_gate).astype(BF16)
        r.w[GATE][:, :, :, at] = term.reshape(2, 4, 80, 512)
        term = dot_tn(r.ffn_in_b[...], grad_up).astype(BF16)
        r.w[UP][:, :, :, at] = term.reshape(2, 4, 80, 512)
    halves = {number: send_half(r, number) for number in (DOWN, GATE, UP)}
    grad_in = grad_in + unturned(r, grad_in_b)
    back, term = norm_back(r.mid[...], gain(r, G_FFN), grad_in)
    note_gain(r, G_FFN, term)
    grad_mid = grad_out + back
    r.grad_mid[...] = grad_mid
    back, term = norm_back(r.proj[...], gain(r, G_POST_ATTN), grad_mid)
    note_gain(r, G_POST_ATTN, term)
    proj_low = back.astype(BF16)
    grad_attn = dot_nt(proj_low, r.w[OUTPUT][...].reshape(1024, 640)).astype(BF16)
    term = dot_tn(r.attn_low[...], proj_low).astype(BF16)
    r.w[OUTPUT][...] = term.reshape(2, 4, 128, 640)
    halves[OUTPUT] = send_half(r, OUTPUT)
    for block in range(2):
        for head in range(HEADS):
            r.grad_attn[head_rows(block, head)] = grad_attn[
                64 * block : 64 * block + 64, HEAD * head : HEAD * head + HEAD
            ]
    dots = jnp.sum(r.grad_attn[...].astype(F32) * r.attn[...], axis=1, keepdims=True)
    r.dots[...] = jnp.broadcast_to(dots, (512, 128))
    return halves


def queries_back(r, spreads):
    total = jnp.zeros((1, HEAD), F32)
    for head in range(HEADS):
        at = slice(HEAD * head, HEAD * head + HEAD)
        grad = jnp.concatenate([r.grad_query[head_rows(block, head)] for block in range(2)], axis=0)
        back, term = norm_back(
            r.query_raw[:, at], gain(r, G_QUERY), rope_back(r, grad * QUARTER)
        )
        total += term
        r.query_low[:, at] = back.astype(BF16)
    note_gain(r, G_QUERY, total)
    r.grad_normed[...] = unturned(r, dot_nt(r.query_low[...], r.w[QUERY][...].reshape(640, 1024)))
    spreads[QUERY].free()
    term = dot_tn(r.normed_b[...], r.query_low[...]).astype(BF16)
    r.w[QUERY][...] = term.reshape(2, 4, 80, 1024)
    return send_half(r, QUERY)


def send_half(r, number):
    grad, half = r.w[number], r.half[number]
    return r.links.across(grad.at[1 - lax.axis_index("dp")], lambda at: half)


def sum_halves(r, number, over):
    part, _, _, by_chip = WEIGHTS[number]
    last = ORDERS[part][2]
    core, mine = lax.axis_index("dp"), place()[last]
    grad, half, land = r.w[number], r.half[number], r.landed[number]
    over.wait()

    def join(*at):
        index = (core, *at)
        grad[index] = (grad[index].astype(F32) + half[at].astype(F32)).astype(BF16)

    if by_chip:
        loop(16, lambda at: join(at // 4, at % 4))
    else:
        rows = half.shape[1] // 16
        loop(
            4 * rows,
            lambda at: join(at // rows, pl.ds(pl.multiple_of((at % rows) * 16, 16), 16)),
        )
    return r.links.ring(
        last,
        lambda step: weight_plane(grad, number, core, shifted(mine, step)),
        lambda step, at: land.at[step - 1],
    )


def repack(r, number, ring):
    part, first, rows, by_chip = WEIGHTS[number]
    count, tiles = plane_tiles(number)
    own, land = own_plane(r, number), r.landed[number]
    ring.wait_all()
    for tile in range(tiles):
        lanes = slice(128 * tile, 128 * tile + 128)
        index = (slice(None),) * (3 if by_chip else 1) + (lanes,)
        total = add_all([own[index]] + [land[(step, *index)] for step in range(3)])
        r.stage[pl.ds(tile, count, stride=tiles)] = total.reshape(count, 128)

    def one(chip):
        r.p[part][chip // 4, chip % 4, first : first + rows] = r.stage[
            pl.ds(pl.multiple_of(chip * rows, 8), rows)
        ].astype(BF16)

    loop(16, one)


def late_second(r, part):
    second = ORDERS[part][1]
    mine = place()[second]
    return r.links.ring(
        second,
        lambda step: r.p[part].at[shifted(mine, step)],
        lambda step, at: r.second[part].at[step - 1],
    )


def late_first(r, part, ring):
    first, second, _ = ORDERS[part]
    mine, own = place()[first], place()[second]
    ring.wait_all()
    for at in range(4):
        r.line[part][at] = add_all(
            [r.p[part][own, at]] + [r.second[part][step, at] for step in range(3)]
        ).astype(BF16)
    return r.links.ring(
        first,
        lambda step: r.line[part].at[shifted(mine, step)],
        lambda step, at: r.first[part].at[step - 1],
    )


def late_end(r, part, ring, out):
    mine = place()[ORDERS[part][0]]
    ring.wait_all()
    out[...] = add_all([r.line[part][mine]] + [r.first[part][step] for step in range(3)])


def scatter_third(r):
    spot = place()
    rings, specials = [], []
    for part, (row, rows) in enumerate(KV_ROWS):
        last = ORDERS[part][2]
        rings.append(
            r.links.ring(
                last,
                lambda step, row=row, rows=rows, last=last: of_plane(
                    r.slots, last, shifted(spot[last], step), pl.ds(row, rows)
                ),
                lambda step, at, rb=r.rb[part]: rb.at[step - 1],
                begin=False,
            )
        )
        specials.append(
            r.links.ring(
                last,
                lambda step, row=row, rows=rows: r.grad_extra.at[2, pl.ds(row, rows)],
                lambda step, at, rs=r.rs[part]: rs.at[step - 1],
                begin=False,
            )
        )
    return rings, specials


def scatter_second(r, thirds, specials):
    spot = place()
    me = lax.axis_index("ctx")
    low_me = my_low(r)
    rings = []
    for part, (row, rows) in enumerate(KV_ROWS):
        first, second, last = ORDERS[part]
        rb, rs, total, land = r.rb[part], r.rs[part], r.g2[part], r.r2[part]
        thirds[part].wait_all()
        specials[part].wait_all()
        special = add_all([r.grad_extra[2, row : row + rows]] + [rs[step] for step in range(3)])
        for at in range(4):
            total[at, 8] = special.astype(BF16)
        senders = [low_of(r, chip_of(spot, last, -step)) for step in (1, 2, 3)]

        def collect(at, i2, i1, rb=rb, total=total, row=row, rows=rows, last=last, senders=senders):
            chip = chip_of(at, last, 0)
            source = low_of(r, chip)
            plane = [at[axis] for axis in (X, Y, Z) if axis != last]
            own = r.slots[at[0], at[1], at[2], pl.ds(row, rows)].astype(F32)
            none = jnp.zeros_like(own)
            low = jnp.where(source < low_me, own, none)
            high = jnp.where(source < low_me, none, own)
            low += jnp.where(chip == me, r.grad_extra[0, pl.ds(row, rows)].astype(F32), none)
            high += jnp.where(chip == me, r.grad_extra[1, pl.ds(row, rows)].astype(F32), none)
            for step in (1, 2, 3):
                came = rb[step - 1, plane[0], plane[1]].astype(F32)
                low += jnp.where(source < senders[step - 1], came, none)
                high += jnp.where(source < senders[step - 1], none, came)
            total[i2, 2 * i1] = low.astype(BF16)
            total[i2, 2 * i1 + 1] = high.astype(BF16)

        plane_loop(part, collect)
        rings.append(
            r.links.ring(
                second,
                lambda step, total=total, second=second: total.at[shifted(spot[second], step)],
                lambda step, at, land=land: land.at[step - 1],
            )
        )
    return rings


def scatter_first(r, seconds):
    spot = place()
    rings = []
    for part in range(3):
        first, second, _ = ORDERS[part]
        total, land, line, end = r.g2[part], r.r2[part], r.f1[part], r.r1[part]
        seconds[part].wait_all()

        def pick(index, total=total, land=land, mine=spot[second]):
            return add_all([total[mine, index]] + [land[step, index] for step in range(3)]).astype(
                BF16
            )

        special = pick(8)
        for at in range(4):
            line[at, 0] = pick(2 * at)
            line[at, 1] = pick(2 * at + 1)
            line[at, 2] = special
        rings.append(
            r.links.ring(
                first,
                lambda step, line=line, first=first: line.at[shifted(spot[first], step)],
                lambda step, at, end=end: end.at[step - 1],
            )
        )
    return rings


def scatter_end(r, firsts):
    spot = place()
    for part, (row, rows) in enumerate(KV_ROWS):
        firsts[part].wait_all()
        mine = spot[ORDERS[part][0]]
        for index in range(3):
            r.kv_sum[index, row : row + rows] = add_all(
                [r.f1[part][mine, index]] + [r.r1[part][step, index] for step in range(3)]
            )


def keys_values_back(r):
    special = jnp.where(my_low(r) == 63, 1.0, 0.0)
    r.kv_sum[0] = r.kv_sum[0] + r.kv_sum[2] * special
    lanes = []
    for lane in range(4):
        pieces = [
            r.kv_sum[block, unit_rows(token, lane)] for block in range(2) for token in range(4)
        ]
        lanes.append(jnp.concatenate(pieces, axis=0))
    grad_keys = jnp.concatenate(lanes[:2], axis=1)
    grad_values = jnp.concatenate(lanes[2:], axis=1)
    back, term = norm_back(r.key_raw[...], gain(r, G_KEY), rope_back(r, grad_keys))
    note_gain(r, G_KEY, term)
    kv_low = jnp.concatenate([back, grad_values], axis=1).astype(BF16)
    terms = dot_tn(r.normed_six[...], kv_low)
    for tile in range(4):
        r.stage[pl.ds(tile, 768, stride=4)] = terms[:, 128 * tile : 128 * tile + 128]
    grad_six = dot_nt(kv_low, r.w_kv[...]).astype(BF16)
    grad_normed = dot_nt(grad_six, r.sixes[...]) + r.grad_normed[...]
    back, term = norm_back(r.x[...], gain(r, G_ATTN), grad_normed)
    note_gain(r, G_ATTN, term)
    r.tokens_grad[...] = low_first(r, (r.grad_mid[...] + back).astype(BF16))
    held = jnp.zeros((128, 128), F32)
    for number, (at, count, _, _) in enumerate(GAINS):
        lanes, owners = gain_maps(r, number)
        term = jnp.where(owners, r.gain_sums[0:1, at : at + count], 0.0).astype(BF16)
        held += dot_nt(term, lanes)
    r.stage[pl.ds(20, 128, stride=24)] = held
    r.stage[3072:3088] = jnp.zeros((16, 128), F32)

    def one(row, i0, i1):
        r.u[0][i0] = r.stage[pl.ds(row, 16)].astype(BF16)
        r.u[1][i1] = r.stage[pl.ds(row + 16, 16)].astype(BF16)

    device_loop(one)


def small_sums(r, between):
    links = r.links
    core = lax.axis_index("dp")
    spot = place()
    overs = [links.across(ref.at[1 - core], lambda at, to=to: to) for ref, to in zip(r.u, r.vh)]
    axes = ((X, Y, Z), (Y, Z, X))
    rings = []
    for unit, order in enumerate(axes):
        half, own, land = r.vh[unit], r.u[unit], r.land3[unit]
        overs[unit].wait()

        def join(number, half=half, own=own):
            at = (number // 4, number % 4)
            index = (core, *at)
            own[index] = (own[index].astype(F32) + half[at].astype(F32)).astype(BF16)

        loop(16, join)
        axis = order[0]
        rings.append(
            links.ring(
                axis,
                lambda step, own=own, axis=axis: own.at[core, shifted(spot[axis], step)],
                lambda step, at, land=land: land.at[step - 1],
            )
        )
    between[0]()
    later = []
    for unit, order in enumerate(axes):
        own, land, out, to = r.u[unit], r.land3[unit], r.sum2[unit], r.land2[unit]
        rings[unit].wait_all()
        mine = spot[order[0]]

        def add(at, own=own, land=land, out=out, mine=mine):
            out[at] = add_all([own[core, mine, at]] + [land[step, at] for step in range(3)]).astype(
                BF16
            )

        loop(4, add)
        axis = order[1]
        later.append(
            links.ring(
                axis,
                lambda step, out=out, axis=axis: out.at[shifted(spot[axis], step)],
                lambda step, at, to=to: to.at[step - 1],
            )
        )
    between[1]()
    last = []
    for unit, order in enumerate(axes):
        own, land, out, to = r.sum2[unit], r.land2[unit], r.sum1[unit], r.land1[unit]
        later[unit].wait_all()
        out[...] = add_all([own[spot[order[1]]]] + [land[step] for step in range(3)]).astype(BF16)
        axis = order[2]
        last.append(
            links.ring(
                axis,
                lambda step, out=out, axis=axis: out.at[shifted(spot[axis], step)],
                lambda step, at, to=to: to.at[step - 1],
            )
        )
    between[2]()
    for unit, order in enumerate(axes):
        last[unit].wait_all()
        r.fk[16 * unit : 16 * unit + 16] = add_all(
            [r.sum1[unit][spot[order[2]]]] + [r.land1[unit][step] for step in range(3)]
        )


def layer(r):
    greet()
    pack(r)
    greeted()
    early_rings, early_held, spreads = early(r)
    unpack_small(r)
    keys_values(r)
    firsts = gather_first(r)
    seconds = gather_second(r, firsts)
    for number in (GATE, UP):
        spreads[number] = Spread(r, number)
    for number in (QUERY, OUTPUT, DOWN):
        spreads[number].pass_on()
    thirds, specials = gather_third(r, seconds)
    spreads[QUERY].finish()
    queries(r)

    def pass_on(number):
        if number == 0:
            spreads[GATE].pass_on()
            spreads[UP].pass_on()

    attention(r, thirds, specials, pass_on)
    feed_forward(r, spreads)
    halves = feed_forward_back(r, spreads)
    rings = {}

    def between(number):
        if number == 0:
            for weight in (DOWN, GATE):
                rings[weight] = sum_halves(r, weight, halves[weight])
        if number == 1:
            for weight in (UP, OUTPUT):
                rings[weight] = sum_halves(r, weight, halves[weight])

    thirds, third_specials = attention_back(r, between)
    half = queries_back(r, spreads)
    for ring in early_rings:
        ring.sent()
    repack(r, DOWN, rings[DOWN])
    late = {2: late_second(r, 2)}
    for ring in seconds:
        ring.sent()
    seconds = scatter_second(r, thirds, third_specials)
    rings[QUERY] = sum_halves(r, QUERY, half)
    repack(r, GATE, rings[GATE])
    repack(r, OUTPUT, rings[OUTPUT])
    late[0] = late_second(r, 0)
    firsts = scatter_first(r, seconds)
    repack(r, UP, rings[UP])
    repack(r, QUERY, rings[QUERY])
    late[1] = late_second(r, 1)
    scatter_end(r, firsts)
    for copy in early_held:
        copy.sent()
    keys_values_back(r)

    def begin_last():
        for part in (2, 0, 1):
            late[part] = late_first(r, part, late[part])

    def finish_last():
        for part, out in enumerate((r.fa, r.fb, r.fc)):
            late_end(r, part, late[part], out)

    small_sums(r, (begin_last, finish_last, lambda: None))
    r.links.close()


def end(r):
    def rows(out, source, base, count, tiles):
        r.stage[base : base + count * tiles] = source
        for tile in range(tiles):
            out[:, 128 * tile : 128 * tile + 128] = columns_of(r, base, count, tiles, tile)

    rows(r.gate_grad, r.fa[0:80], 0, 5, 16)
    rows(r.output_grad, r.fa[80:120], 80, 8, 5)
    rows(r.up_grad, r.fb[0:80], 128, 5, 16)
    rows(r.query_grad, r.fb[80:120], 208, 5, 8)
    rows(r.down_grad, r.fc[...], 256, 16, 5)
    r.stage[336:368] = r.fk[...]
    for tile in range(4):
        out = (r.key_grad, r.value_grad)[tile // 2]
        half = 128 * (tile % 2)
        out[:, half : half + 128] = columns_of(r, 336, 5, 4, tile)
    line = r.fk[16:24]
    gain_grads = (r.grad_attn_norm, r.grad_post_attn, r.grad_ffn_norm, r.grad_post_ffn, r.grad_q, r.grad_k)
    for number, (_, _, held, lane) in enumerate(GAINS):
        out = gain_grads[number]
        moved = line if lane == 0 else pltpu.roll(line, 128 - lane, 1)
        out[...] = moved[4:5, :held]
    r.final_out[0] = r.block_out[...]
    r.final_grad[0] = r.tokens_grad[...]


def by_part(*dims):
    return [hold(BF16, *dims, rows, 128) for _, rows in KV_ROWS]


def by_flat(*dims):
    return [hold(BF16, *dims, rows, 128) for rows in (128, 128, 80)]


def by_unit(*dims):
    return [hold(BF16, *dims, 16, 128) for _ in range(2)]


def by_weight(lead, core):
    return [
        hold(BF16, *core, *lead, 80, 2048),
        hold(BF16, *core, *lead, 128, 640),
        hold(BF16, *core, *lead, 80, 2048),
        hold(BF16, *core, *lead, 80, 1024),
        hold(BF16, *core, *lead, 4, 4, 16, 640),
    ]


def buffers():
    return dict(
        stage=hold(F32, 3088, 128),
        x=hold(F32, 128, 640),
        cos=hold(F32, 128, 128),
        sin=hold(F32, 128, 128),
        gains=hold(F32, 8, 3072),
        gain_sums=hold(F32, 8, 3072),
        turning=hold(BF16, 640, 640),
        sixes=hold(BF16, 640, 768),
        key_base=hold(jnp.int32, 32, 16, 128),
        key_rows=hold(jnp.int32, 32, 256),
        p=by_flat(4, 4),
        second=by_flat(3, 4),
        line=by_flat(4),
        first=by_flat(3),
        u=by_unit(2, 4, 4, 4),
        vh=by_unit(4, 4, 4),
        land3=by_unit(3, 4, 4),
        sum2=by_unit(4, 4),
        land2=by_unit(3, 4),
        sum1=by_unit(4),
        land1=by_unit(3),
        w_kv=hold(BF16, 768, 512),
        w=by_weight((4,), (2,)),
        half=by_weight((4,), ()),
        landed=[
            hold(BF16, 3, 80, 2048),
            hold(BF16, 3, 128, 640),
            hold(BF16, 3, 80, 2048),
            hold(BF16, 3, 80, 1024),
            hold(BF16, 3, 4, 4, 16, 640),
        ],
        kv3=hold(BF16, 3, 256, 128),
        f1=by_part(4, 3),
        g2=by_part(4, 9),
        sel=by_part(3, 4, 4),
        sp=by_part(),
        rsp=by_part(4),
        rb=by_part(3, 4, 4),
        rs=by_part(3),
        r2=by_part(3, 9),
        r1=by_part(3, 3),
        slots=hold(BF16, 4, 4, 4, 256, 128),
        extra=hold(BF16, 3, 256, 128),
        grad_extra=hold(BF16, 3, 256, 128),
        kv_sum=hold(F32, 3, 256, 128),
        normed=hold(BF16, 128, 640),
        normed_six=hold(BF16, 128, 768),
        normed_b=hold(BF16, 128, 640),
        key_raw=hold(F32, 128, 256),
        query_raw=hold(F32, 128, 1024),
        query=hold(BF16, 512, 256),
        attn=hold(F32, 512, 256),
        total=hold(F32, 512, 128),
        dots=hold(F32, 512, 128),
        attn_low=hold(BF16, 128, 1024),
        proj=hold(F32, 128, 640),
        mid=hold(F32, 128, 640),
        ffn_in=hold(BF16, 128, 640),
        ffn_in_b=hold(BF16, 128, 640),
        gate=hold(F32, 128, 2048),
        up=hold(F32, 128, 2048),
        hidden=hold(BF16, 128, 2048),
        ffn_out=hold(F32, 128, 640),
        low_grad=hold(BF16, 128, 640),
        grad_mid=hold(F32, 128, 640),
        grad_attn=hold(BF16, 512, 256),
        grad_query=hold(F32, 512, 256),
        query_low=hold(BF16, 128, 1024),
        grad_normed=hold(F32, 128, 640),
    )


def on_device(
    tokens,
    doc_lengths,
    block_order,
    attn_norm,
    query_weight,
    key_weight,
    value_weight,
    query_gain,
    key_gain,
    output_weight,
    attn_post_norm,
    ffn_norm,
    gate_weight,
    up_weight,
    down_weight,
    ffn_post_norm,
    out_cot,
):
    gain_row = jnp.concatenate(
        [attn_norm, attn_post_norm, ffn_norm, ffn_post_norm, query_gain, key_gain]
        + [jnp.zeros((104,), BF16)]
    )[None]
    frequency = (ROPE_BASE ** (-2.0 * jnp.arange(128, dtype=F32) / 256))[None]
    made = run(
        layer,
        dict(block_order=block_order, doc_lengths=doc_lengths),
        dict(
            tokens=tokens,
            out_cot=out_cot,
            gain_row=gain_row,
            table=jnp.asarray(number_table()),
            frequency=frequency,
            gate_weight=gate_weight,
            output_weight=output_weight,
            up_weight=up_weight,
            query_weight=query_weight,
            down_weight=down_weight,
            key_weight=key_weight,
            value_weight=value_weight,
        ),
        dict(
            block_out=hold(BF16, 128, 640),
            tokens_grad=hold(BF16, 128, 640),
            fa=hold(F32, 128, 128),
            fb=hold(F32, 128, 128),
            fc=hold(F32, 80, 128),
            fk=hold(F32, 32, 128),
        ),
        buffers(),
        number=1,
        copies=260,
    )
    results = run(
        end,
        {},
        made,
        dict(
            final_out=hold(BF16, 1, 128, 640),
            final_grad=hold(BF16, 1, 128, 640),
            grad_attn_norm=hold(F32, 1, 5),
            query_grad=hold(F32, 5, 1024),
            key_grad=hold(F32, 5, 256),
            value_grad=hold(F32, 5, 256),
            grad_q=hold(F32, 1, 2),
            grad_k=hold(F32, 1, 2),
            output_grad=hold(F32, 8, 640),
            grad_post_attn=hold(F32, 1, 5),
            grad_ffn_norm=hold(F32, 1, 5),
            gate_grad=hold(F32, 5, 2048),
            up_grad=hold(F32, 5, 2048),
            down_grad=hold(F32, 16, 640),
            grad_post_ffn=hold(F32, 1, 5),
        ),
        dict(stage=hold(F32, 3088, 128)),
    )
    return tuple(
        value.reshape(-1) if value.shape[0] == 1 and value.ndim == 2 else value
        for value in results.values()
    )


def solution(mesh):
    rows = P(("dp", "ctx"), None)
    vector = P(("dp", "ctx"))
    stream = P("dp", "ctx", None)
    return jax.shard_map(
        on_device,
        mesh=mesh,
        in_specs=(
            stream,
            P("dp", None),
            P(),
            vector,
            rows,
            rows,
            rows,
            vector,
            vector,
            rows,
            vector,
            vector,
            rows,
            rows,
            rows,
            vector,
            stream,
        ),
        out_specs=(
            stream,
            stream,
            vector,
            rows,
            rows,
            rows,
            vector,
            vector,
            rows,
            vector,
            vector,
            rows,
            rows,
            rows,
            vector,
        ),
        check_vma=False,
    )
```

time: 2460 us -> 190 us (0.08)
  waiting for transfers between devices: 1230 us -> 0 us
  blocking collectives: 763 us -> 0 us
  matrix products: 199 us -> 0 us
  Pallas kernels: 0 us -> 185 us
  local copies, waits for them, and re-layouts: 179 us -> 3.26 us
  loops' own time: 34.2 us -> 0 us
  other arithmetic: 33.6 us -> 0.52 us
    reduce_scatter x2 -> x0, waiting for transfers between devices: 1040 us -> none  [the longest x1 659 us: on_device(): lax.psum_scatter(down_term, ('dp', 'ctx'), scatter_dimension=0, tiled=True)]
    all_gather x2 -> x0, blocking collectives: 637 us -> none  [the longest x1 322 us: on_device(): lax.all_gather(value_weight, ('dp', 'ctx'), axis=0, tiled=True)]
    dot_general x165 -> x0, matrix products: 199 us -> none  [the longest x48 63.4 us: block_scores(): jnp.einsum('ihd,jd->hij', query_rot, keys_part, preferred_element_type=jn...]
    pallas_call x0 -> x2, Pallas kernels: none -> 185 us  [run(): pl.pallas_call(kernel, out_shape=[jax.ShapeDtypeStruct(out.shape, out.dty...]
    unnamed x10 -> x0, waiting for transfers between devices: 145 us -> none
    unnamed x2 -> x0, blocking collectives: 126 us -> none
    dynamic_slice x145 -> x0, local copies, waits for them, and re-layouts: 112 us -> none  [the longest x48 38.5 us: on_device(): lax.scan(total_step, (start_max, jnp.zeros_like(start_max)), block_steps)]
    all_gather x6 -> x0, waiting for transfers between devices: 50.4 us -> none  [the longest x1 50.3 us: on_device(): all_kv = lax.all_gather(key_value, 'ctx', axis=0, tiled=True)]
  transfers between devices with their start and end apart: 9 -> 0, of which waited for: 4 -> 0; matrix products, arithmetic and copies ran while one was open for 10% -> 0% of each run, Pallas kernels for 0% -> 0%
where the time goes in v2:
time: 190 us
  Pallas kernels  185 us (97%)
  local copies, waits for them, and re-layouts  3.26 us (2%)
    pallas_call x2, Pallas kernels, run(): pl.pallas_call(kernel, out_shape=[jax.ShapeDtypeStruct(out.shape, out.dty...  185 us

profile of v2, /device:TPU:0, one launch (start us, length us, event | category | flops | bytes accessed | tf_op | source)
XLA Modules:
  0.0 190.0 jit_solution(5796449131756799357)
XLA Ops:
  0.6 0.0 copy-start.2
  0.7 0.0 copy-start.1
  0.7 0.0 copy-start
  0.7 0.6 copy-done.2
  1.3 0.0 copy-done.1
  1.3 0.0 copy-done
  1.3 2.6 %concatenate.3 = bf16[128]{0:T(256)(128)(2,1)} concatenate(bf16[5]{0:T(256)(128)(2,1)S(1)} %copy-done, bf16[5]{0:T(256)(128)(2,1)S(1)} %copy-done.1, bf16[5]{0:T(256)(128)(2,1)S(1)} %copy-done.2, bf16[5]{0:T(256)(128)(2,1)} %param.33, bf16[2]{0:T(256)(128)(2,1)} %param.25, bf16[2]{0:T(256)(128)(2,1)} %param.26, bf16[104]{0:T(256)(128)(2,1)S(1)} %broadcast_in_dim.7), dimensions={0} | concatenate | bytes 512 | tf_op jit(solution)/shard_map/concatenate | solution.py:1472
  3.9 0.5 multiply_power_fusion.refs_6_
  4.5 183.5 %shard_map.289 = (bf16[128,640]{1,0:T(8,128)(2,1)}, bf16[128,640]{1,0:T(8,128)(2,1)}, f32[128,128]{1,0:T(8,128)}, f32[128,128]{1,0:T(8,128)}, f32[80,128]{1,0:T(8,128)}, /*index=5*/f32[32,128]{1,0:T(8,128)}) custom-call(s32[128]{0:T(128)} %refs_0_.1, s32[1,8]{1,0:T(1,128)} %refs_1_.1, bf16[1,128,640]{2,1,0:T(8,128)(2,1)} %refs_2_.1, ...), custom_call_target="tpu_custom_call" | custom-call | tf_op jit(solution)/shard_map/pallas_call | solution.py:168
  188.0 1.9 shard_map.290
  (1 shorter events, 0.0 us)
Async XLA Ops:
  0.6 0.7 copy-start.2
  0.7 0.7 copy-start.1
  0.7 0.7 copy-start

commit v3 on v2

--- a/solution.py
+++ b/solution.py
@@ -61,87 +61,105 @@
 
 
 class Ring:
-    def __init__(self, links, axis, source, landing):
+    def __init__(self, links, axis, source, landing, whole, steps, apart, sends):
         self.links, self.axis, self.source, self.landing = links, axis, source, landing
-        self.numbers = [links.number() for _ in range(3)]
+        self.whole, self.apart = whole, apart
+        self.sends = links.sends(whole) if sends is None else sends
+        if apart:
+            self.numbers = {step: links.receive() for step in steps}
+        else:
+            self.numbers = dict.fromkeys(steps, links.receive())
 
     def copy(self, step, sender):
         return self.links.copy(
-            self.numbers[step - 1],
+            self.sends,
+            self.numbers[step],
             self.source(step),
             self.landing(step, sender),
             peer(self.axis, step),
         )
 
     def start(self, step):
-        self.links.start(self.copy(step, place()[self.axis]))
+        self.copy(step, place()[self.axis]).start()
 
     def wait(self, step):
         self.copy(step, shifted(place()[self.axis], -step)).wait_recv()
 
     def wait_all(self):
-        for step in (1, 2, 3):
-            self.wait(step)
+        if self.apart:
+            for step in self.numbers:
+                self.wait(step)
+        else:
+            step = next(iter(self.numbers))
+            self.links.copy(
+                self.sends, self.numbers[step], self.whole, self.whole, peer(self.axis, step)
+            ).wait_recv()
 
     def sent(self):
-        for step in (1, 2, 3):
-            self.links.sent(self.numbers[step - 1])
+        self.links.settle((self.sends,))
 
 
 class Across:
-    def __init__(self, links, source, landing):
-        mine = lax.axis_index("dp")
-        self.links, self.number = links, links.number()
-        links.start(links.copy(self.number, source, landing(mine), other_core()))
-        self.came = links.copy(self.number, source, landing(1 - mine), other_core())
+    def __init__(self, links, whole):
+        self.links, self.whole = links, whole
+        self.sends, self.number = links.sends(whole), links.receive()
+
+    def add(self, source, landing):
+        there = landing(lax.axis_index("dp"))
+        self.links.copy(self.sends, self.number, source, there, other_core()).start()
 
     def wait(self):
-        self.came.wait_recv()
+        self.links.copy(
+            self.sends, self.number, self.whole, self.whole, other_core()
+        ).wait_recv()
 
     def sent(self):
-        self.links.sent(self.number)
+        self.links.settle((self.sends,))
 
 
 class Links:
     def __init__(self, send, recv):
-        self.send, self.recv, self.used, self.open = send, recv, 0, {}
-
-    def number(self):
-        self.used += 1
-        return self.used - 1
-
-    def copy(self, number, source, landing, device):
-        copy = pltpu.make_async_remote_copy(
+        self.send, self.recv = send, recv
+        self.sending, self.receiving, self.open = 0, 0, {}
+
+    def sends(self, whole):
+        self.open[self.sending] = whole
+        self.sending += 1
+        return self.sending - 1
+
+    def receive(self):
+        self.receiving += 1
+        return self.receiving - 1
+
+    def copy(self, send, recv, source, landing, device):
+        return pltpu.make_async_remote_copy(
             src_ref=source,
             dst_ref=landing,
-            send_sem=self.send.at[number],
-            recv_sem=self.recv.at[number],
+            send_sem=self.send.at[send],
+            recv_sem=self.recv.at[recv],
             device_id=device,
             device_id_type=MESH,
         )
-        self.latest = (number, copy)
-        return copy
-
-    def start(self, copy):
-        copy.start()
-        self.open[self.latest[0]] = copy
-
-    def sent(self, number):
-        self.open.pop(number).wait_send()
-
-    def ring(self, axis, source, landing, begin=True):
-        ring = Ring(self, axis, source, landing)
+
+    def ring(
+        self, axis, source, landing, whole, begin=True, steps=(1, 2, 3), apart=False, sends=None
+    ):
+        ring = Ring(self, axis, source, landing, whole, steps, apart, sends)
         if begin:
-            for step in (1, 2, 3):
+            for step in steps:
                 ring.start(step)
         return ring
 
-    def across(self, source, landing):
-        return Across(self, source, landing)
-
-    def close(self):
-        for number in tuple(self.open):
-            self.sent(number)
+    def across(self, source, landing, whole):
+        across = Across(self, whole)
+        across.add(source, landing)
+        return across
+
+    def settle(self, numbers=None):
+        for number in tuple(self.open if numbers is None else numbers):
+            if number in self.open:
+                whole = self.open.pop(number)
+                self.copy(number, 0, whole, whole, other_core()).wait_send()
 
 
 VMEM = pl.BlockSpec(memory_space=pltpu.VMEM)
@@ -152,7 +170,7 @@
     return pltpu.VMEM(shape, kind)
 
 
-def run(stage, numbers, ins, outs, scratch, number=None, copies=0):
+def run(stage, numbers, ins, outs, scratch, number=None, copies=()):
     flat, shape = jax.tree.flatten(scratch, is_leaf=lambda leaf: not isinstance(leaf, (dict, list)))
 
     def kernel(*refs):
@@ -170,7 +188,7 @@
         out_shape=[jax.ShapeDtypeStruct(out.shape, out.dtype) for out in outs.values()],
         in_specs=[SMEM] * len(numbers) + [VMEM] * len(ins),
         out_specs=[VMEM] * len(outs),
-        scratch_shapes=flat + [pltpu.SemaphoreType.DMA((copies,))] * (2 if copies else 0),
+        scratch_shapes=flat + [pltpu.SemaphoreType.DMA((count,)) for count in copies],
         compiler_params=pltpu.CompilerParams(vmem_limit_bytes=60 * MIB, **remote),
     )(*numbers.values(), *ins.values())
     return dict(zip(outs, results))
@@ -233,14 +251,19 @@
 
 
 def number_table():
-    table = np.zeros((8, 768), np.int32)
+    def turned_device(device):
+        core, x, y, z = device // 64, (device // 16) % 4, (device // 4) % 4, device % 4
+        return ((core * 4 + y) * 4 + z) * 4 + x
+
+    table = np.zeros((8, 640), np.int32)
     k = np.arange(640)
-    table[0, :640], table[1, :640] = k % 5, k // 5
+    table[0], table[1] = k % 5, turned_device(k // 5)
     core, y, z, x, row = k // 320, (k // 80) % 4, (k // 20) % 4, (k // 5) % 4, k % 5
-    table[2, :640] = (((core * 4 + x) * 4 + y) * 4 + z) * 5 + row
-    k = np.arange(768)
-    table[3] = np.where(k % 6 < 5, 5 * (k // 6) + k % 6, -1)
-    table[4, :256], table[5, :256] = np.arange(256) % 2, np.arange(256) // 2
+    table[2] = (((core * 4 + x) * 4 + y) * 4 + z) * 5 + row
+    table[3, :512] = 5 * (k[:512] // 4) + k[:512] % 4
+    device = np.arange(128)
+    table[3, 512 + turned_device(device)] = 5 * device + 4
+    table[4, :256], table[5, :256] = k[:256] % 2, turned_device(k[:256] // 2)
     return table
 
 
@@ -290,7 +313,10 @@
         weight = (r.key_weight, r.value_weight)[tile // 2]
         half = 128 * (tile % 2)
         r.stage[pl.ds(336 + tile, 5, stride=4)] = weight[:, half : half + 128].astype(F32)
-    r.stage[356:357] = r.gain_row[...].astype(F32)
+    r.stage[356:357] = jnp.zeros((1, 128), F32)
+    own = (r.attn_norm, r.attn_post_norm, r.ffn_norm, r.ffn_post_norm, r.query_gain, r.key_gain)
+    for ref, (_, _, held, lane) in zip(own, GAINS):
+        r.stage[356:357, lane : lane + held] = ref[...].astype(F32)
     spot = place()
     for part, ref in enumerate(r.p):
         first, second, _ = ORDERS[part]
@@ -310,8 +336,8 @@
     angles = position * r.frequency[...]
     r.cos[...] = jnp.cos(angles)
     r.sin[...] = jnp.sin(angles)
-    r.turning[...] = one_hot(640, r.table[2:3, :640])
-    r.sixes[...] = one_hot(640, r.table[3:4, :])
+    r.turning[...] = one_hot(640, r.table[2:3])
+    r.splitting[...] = one_hot(640, r.table[3:4])
 
 
 NEVER = -(1 << 20)
@@ -356,7 +382,10 @@
     def small(axis, unit, index_of):
         ref = r.u[unit]
         ring = links.ring(
-            axis, lambda step: ref.at[index_of(spot[axis])], lambda step, at: ref.at[index_of(at)]
+            axis,
+            lambda step: ref.at[index_of(spot[axis])],
+            lambda step, at: ref.at[index_of(at)],
+            ref.at[index_of(pl.ds(0, 3))],
         )
         held.append(ring)
         return ring
@@ -374,6 +403,7 @@
                 first,
                 lambda step, ref=ref, row=row, first=first: ref.at[row, spot[first]],
                 lambda step, at, ref=ref, row=row: ref.at[row, at],
+                ref.at[row, pl.ds(0, 3)],
             )
         )
     tables(r)
@@ -389,6 +419,7 @@
                 second,
                 lambda step, ref=ref, second=second: ref.at[spot[second]],
                 lambda step, at, ref=ref: ref.at[at],
+                ref.at[pl.ds(0, 3)],
             )
         )
     key_tables(r)
@@ -401,34 +432,31 @@
         rings[3 + part].wait_all()
         for number in weights:
             unpack(r, number)
-            if number not in (GATE, UP):
-                spreads[number] = Spread(r, number)
+        for piece in EARLY_PIECES[part]:
+            spreads[piece] = Spread(r, piece)
     one.wait_all()
-    three = links.across(r.u[0].at[core], lambda at: r.u[0].at[at])
+    three = links.across(r.u[0].at[core], lambda at: r.u[0].at[at], r.u[0].at[core])
     two.wait_all()
-    four = links.across(r.u[1].at[core], lambda at: r.u[1].at[at])
+    four = links.across(r.u[1].at[core], lambda at: r.u[1].at[at], r.u[1].at[core])
     three.wait()
     four.wait()
     return rings, held + [three, four], spreads
 
 
-def device_loop(body):
-    def one(number):
-        core, x, y, z = number // 64, (number // 16) % 4, (number // 4) % 4, number % 4
-        body(pl.multiple_of(number * 24, 8), (core, x, y, z), (core, y, z, x))
-
-    loop(128, one)
+SMALL = 2048
 
 
 def unpack_small(r):
-    def one(row, i0, i1):
-        r.stage[pl.ds(row, 16)] = r.u[0][i0].astype(F32)
-        r.stage[pl.ds(row + 16, 8)] = r.u[1][i1].astype(F32)[:8]
-
-    device_loop(one)
+    for unit in range(2):
+        for core in range(2):
+            for plane in range(4):
+                row = SMALL * unit + 1024 * core + 256 * plane
+                r.stage[row : row + 256] = r.u[unit][core, plane].astype(F32).reshape(256, 128)
     for tile in range(4):
-        r.w_kv[:, 128 * tile : 128 * tile + 128] = columns_of(r, 0, 768, 4, tile).astype(BF16)
-    held = r.stage[pl.ds(20, 128, stride=24)].astype(BF16)
+        lanes = slice(128 * tile, 128 * tile + 128)
+        r.w_kv[:512, lanes] = columns_of(r, 0, 512, 4, tile).astype(BF16)
+        r.w_kv[512:, lanes] = columns_of(r, SMALL, 128, 16, tile).astype(BF16)
+    held = columns_of(r, SMALL, 128, 16, 4).astype(BF16)
     for number, (at, columns, _, _) in enumerate(GAINS):
         lanes, owners = gain_maps(r, number)
         spread = jnp.where(owners, dot32(held, lanes), 0.0)
@@ -515,8 +543,8 @@
     x = r.x[...]
     normed = rms_scale(x, gain(r, G_ATTN)).astype(BF16)
     r.normed[...] = normed
-    r.normed_six[...] = dot32(normed, r.sixes[...]).astype(BF16)
-    raw = dot32(r.normed_six[...], r.w_kv[...])
+    r.normed_split[...] = dot32(normed, r.splitting[...]).astype(BF16)
+    raw = dot32(r.normed_split[...], r.w_kv[...])
     r.key_raw[...] = raw[:, :HEAD]
     keys = rope(r, rms_scale(raw[:, :HEAD], gain(r, G_KEY)))
     both = jnp.concatenate([keys, raw[:, HEAD:]], axis=1).astype(BF16)
@@ -526,8 +554,6 @@
             r.kv3[block, 16 * unit : 16 * unit + 16] = both[
                 row : row + 16, 128 * lane : 128 * lane + 128
             ]
-    own = r.kv3[0]
-    r.kv3[2] = jnp.where(my_low(r) == 63, own, jnp.zeros_like(own))
 
 
 def of_plane(ref, axis, at, *rest):
@@ -545,45 +571,124 @@
 def plane_loop(part, body):
     first, second, last = ORDERS[part]
 
-    def one(number):
-        spot = [None] * 3
-        spot[first], spot[second], spot[last] = number % 4, number // 4, place()[last]
-        body(spot, number // 4, number % 4)
-
-    loop(16, one)
+    def row(i2):
+        for i1 in range(4):
+            spot = [None] * 3
+            spot[first], spot[second], spot[last] = i1, i2, place()[last]
+            body(spot, i2, i1)
+
+    loop(4, row)
+
+
+PIECES = (
+    (GATE, 0, 1024),
+    (GATE, 1024, 1024),
+    (OUTPUT, 0, 640),
+    (UP, 0, 1024),
+    (UP, 1024, 1024),
+    (QUERY, 0, 1024),
+    (DOWN, 0, 2),
+    (DOWN, 2, 2),
+)
+GATE_ONE, GATE_TWO, OUT, UP_ONE, UP_TWO, ASK, DOWN_ONE, DOWN_TWO = range(8)
+EARLY_PIECES = ((OUT, GATE_ONE), (ASK, UP_ONE), (DOWN_ONE,))
+LATE_PIECES = (GATE_TWO, UP_TWO, DOWN_TWO)
+
+
+def window(ref, dim, first, count):
+    index = [slice(None)] * len(ref.shape)
+    index[dim] = pl.ds(first, count)
+    return ref.at[tuple(index)]
+
+
+def piece_of(piece, ref, chips=4):
+    number, first, count = PIECES[piece]
+    rank = len(ref.shape)
+    return window(ref, rank - 1 - chips if number == DOWN else rank - 1, first, count)
+
+
+def half_of(piece, plane, half):
+    number, _, count = PIECES[piece]
+    if number == DOWN:
+        return window(plane, len(plane.shape) - 4, half, 1)
+    if number == OUTPUT:
+        return window(plane, len(plane.shape) - 2, 64 * half, 64)
+    return window(plane, len(plane.shape) - 1, count // 2 * half, count // 2)
+
+
+def piece_plane(r, piece, core, at):
+    number = PIECES[piece][0]
+    return piece_of(piece, weight_plane(r.w[number], number, core, at), 3)
+
+
+def piece_axis(piece):
+    return ORDERS[WEIGHTS[PIECES[piece][0]][0]][2]
 
 
 class Spread:
-    def __init__(self, r, number):
-        self.links, self.axis = r.links, ORDERS[WEIGHTS[number][0]][2]
-        self.at = lambda core, at: weight_plane(r.w[number], number, core, at)
-        self.core, self.mine = lax.axis_index("dp"), place()[self.axis]
-        self.ring = r.links.ring(
-            self.axis,
-            lambda step: self.at(self.core, self.mine),
-            lambda step, at: self.at(self.core, at),
-        )
-        self.overs = []
+    def __init__(self, r, piece):
+        self.links, axis = r.links, piece_axis(piece)
+        self.core, self.mine = lax.axis_index("dp"), place()[axis]
+        self.at = lambda core, at: piece_plane(r, piece, core, at)
+
+        def half(at, which):
+            return half_of(piece, self.at(self.core, at), which)
+
+        both = piece_of(piece, r.w[PIECES[piece][0]])
+        dim = 3 if PIECES[piece][0] == DOWN else 1
+        planes = window(both, dim, 0, 3).at[self.core]
+        sends = r.links.sends(planes)
+        self.near = [
+            r.links.ring(
+                axis,
+                lambda step, which=which: half(self.mine, which),
+                lambda step, at, which=which: half(at, which),
+                None,
+                steps=(1, 3),
+                apart=True,
+                sends=sends,
+            )
+            for which in range(2)
+        ]
+
+        def passed(step, at):
+            return half(shifted(at, -step), 0 if step == 1 else 1)
+
+        self.far = r.links.ring(
+            axis,
+            lambda step: passed(step, self.mine),
+            passed,
+            None,
+            begin=False,
+            steps=(1, 3),
+            apart=True,
+            sends=sends,
+        )
+        self.across = Across(r.links, both.at[self.core])
         self.over(self.mine)
 
     def over(self, at):
-        self.overs.append(
-            self.links.across(self.at(self.core, at), lambda core: self.at(core, at))
-        )
+        self.across.add(self.at(self.core, at), lambda core: self.at(core, at))
+
+    def forward(self):
+        for which, step in enumerate((1, 3)):
+            self.near[which].wait(step)
+            self.far.start(step)
 
     def pass_on(self):
-        for step in (1, 3, 2):
-            self.ring.wait(step)
-            self.over(shifted(self.mine, -step))
+        for which, step in enumerate((3, 1)):
+            self.near[which].wait(step)
+        self.over(shifted(self.mine, 1))
+        self.over(shifted(self.mine, 3))
+        self.far.wait_all()
+        self.over(shifted(self.mine, 2))
 
     def finish(self):
-        for over in self.overs:
-            over.wait()
+        self.across.wait()
 
     def free(self):
-        self.ring.sent()
-        for over in self.overs:
-            over.sent()
+        self.far.sent()
+        self.across.sent()
 
 
 def gather_first(r):
@@ -595,6 +700,7 @@
                 ORDERS[part][0],
                 lambda step, own=own: own,
                 lambda step, at, ref=r.f1[part]: ref.at[at],
+                r.f1[part].at[pl.ds(0, 3)],
             )
         )
     return rings
@@ -611,12 +717,12 @@
         for at in range(4):
             g2[mine, 2 * at] = f1[at, 0]
             g2[mine, 2 * at + 1] = f1[at, 1]
-        g2[mine, 8] = add_all([f1[at, 2] for at in range(4)]).astype(BF16)
         rings.append(
             r.links.ring(
                 second,
                 lambda step, g2=g2, mine=mine: g2.at[mine],
                 lambda step, at, g2=g2: g2.at[at],
+                g2.at[pl.ds(0, 3)],
             )
         )
     return rings
@@ -631,8 +737,9 @@
         g2, sel, sp, rsp = r.g2[part], r.sel[part], r.sp[part], r.rsp[part]
         seconds[part].wait_all()
         targets = [low_of(r, chip_of(spot, last, step)) for step in (1, 2, 3)]
-
-        def choose(at, i2, i1, g2=g2, sel=sel, row=row, rows=rows, last=last, targets=targets):
+        sp[...] = jnp.zeros_like(sp)
+
+        def choose(at, i2, i1, g2=g2, sel=sel, sp=sp, row=row, rows=rows, last=last, targets=targets):
             low = g2[i2, 2 * i1]
             high = g2[i2, 2 * i1 + 1]
             source = low_of(r, chip_of(at, last, 0))
@@ -642,9 +749,9 @@
                 sel[step - 1, plane[0], plane[1]] = jnp.where(
                     source < targets[step - 1], low, high
                 )
+            sp[...] = jnp.where(source == 63, low, sp[...])
 
         plane_loop(part, choose)
-        sp[...] = add_all([g2[at, 8] for at in range(4)]).astype(BF16)
         rings.append(
             r.links.ring(
                 last,
@@ -652,14 +759,19 @@
                 lambda step, at, row=row, rows=rows, last=last: of_plane(
                     r.slots, last, at, pl.ds(row, rows)
                 ),
+                sel,
+                apart=True,
             )
         )
         specials.append(
             r.links.ring(
-                last, lambda step, sp=sp: sp, lambda step, at, rsp=rsp: rsp.at[at]
+                last,
+                lambda step, sp=sp: sp,
+                lambda step, at, rsp=rsp: rsp.at[at],
+                rsp.at[pl.ds(0, 3)],
             )
         )
-    r.extra[0:2] = r.kv3[0:2]
+    r.extra[0:2] = r.kv3[...]
     return rings, specials
 
 
@@ -864,7 +976,7 @@
 
 
 def feed_forward(r, spreads):
-    spreads[OUTPUT].finish()
+    spreads[OUT].finish()
     for block in range(2):
         for head in range(HEADS):
             r.attn_low[64 * block : 64 * block + 64, HEAD * head : HEAD * head + HEAD] = r.attn[
@@ -874,8 +986,8 @@
     r.mid[...] = r.x[...] + rms_scale(r.proj[...], gain(r, G_POST_ATTN))
     r.ffn_in[...] = rms_scale(r.mid[...], gain(r, G_FFN)).astype(BF16)
     r.ffn_in_b[...] = turned(r, r.ffn_in[...])
-    spreads[GATE].finish()
-    spreads[UP].finish()
+    for piece in (GATE_ONE, GATE_TWO, UP_ONE, UP_TWO):
+        spreads[piece].finish()
     for number in range(4):
         at = slice(512 * number, 512 * number + 512)
         gate = dot32(r.ffn_in[...], columns(r.w[GATE], 512 * number, 512))
@@ -883,7 +995,8 @@
         r.gate[:, at] = gate
         r.up[:, at] = up
         r.hidden[:, at] = (gelu_parts(gate)[0] * up).astype(BF16)
-    spreads[DOWN].finish()
+    spreads[DOWN_ONE].finish()
+    spreads[DOWN_TWO].finish()
     r.ffn_out[...] = dot32(r.hidden[...], r.w[DOWN][...].reshape(2048, 640))
     out = r.mid[...] + rms_scale(r.ffn_out[...], gain(r, G_POST_FFN))
     r.block_out[...] = low_first(r, out.astype(BF16))
@@ -895,13 +1008,14 @@
 
 
 def feed_forward_back(r, spreads):
-    for number in (GATE, OUTPUT, UP, DOWN):
-        spreads[number].free()
+    for piece in (GATE_ONE, GATE_TWO, OUT, UP_ONE, UP_TWO, DOWN_ONE, DOWN_TWO):
+        spreads[piece].free()
     grad_out = low_first(r, r.out_cot[0].astype(F32))
     grad_ffn_out, term = norm_back(r.ffn_out[...], gain(r, G_POST_FFN), grad_out)
     note_gain(r, G_POST_FFN, term)
     low_grad = grad_ffn_out.astype(BF16)
     r.low_grad[...] = low_grad
+    halves = {}
     grad_in = jnp.zeros((128, 640), F32)
     grad_in_b = jnp.zeros((128, 640), F32)
     for number in range(4):
@@ -924,7 +1038,11 @@
         r.w[GATE][:, :, :, at] = term.reshape(2, 4, 80, 512)
         term = dot_tn(r.ffn_in_b[...], grad_up).astype(BF16)
         r.w[UP][:, :, :, at] = term.reshape(2, 4, 80, 512)
-    halves = {number: send_half(r, number) for number in (DOWN, GATE, UP)}
+        if number == 1:
+            halves[GATE_ONE] = send_half(r, GATE_ONE)
+            halves[UP_ONE] = send_half(r, UP_ONE)
+    for piece in (DOWN_ONE, DOWN_TWO, GATE_TWO, UP_TWO):
+        halves[piece] = send_half(r, piece)
     grad_in = grad_in + unturned(r, grad_in_b)
     back, term = norm_back(r.mid[...], gain(r, G_FFN), grad_in)
     note_gain(r, G_FFN, term)
@@ -936,7 +1054,7 @@
     grad_attn = dot_nt(proj_low, r.w[OUTPUT][...].reshape(1024, 640)).astype(BF16)
     term = dot_tn(r.attn_low[...], proj_low).astype(BF16)
     r.w[OUTPUT][...] = term.reshape(2, 4, 128, 640)
-    halves[OUTPUT] = send_half(r, OUTPUT)
+    halves[OUT] = send_half(r, OUT)
     for block in range(2):
         for head in range(HEADS):
             r.grad_attn[head_rows(block, head)] = grad_attn[
@@ -959,52 +1077,87 @@
         r.query_low[:, at] = back.astype(BF16)
     note_gain(r, G_QUERY, total)
     r.grad_normed[...] = unturned(r, dot_nt(r.query_low[...], r.w[QUERY][...].reshape(640, 1024)))
-    spreads[QUERY].free()
+    spreads[ASK].free()
     term = dot_tn(r.normed_b[...], r.query_low[...]).astype(BF16)
     r.w[QUERY][...] = term.reshape(2, 4, 80, 1024)
-    return send_half(r, QUERY)
-
-
-def send_half(r, number):
-    grad, half = r.w[number], r.half[number]
-    return r.links.across(grad.at[1 - lax.axis_index("dp")], lambda at: half)
-
-
-def sum_halves(r, number, over):
-    part, _, _, by_chip = WEIGHTS[number]
-    last = ORDERS[part][2]
-    core, mine = lax.axis_index("dp"), place()[last]
-    grad, half, land = r.w[number], r.half[number], r.landed[number]
-    over.wait()
-
-    def join(*at):
-        index = (core, *at)
-        grad[index] = (grad[index].astype(F32) + half[at].astype(F32)).astype(BF16)
-
-    if by_chip:
-        loop(16, lambda at: join(at // 4, at % 4))
+    return send_half(r, ASK)
+
+
+def send_half(r, piece):
+    number = PIECES[piece][0]
+    grad, half = piece_of(piece, r.w[number]), piece_of(piece, r.half[number])
+    return r.links.across(grad.at[1 - lax.axis_index("dp")], lambda at: half, half)
+
+
+def add_rows(count, to, value):
+    def one(at):
+        rows = pl.ds(pl.multiple_of(at * 16, 16), 16)
+        to[rows] = (to[rows].astype(F32) + value[rows].astype(F32)).astype(BF16)
+
+    loop(count // 16, one)
+
+
+def add_into(to, value):
+    lead = to.shape[:-2]
+    if not lead:
+        add_rows(to.shape[0], to, value)
+    elif len(lead) == 1:
+        for at in range(lead[0]):
+            add_rows(to.shape[1], to.at[at], value.at[at])
     else:
-        rows = half.shape[1] // 16
-        loop(
-            4 * rows,
-            lambda at: join(at // rows, pl.ds(pl.multiple_of((at % rows) * 16, 16), 16)),
-        )
-    return r.links.ring(
-        last,
-        lambda step: weight_plane(grad, number, core, shifted(mine, step)),
-        lambda step, at: land.at[step - 1],
-    )
-
-
-def repack(r, number, ring):
+        for at in range(lead[0]):
+            add_into(to.at[at], value.at[at])
+
+
+class Gather:
+    def __init__(self, r, piece, over):
+        self.piece, axis = piece, piece_axis(piece)
+        core, mine = lax.axis_index("dp"), place()[axis]
+        number = PIECES[piece][0]
+        over.wait()
+        add_into(piece_of(piece, r.w[number]).at[core], piece_of(piece, r.half[number]))
+        self.land = piece_of(piece, r.landed[number], 3)
+        self.at = lambda step: piece_plane(r, piece, core, shifted(mine, step))
+        sends = r.links.sends(self.land)
+        self.far = r.links.ring(
+            axis,
+            lambda step: half_of(piece, self.at(2), 0 if step == 1 else 1),
+            lambda step, at: half_of(piece, self.land.at[2], 0 if step == 1 else 1),
+            None,
+            steps=(1, 3),
+            apart=True,
+            sends=sends,
+        )
+        self.near = r.links.ring(
+            axis,
+            self.at,
+            lambda step, at: self.land.at[0 if step == 1 else 1],
+            self.land.at[pl.ds(0, 2)],
+            begin=False,
+            steps=(1, 3),
+            sends=sends,
+        )
+
+    def relay(self):
+        for which, step in enumerate((1, 3)):
+            self.far.wait(step)
+            add_into(
+                half_of(self.piece, self.at(step), which),
+                half_of(self.piece, self.land.at[2], which),
+            )
+            self.near.start(step)
+
+
+def repack(r, number, *gathers):
     part, first, rows, by_chip = WEIGHTS[number]
     count, tiles = plane_tiles(number)
     own, land = own_plane(r, number), r.landed[number]
-    ring.wait_all()
+    for gather in gathers:
+        gather.near.wait_all()
     for tile in range(tiles):
         lanes = slice(128 * tile, 128 * tile + 128)
         index = (slice(None),) * (3 if by_chip else 1) + (lanes,)
-        total = add_all([own[index]] + [land[(step, *index)] for step in range(3)])
+        total = add_all([own[index]] + [land[(step, *index)] for step in range(2)])
         r.stage[pl.ds(tile, count, stride=tiles)] = total.reshape(count, 128)
 
     def one(chip):
@@ -1022,6 +1175,7 @@
         second,
         lambda step: r.p[part].at[shifted(mine, step)],
         lambda step, at: r.second[part].at[step - 1],
+        r.second[part],
     )
 
 
@@ -1037,6 +1191,7 @@
         first,
         lambda step: r.line[part].at[shifted(mine, step)],
         lambda step, at: r.first[part].at[step - 1],
+        r.first[part],
     )
 
 
@@ -1058,6 +1213,7 @@
                     r.slots, last, shifted(spot[last], step), pl.ds(row, rows)
                 ),
                 lambda step, at, rb=r.rb[part]: rb.at[step - 1],
+                r.rb[part],
                 begin=False,
             )
         )
@@ -1066,6 +1222,7 @@
                 last,
                 lambda step, row=row, rows=rows: r.grad_extra.at[2, pl.ds(row, rows)],
                 lambda step, at, rs=r.rs[part]: rs.at[step - 1],
+                r.rs[part],
                 begin=False,
             )
         )
@@ -1083,24 +1240,26 @@
         thirds[part].wait_all()
         specials[part].wait_all()
         special = add_all([r.grad_extra[2, row : row + rows]] + [rs[step] for step in range(3)])
-        for at in range(4):
-            total[at, 8] = special.astype(BF16)
+        r.sp[part][...] = special.astype(BF16)
         senders = [low_of(r, chip_of(spot, last, -step)) for step in (1, 2, 3)]
 
-        def collect(at, i2, i1, rb=rb, total=total, row=row, rows=rows, last=last, senders=senders):
+        def collect(
+            at, i2, i1, rb=rb, sp=r.sp[part], total=total, row=row, rows=rows, last=last, senders=senders
+        ):
             chip = chip_of(at, last, 0)
             source = low_of(r, chip)
             plane = [at[axis] for axis in (X, Y, Z) if axis != last]
-            own = r.slots[at[0], at[1], at[2], pl.ds(row, rows)].astype(F32)
-            none = jnp.zeros_like(own)
-            low = jnp.where(source < low_me, own, none)
-            high = jnp.where(source < low_me, none, own)
-            low += jnp.where(chip == me, r.grad_extra[0, pl.ds(row, rows)].astype(F32), none)
-            high += jnp.where(chip == me, r.grad_extra[1, pl.ds(row, rows)].astype(F32), none)
+            both = r.slots[at[0], at[1], at[2], pl.ds(row, rows)].astype(F32)
+            none = jnp.zeros_like(both)
+            low = jnp.where(source < low_me, both, none)
             for step in (1, 2, 3):
                 came = rb[step - 1, plane[0], plane[1]].astype(F32)
                 low += jnp.where(source < senders[step - 1], came, none)
-                high += jnp.where(source < senders[step - 1], none, came)
+                both += came
+            high = both - low
+            low += jnp.where(chip == me, r.grad_extra[0, pl.ds(row, rows)].astype(F32), none)
+            high += jnp.where(chip == me, r.grad_extra[1, pl.ds(row, rows)].astype(F32), none)
+            low += jnp.where(source == 63, sp[...].astype(F32), none)
             total[i2, 2 * i1] = low.astype(BF16)
             total[i2, 2 * i1 + 1] = high.astype(BF16)
 
@@ -1110,6 +1269,7 @@
                 second,
                 lambda step, total=total, second=second: total.at[shifted(spot[second], step)],
                 lambda step, at, land=land: land.at[step - 1],
+                land,
             )
         )
     return rings
@@ -1128,16 +1288,15 @@
                 BF16
             )
 
-        special = pick(8)
         for at in range(4):
             line[at, 0] = pick(2 * at)
             line[at, 1] = pick(2 * at + 1)
-            line[at, 2] = special
         rings.append(
             r.links.ring(
                 first,
                 lambda step, line=line, first=first: line.at[shifted(spot[first], step)],
                 lambda step, at, end=end: end.at[step - 1],
+                end,
             )
         )
     return rings
@@ -1148,15 +1307,13 @@
     for part, (row, rows) in enumerate(KV_ROWS):
         firsts[part].wait_all()
         mine = spot[ORDERS[part][0]]
-        for index in range(3):
+        for index in range(2):
             r.kv_sum[index, row : row + rows] = add_all(
                 [r.f1[part][mine, index]] + [r.r1[part][step, index] for step in range(3)]
             )
 
 
 def keys_values_back(r):
-    special = jnp.where(my_low(r) == 63, 1.0, 0.0)
-    r.kv_sum[0] = r.kv_sum[0] + r.kv_sum[2] * special
     lanes = []
     for lane in range(4):
         pieces = [
@@ -1168,11 +1325,14 @@
     back, term = norm_back(r.key_raw[...], gain(r, G_KEY), rope_back(r, grad_keys))
     note_gain(r, G_KEY, term)
     kv_low = jnp.concatenate([back, grad_values], axis=1).astype(BF16)
-    terms = dot_tn(r.normed_six[...], kv_low)
+    terms = dot_tn(r.normed_split[...], kv_low)
+    r.stage[SMALL : 2 * SMALL] = jnp.zeros((SMALL, 128), F32)
     for tile in range(4):
-        r.stage[pl.ds(tile, 768, stride=4)] = terms[:, 128 * tile : 128 * tile + 128]
-    grad_six = dot_nt(kv_low, r.w_kv[...]).astype(BF16)
-    grad_normed = dot_nt(grad_six, r.sixes[...]) + r.grad_normed[...]
+        lanes = slice(128 * tile, 128 * tile + 128)
+        r.stage[pl.ds(tile, 512, stride=4)] = terms[:512, lanes]
+        r.stage[pl.ds(SMALL + tile, 128, stride=16)] = terms[512:, lanes]
+    grad_split = dot_nt(kv_low, r.w_kv[...]).astype(BF16)
+    grad_normed = dot_nt(grad_split, r.splitting[...]) + r.grad_normed[...]
     back, term = norm_back(r.x[...], gain(r, G_ATTN), grad_normed)
     note_gain(r, G_ATTN, term)
     r.tokens_grad[...] = low_first(r, (r.grad_mid[...] + back).astype(BF16))
@@ -1181,21 +1341,19 @@
         lanes, owners = gain_maps(r, number)
         term = jnp.where(owners, r.gain_sums[0:1, at : at + count], 0.0).astype(BF16)
         held += dot_nt(term, lanes)
-    r.stage[pl.ds(20, 128, stride=24)] = held
-    r.stage[3072:3088] = jnp.zeros((16, 128), F32)
-
-    def one(row, i0, i1):
-        r.u[0][i0] = r.stage[pl.ds(row, 16)].astype(BF16)
-        r.u[1][i1] = r.stage[pl.ds(row + 16, 16)].astype(BF16)
-
-    device_loop(one)
+    r.stage[pl.ds(SMALL + 4, 128, stride=16)] = held
+    for unit in range(2):
+        for core in range(2):
+            for plane in range(4):
+                row = SMALL * unit + 1024 * core + 256 * plane
+                r.u[unit][core, plane] = r.stage[row : row + 256].astype(BF16).reshape(4, 4, 16, 128)
 
 
 def small_sums(r, between):
     links = r.links
     core = lax.axis_index("dp")
     spot = place()
-    overs = [links.across(ref.at[1 - core], lambda at, to=to: to) for ref, to in zip(r.u, r.vh)]
+    overs = [links.across(ref.at[1 - core], lambda at, to=to: to, to) for ref, to in zip(r.u, r.vh)]
     axes = ((X, Y, Z), (Y, Z, X))
     rings = []
     for unit, order in enumerate(axes):
@@ -1214,6 +1372,7 @@
                 axis,
                 lambda step, own=own, axis=axis: own.at[core, shifted(spot[axis], step)],
                 lambda step, at, land=land: land.at[step - 1],
+                land,
             )
         )
     between[0]()
@@ -1235,6 +1394,7 @@
                 axis,
                 lambda step, out=out, axis=axis: out.at[shifted(spot[axis], step)],
                 lambda step, at, to=to: to.at[step - 1],
+                to,
             )
         )
     between[1]()
@@ -1249,6 +1409,7 @@
                 axis,
                 lambda step, out=out, axis=axis: out.at[shifted(spot[axis], step)],
                 lambda step, at, to=to: to.at[step - 1],
+                to,
             )
         )
     between[2]()
@@ -1268,64 +1429,86 @@
     keys_values(r)
     firsts = gather_first(r)
     seconds = gather_second(r, firsts)
-    for number in (GATE, UP):
-        spreads[number] = Spread(r, number)
-    for number in (QUERY, OUTPUT, DOWN):
-        spreads[number].pass_on()
+    early_pieces = (ASK, OUT, GATE_ONE, UP_ONE, DOWN_ONE)
+    for piece in early_pieces:
+        spreads[piece].forward()
+    before = tuple(r.links.open)
+    for piece in LATE_PIECES:
+        spreads[piece] = Spread(r, piece)
     thirds, specials = gather_third(r, seconds)
-    spreads[QUERY].finish()
+    for piece in early_pieces:
+        spreads[piece].pass_on()
+    for piece in LATE_PIECES:
+        spreads[piece].forward()
+    spreads[ASK].finish()
     queries(r)
 
     def pass_on(number):
         if number == 0:
-            spreads[GATE].pass_on()
-            spreads[UP].pass_on()
+            r.links.settle(before)
+        if number == 2:
+            for piece in LATE_PIECES:
+                spreads[piece].pass_on()
 
     attention(r, thirds, specials, pass_on)
     feed_forward(r, spreads)
+    before = tuple(r.links.open)
     halves = feed_forward_back(r, spreads)
-    rings = {}
+    sums = {}
+
+    def start_sums(*pieces):
+        for piece in pieces:
+            sums[piece] = Gather(r, piece, halves[piece])
+
+    def relay(*pieces):
+        for piece in pieces:
+            sums[piece].relay()
 
     def between(number):
-        if number == 0:
-            for weight in (DOWN, GATE):
-                rings[weight] = sum_halves(r, weight, halves[weight])
-        if number == 1:
-            for weight in (UP, OUTPUT):
-                rings[weight] = sum_halves(r, weight, halves[weight])
+        pass
 
     thirds, third_specials = attention_back(r, between)
-    half = queries_back(r, spreads)
+    halves[ASK] = queries_back(r, spreads)
     for ring in early_rings:
         ring.sent()
-    repack(r, DOWN, rings[DOWN])
-    late = {2: late_second(r, 2)}
     for ring in seconds:
         ring.sent()
+    r.links.settle(before)
+    before = tuple(r.links.open)
+    start_sums(GATE_ONE, UP_ONE, DOWN_ONE, GATE_TWO, UP_TWO, DOWN_TWO, OUT, ASK)
     seconds = scatter_second(r, thirds, third_specials)
-    rings[QUERY] = sum_halves(r, QUERY, half)
-    repack(r, GATE, rings[GATE])
-    repack(r, OUTPUT, rings[OUTPUT])
-    late[0] = late_second(r, 0)
+    relay(GATE_ONE, UP_ONE, DOWN_ONE, OUT)
     firsts = scatter_first(r, seconds)
-    repack(r, UP, rings[UP])
-    repack(r, QUERY, rings[QUERY])
-    late[1] = late_second(r, 1)
+    relay(GATE_TWO, UP_TWO, DOWN_TWO, ASK)
     scatter_end(r, firsts)
     for copy in early_held:
         copy.sent()
     keys_values_back(r)
-
-    def begin_last():
+    late = {}
+
+    def begin_late():
+        r.links.settle(before)
+        repack(r, DOWN, sums[DOWN_ONE], sums[DOWN_TWO])
+        late[2] = late_second(r, 2)
+        repack(r, GATE, sums[GATE_ONE], sums[GATE_TWO])
+        repack(r, OUTPUT, sums[OUT])
+        late[0] = late_second(r, 0)
+        repack(r, UP, sums[UP_ONE], sums[UP_TWO])
+        repack(r, QUERY, sums[ASK])
+        late[1] = late_second(r, 1)
+
+    def go_on_late():
+        r.links.settle(tuple(r.links.open)[:-10])
         for part in (2, 0, 1):
             late[part] = late_first(r, part, late[part])
 
-    def finish_last():
+    def finish_late():
         for part, out in enumerate((r.fa, r.fb, r.fc)):
             late_end(r, part, late[part], out)
 
-    small_sums(r, (begin_last, finish_last, lambda: None))
-    r.links.close()
+    small_sums(r, (begin_late, go_on_late, finish_late))
+    r.links.settle()
+    assert (r.links.sending, r.links.receiving) <= COPIES and r.links.receiving <= COPIES[1]
 
 
 def end(r):
@@ -1354,6 +1537,9 @@
     r.final_grad[0] = r.tokens_grad[...]
 
 
+COPIES = (96, 160)
+
+
 def by_part(*dims):
     return [hold(BF16, *dims, rows, 128) for _, rows in KV_ROWS]
 
@@ -1378,14 +1564,14 @@
 
 def buffers():
     return dict(
-        stage=hold(F32, 3088, 128),
+        stage=hold(F32, 4096, 128),
         x=hold(F32, 128, 640),
         cos=hold(F32, 128, 128),
         sin=hold(F32, 128, 128),
         gains=hold(F32, 8, 3072),
         gain_sums=hold(F32, 8, 3072),
         turning=hold(BF16, 640, 640),
-        sixes=hold(BF16, 640, 768),
+        splitting=hold(BF16, 640, 640),
         key_base=hold(jnp.int32, 32, 16, 128),
         key_rows=hold(jnp.int32, 32, 256),
         p=by_flat(4, 4),
@@ -1399,7 +1585,7 @@
         land2=by_unit(3, 4),
         sum1=by_unit(4),
         land1=by_unit(3),
-        w_kv=hold(BF16, 768, 512),
+        w_kv=hold(BF16, 640, 512),
         w=by_weight((4,), (2,)),
         half=by_weight((4,), ()),
         landed=[
@@ -1409,22 +1595,22 @@
             hold(BF16, 3, 80, 1024),
             hold(BF16, 3, 4, 4, 16, 640),
         ],
-        kv3=hold(BF16, 3, 256, 128),
-        f1=by_part(4, 3),
-        g2=by_part(4, 9),
+        kv3=hold(BF16, 2, 256, 128),
+        f1=by_part(4, 2),
+        g2=by_part(4, 8),
         sel=by_part(3, 4, 4),
         sp=by_part(),
         rsp=by_part(4),
         rb=by_part(3, 4, 4),
         rs=by_part(3),
-        r2=by_part(3, 9),
-        r1=by_part(3, 3),
+        r2=by_part(3, 8),
+        r1=by_part(3, 2),
         slots=hold(BF16, 4, 4, 4, 256, 128),
         extra=hold(BF16, 3, 256, 128),
         grad_extra=hold(BF16, 3, 256, 128),
-        kv_sum=hold(F32, 3, 256, 128),
+        kv_sum=hold(F32, 2, 256, 128),
         normed=hold(BF16, 128, 640),
-        normed_six=hold(BF16, 128, 768),
+        normed_split=hold(BF16, 128, 640),
         normed_b=hold(BF16, 128, 640),
         key_raw=hold(F32, 128, 256),
         query_raw=hold(F32, 128, 1024),
@@ -1469,20 +1655,20 @@
     ffn_post_norm,
     out_cot,
 ):
-    gain_row = jnp.concatenate(
-        [attn_norm, attn_post_norm, ffn_norm, ffn_post_norm, query_gain, key_gain]
-        + [jnp.zeros((104,), BF16)]
-    )[None]
-    frequency = (ROPE_BASE ** (-2.0 * jnp.arange(128, dtype=F32) / 256))[None]
     made = run(
         layer,
         dict(block_order=block_order, doc_lengths=doc_lengths),
         dict(
             tokens=tokens,
             out_cot=out_cot,
-            gain_row=gain_row,
+            attn_norm=attn_norm[None],
+            attn_post_norm=attn_post_norm[None],
+            ffn_norm=ffn_norm[None],
+            ffn_post_norm=ffn_post_norm[None],
+            query_gain=query_gain[None],
+            key_gain=key_gain[None],
             table=jnp.asarray(number_table()),
-            frequency=frequency,
+            frequency=jnp.asarray(ROPE_BASE ** (-2.0 * np.arange(128) / 256), F32)[None],
             gate_weight=gate_weight,
             output_weight=output_weight,
             up_weight=up_weight,
@@ -1501,7 +1687,7 @@
         ),
         buffers(),
         number=1,
-        copies=260,
+        copies=COPIES,
     )
     results = run(
         end,

time: 190 us -> 147 us (0.77)
  Pallas kernels: 185 us -> 144 us
  local copies, waits for them, and re-layouts: 3.26 us -> 0 us
    pallas_call x2, Pallas kernels: 185 us -> 144 us  [run(): pl.pallas_call(kernel, out_shape=[jax.ShapeDtypeStruct(out.shape, out.dty...]
    concatenate x1 -> x0, local copies, waits for them, and re-layouts: 2.61 us -> none  [on_device(): jnp.concatenate([attn_norm, attn_post_norm, ffn_norm, ffn_post_norm, quer...]
where the time goes in v3:
time: 147 us; the launch traced here: 145 us
  Pallas kernels  144 us (98%)
    pallas_call x2, Pallas kernels, run(): pl.pallas_call(kernel, out_shape=[jax.ShapeDtypeStruct(out.shape, out.dty...  144 us

profile of v3, /device:TPU:0, one launch (start us, length us, event | category | flops | bytes accessed | tf_op | source)
XLA Modules:
  0.0 145.2 jit_solution(54043309515355595)
XLA Ops:
  0.7 142.5 %shard_map.298 = (bf16[128,640]{1,0:T(8,128)(2,1)}, bf16[128,640]{1,0:T(8,128)(2,1)}, f32[128,128]{1,0:T(8,128)}, f32[128,128]{1,0:T(8,128)}, f32[80,128]{1,0:T(8,128)}, /*index=5*/f32[32,128]{1,0:T(8,128)}) custom-call(s32[128]{0:T(128)} %refs_0_.1, s32[1,8]{1,0:T(1,128)} %refs_1_.1, bf16[1,128,640]{2,1,0:T(8,128)(2,1)} %refs_2_.1, ...), custom_call_target="tpu_custom_call" | custom-call | tf_op jit(solution)/shard_map/pallas_call | solution.py:186
  143.2 1.9 %shard_map.299 = (bf16[1,128,640]{2,1,0:T(8,128)(2,1)}, bf16[1,128,640]{2,1,0:T(8,128)(2,1)}, f32[1,5]{1,0:T(1,128)}, f32[5,1024]{1,0:T(8,128)}, f32[5,256]{1,0:...) custom-call(bf16[128,640]{1,0:T(8,128)(2,1)} %get-tuple-element.36.r, ...), custom_call_target="tpu_custom_call" | custom-call | tf_op jit(solution)/shard_map/pallas_call | solution.py:186

commit v4 on v3

--- a/solution.py
+++ b/solution.py
@@ -79,8 +79,13 @@
             peer(self.axis, step),
         )
 
-    def start(self, step):
-        self.copy(step, place()[self.axis]).start()
+    def start(self, step, *index):
+        source, landing = self.source(step), self.landing(step, place()[self.axis])
+        if index:
+            source, landing = source.at[index], landing.at[index]
+        self.links.copy(
+            self.sends, self.numbers[step], source, landing, peer(self.axis, step)
+        ).start()
 
     def wait(self, step):
         self.copy(step, shifted(place()[self.axis], -step)).wait_recv()
@@ -164,33 +169,45 @@
 
 VMEM = pl.BlockSpec(memory_space=pltpu.VMEM)
 SMEM = pl.BlockSpec(memory_space=pltpu.SMEM)
+ANY = pl.BlockSpec(memory_space=pl.ANY)
 
 
 def hold(kind, *shape):
     return pltpu.VMEM(shape, kind)
 
 
-def run(stage, numbers, ins, outs, scratch, number=None, copies=()):
+def run(stage, numbers, ins, outs, scratch, number=None, copies=(), fetched={}):
     flat, shape = jax.tree.flatten(scratch, is_leaf=lambda leaf: not isinstance(leaf, (dict, list)))
 
     def kernel(*refs):
-        count = len(numbers) + len(ins) + len(outs)
-        named = dict(zip((*numbers, *ins, *outs), refs))
-        named.update(jax.tree.unflatten(shape, refs[count : count + len(flat)]))
+        count = len(numbers) + len(fetched) + len(ins) + len(outs)
+        named = dict(zip((*numbers, *fetched, *ins, *outs), refs))
+        rest = refs[count + len(flat) :]
         r = SimpleNamespace(**named)
+        vars(r).update(jax.tree.unflatten(shape, refs[count : count + len(flat)]))
+        r.fetches = {}
+        for at, name in enumerate(fetched):
+            held = rest[at]
+            copy = pltpu.make_async_copy(named[name], held, rest[len(fetched)].at[at])
+            copy.start()
+            r.fetches[name] = copy
+            setattr(r, name, held)
         if copies:
-            r.links = Links(*refs[count + len(flat) :])
+            r.links = Links(*rest[-2:])
         stage(r)
 
     remote = dict(collective_id=number, has_side_effects=True) if copies else {}
     results = pl.pallas_call(
         kernel,
         out_shape=[jax.ShapeDtypeStruct(out.shape, out.dtype) for out in outs.values()],
-        in_specs=[SMEM] * len(numbers) + [VMEM] * len(ins),
+        in_specs=[SMEM] * len(numbers) + [ANY] * len(fetched) + [VMEM] * len(ins),
         out_specs=[VMEM] * len(outs),
-        scratch_shapes=flat + [pltpu.SemaphoreType.DMA((count,)) for count in copies],
+        scratch_shapes=flat
+        + [pltpu.VMEM(value.shape, value.dtype) for value in fetched.values()]
+        + ([pltpu.SemaphoreType.DMA((len(fetched),))] if fetched else [])
+        + [pltpu.SemaphoreType.DMA((count,)) for count in copies],
         compiler_params=pltpu.CompilerParams(vmem_limit_bytes=60 * MIB, **remote),
-    )(*numbers.values(), *ins.values())
+    )(*numbers.values(), *fetched.values(), *ins.values())
     return dict(zip(outs, results))
 
 
@@ -318,10 +335,11 @@
     for ref, (_, _, held, lane) in zip(own, GAINS):
         r.stage[356:357, lane : lane + held] = ref[...].astype(F32)
     spot = place()
-    for part, ref in enumerate(r.p):
-        first, second, _ = ORDERS[part]
+    for number, ref in enumerate(r.p):
+        first, second, _ = weight_order(number)
         rows = ref.shape[2]
-        ref[spot[second], spot[first]] = r.stage[128 * part : 128 * part + rows].astype(BF16)
+        start = (0, 80, 128, 208, 256)[number]
+        ref[spot[second], spot[first]] = r.stage[start : start + rows].astype(BF16)
     core = lax.axis_index("dp")
     x, y, z = spot
     r.u[0][core, x, y, z] = r.stage[336:352].astype(BF16)
@@ -395,8 +413,8 @@
     one = small(Z, 0, lambda at: (core, x, y, at))
     two = small(X, 1, lambda at: (core, y, z, at))
     rings = []
-    for part, ref in enumerate(r.p):
-        first, second, _ = ORDERS[part]
+    for number, ref in enumerate(r.p):
+        first, second, _ = weight_order(number)
         row = spot[second]
         rings.append(
             links.ring(
@@ -411,9 +429,9 @@
     one = small(Y, 0, lambda at: (core, x, at))
     two.wait_all()
     two = small(Z, 1, lambda at: (core, y, at))
-    for part, ref in enumerate(r.p):
-        rings[part].wait_all()
-        second = ORDERS[part][1]
+    for number, ref in enumerate(r.p):
+        rings[number].wait_all()
+        second = weight_order(number)[1]
         rings.append(
             links.ring(
                 second,
@@ -428,16 +446,20 @@
     two.wait_all()
     two = small(Y, 1, lambda at: (core, at))
     spreads = {}
-    for part, weights in ((2, (DOWN,)), (0, (GATE, OUTPUT)), (1, (QUERY, UP))):
-        rings[3 + part].wait_all()
-        for number in weights:
+
+    def begin(*numbers):
+        for number in numbers:
+            rings[5 + number].wait_all()
             unpack(r, number)
-        for piece in EARLY_PIECES[part]:
-            spreads[piece] = Spread(r, piece)
+            for piece in EARLY_PIECES[number]:
+                spreads[piece] = Spread(r, piece)
+
+    begin(DOWN, GATE, OUTPUT)
     one.wait_all()
     three = links.across(r.u[0].at[core], lambda at: r.u[0].at[at], r.u[0].at[core])
     two.wait_all()
     four = links.across(r.u[1].at[core], lambda at: r.u[1].at[at], r.u[1].at[core])
+    begin(QUERY, UP)
     three.wait()
     four.wait()
     return rings, held + [three, four], spreads
@@ -463,19 +485,21 @@
         r.gains[0:1, at : at + columns] = jnp.sum(spread, axis=0, keepdims=True)
 
 
-WEIGHTS = ((0, 0, 80, False), (0, 80, 40, False), (1, 0, 80, False), (1, 80, 40, False), (2, 0, 80, True))
+WEIGHTS = ((0, 80, False), (0, 40, False), (1, 80, False), (1, 40, False), (2, 80, True))
 GATE, OUTPUT, UP, QUERY, DOWN = range(5)
 
 
+def weight_order(number):
+    return ORDERS[WEIGHTS[number][0]]
+
+
 def own_plane(r, number):
-    part = WEIGHTS[number][0]
-    return weight_plane(r.w[number], number, lax.axis_index("dp"), place()[ORDERS[part][2]])
+    return weight_plane(r.w[number], number, lax.axis_index("dp"), place()[weight_order(number)[2]])
 
 
 def weight_plane(ref, number, core, at):
-    part, _, _, by_chip = WEIGHTS[number]
-    if by_chip:
-        return of_plane(ref.at[core], ORDERS[part][2], at)
+    if WEIGHTS[number][2]:
+        return of_plane(ref.at[core], weight_order(number)[2], at)
     return ref.at[core, at]
 
 
@@ -484,13 +508,13 @@
 
 
 def unpack(r, number):
-    part, first, rows, by_chip = WEIGHTS[number]
+    _, rows, by_chip = WEIGHTS[number]
     count, tiles = plane_tiles(number)
     plane = own_plane(r, number)
 
     def one(chip):
-        r.stage[pl.ds(pl.multiple_of(chip * rows, 8), rows)] = r.p[part][
-            chip // 4, chip % 4, first : first + rows
+        r.stage[pl.ds(pl.multiple_of(chip * rows, 8), rows)] = r.p[number][
+            chip // 4, chip % 4, :rows
         ].astype(F32)
 
     loop(16, one)
@@ -544,6 +568,18 @@
     normed = rms_scale(x, gain(r, G_ATTN)).astype(BF16)
     r.normed[...] = normed
     r.normed_split[...] = dot32(normed, r.splitting[...]).astype(BF16)
+    split = r.normed_split[...].astype(F32)
+    none = jnp.zeros((128, 64), F32)
+    zero, one = (
+        jnp.concatenate(
+            [split[:, 256 * core : 256 * core + 256], split[:, 512 + 64 * core : 576 + 64 * core], none],
+            axis=1,
+        )
+        for core in range(2)
+    )
+    core = lax.axis_index("dp")
+    r.both_split[core] = jnp.where(core == 0, zero, one).astype(BF16)
+    r.out_split[...] = jnp.where(core == 0, one, zero).astype(BF16)
     raw = dot32(r.normed_split[...], r.w_kv[...])
     r.key_raw[...] = raw[:, :HEAD]
     keys = rope(r, rms_scale(raw[:, :HEAD], gain(r, G_KEY)))
@@ -591,7 +627,7 @@
     (DOWN, 2, 2),
 )
 GATE_ONE, GATE_TWO, OUT, UP_ONE, UP_TWO, ASK, DOWN_ONE, DOWN_TWO = range(8)
-EARLY_PIECES = ((OUT, GATE_ONE), (ASK, UP_ONE), (DOWN_ONE,))
+EARLY_PIECES = ((GATE_ONE,), (OUT,), (UP_ONE,), (ASK,), (DOWN_ONE,))
 LATE_PIECES = (GATE_TWO, UP_TWO, DOWN_TWO)
 
 
@@ -622,7 +658,7 @@
 
 
 def piece_axis(piece):
-    return ORDERS[WEIGHTS[PIECES[piece][0]][0]][2]
+    return weight_order(PIECES[piece][0])[2]
 
 
 class Spread:
@@ -917,15 +953,19 @@
                 :, 128 * lane : 128 * lane + 128
             ].reshape(4, 4, 16, 128)
 
-    for plane in range(4):
-        chunk(3, plane)
-    between(0)
+    every = (slice(None), slice(None))
     rings, specials = scatter_third(r)
     for number, step in enumerate((1, 3, 2)):
         for token in range(3):
             chunk(token, shifted(spot[chunk_axis(token)], step))
-            rings[token].start(step)
-        between(number + 1)
+            rings[token].start(step, *every, pl.ds(0, 64))
+        between(number)
+    for plane in range(4):
+        chunk(3, plane)
+    for step in (1, 3, 2):
+        for part, (_, rows) in enumerate(KV_ROWS):
+            rings[part].start(step, *every, pl.ds(64, rows - 64))
+    between(3)
     keys, values = extra_kv(r)
     places = extra_places(r, lax.broadcasted_iota(jnp.int32, (192, 1), 0))
     grads = grads_of(keys, values, (places >= earliest) & (places <= latest))
@@ -953,12 +993,15 @@
 
 def queries(r):
     r.normed_b[...] = turned(r, r.normed[...])
+    split_rows(r.both_normed, r.out_normed, r.normed_b[...])
+    shared = share(r, r.both_normed, r.out_normed)
     r.query_raw[...] = dot32(r.normed_b[...], r.w[QUERY][...].reshape(640, 1024))
     for head in range(HEADS):
         raw = r.query_raw[:, HEAD * head : HEAD * head + HEAD]
         rotated = rope(r, rms_scale(raw, gain(r, G_QUERY))).astype(BF16)
         for block in range(2):
             r.query[head_rows(block, head)] = rotated[64 * block : 64 * block + 64]
+    return shared
 
 
 def gelu_parts(gate):
@@ -973,6 +1016,35 @@
 
 def down_rows(ref, number):
     return ref.at[number // 2, pl.ds(2 * (number % 2), 2)]
+
+
+def split_rows(both, out, values):
+    core = lax.axis_index("dp")
+    values = values.astype(F32)
+    none = jnp.zeros((128, 64), F32)
+    low = jnp.concatenate([values[:, :320], none], axis=1)
+    high = jnp.concatenate([values[:, 320:], none], axis=1)
+    both[core] = jnp.where(core == 0, low, high).astype(BF16)
+    out[...] = jnp.where(core == 0, high, low).astype(BF16)
+
+
+def share(r, both, source):
+    return r.links.across(source, lambda core: both.at[core], source)
+
+
+def own_columns(ref, width, core):
+    return ref.at[:, pl.ds(pl.multiple_of(core * width, width), width)]
+
+
+def share_columns(r, both, ref):
+    core = lax.axis_index("dp")
+    width = ref.shape[1] // 2
+    both[core] = own_columns(ref, width, core)[...]
+    return share(r, both, own_columns(ref, width, 1 - core))
+
+
+def pair(both):
+    return both[...].reshape(256, both.shape[2])
 
 
 def feed_forward(r, spreads):
@@ -982,6 +1054,7 @@
             r.attn_low[64 * block : 64 * block + 64, HEAD * head : HEAD * head + HEAD] = r.attn[
                 head_rows(block, head)
             ].astype(BF16)
+    shared = {OUTPUT: share_columns(r, r.both_attn, r.attn_low)}
     r.proj[...] = dot32(r.attn_low[...], r.w[OUTPUT][...].reshape(1024, 640))
     r.mid[...] = r.x[...] + rms_scale(r.proj[...], gain(r, G_POST_ATTN))
     r.ffn_in[...] = rms_scale(r.mid[...], gain(r, G_FFN)).astype(BF16)
@@ -995,11 +1068,17 @@
         r.gate[:, at] = gate
         r.up[:, at] = up
         r.hidden[:, at] = (gelu_parts(gate)[0] * up).astype(BF16)
+    split_rows(r.both_in, r.out_in, r.ffn_in[...])
+    shared[GATE] = share(r, r.both_in, r.out_in)
+    split_rows(r.both_in_b, r.out_in_b, r.ffn_in_b[...])
+    shared[UP] = share(r, r.both_in_b, r.out_in_b)
+    shared[DOWN] = share_columns(r, r.both_hidden, r.hidden)
     spreads[DOWN_ONE].finish()
     spreads[DOWN_TWO].finish()
     r.ffn_out[...] = dot32(r.hidden[...], r.w[DOWN][...].reshape(2048, 640))
     out = r.mid[...] + rms_scale(r.ffn_out[...], gain(r, G_POST_FFN))
     r.block_out[...] = low_first(r, out.astype(BF16))
+    return shared
 
 
 def note_gain(r, number, term):
@@ -1007,24 +1086,23 @@
     r.gain_sums[0:1, at : at + count] = term
 
 
-def feed_forward_back(r, spreads):
+def feed_forward_back(r, spreads, shared, start):
+    core = lax.axis_index("dp")
     for piece in (GATE_ONE, GATE_TWO, OUT, UP_ONE, UP_TWO, DOWN_ONE, DOWN_TWO):
         spreads[piece].free()
     grad_out = low_first(r, r.out_cot[0].astype(F32))
     grad_ffn_out, term = norm_back(r.ffn_out[...], gain(r, G_POST_FFN), grad_out)
     note_gain(r, G_POST_FFN, term)
     low_grad = grad_ffn_out.astype(BF16)
-    r.low_grad[...] = low_grad
-    halves = {}
+    r.both_low[core] = low_grad
+    low_shared = share(r, r.both_low, r.both_low.at[core])
     grad_in = jnp.zeros((128, 640), F32)
     grad_in_b = jnp.zeros((128, 640), F32)
+    grads_shared = []
     for number in range(4):
         at = slice(512 * number, 512 * number + 512)
         down = down_rows(r.w[DOWN], number)
         grad_hidden = dot_nt(low_grad, down[...].reshape(512, 640))
-        down[...] = (
-            dot_tn(r.hidden[:, at], low_grad).astype(BF16).reshape(2, 4, 4, 16, 640)
-        )
         gate, up = r.gate[:, at], r.up[:, at]
         activated, inner = gelu_parts(gate)
         slope = 0.5 * (1.0 + inner) + 0.5 * gate * (1.0 - inner * inner) * GELU * (
@@ -1032,17 +1110,41 @@
         )
         grad_gate = (grad_hidden * up * slope).astype(BF16)
         grad_up = (grad_hidden * activated).astype(BF16)
+        r.both_gate[core, :, at] = grad_gate
+        r.both_up[core, :, at] = grad_up
         grad_in += dot_nt(grad_gate, columns(r.w[GATE], 512 * number, 512))
         grad_in_b += dot_nt(grad_up, columns(r.w[UP], 512 * number, 512))
-        term = dot_tn(r.ffn_in[...], grad_gate).astype(BF16)
-        r.w[GATE][:, :, :, at] = term.reshape(2, 4, 80, 512)
-        term = dot_tn(r.ffn_in_b[...], grad_up).astype(BF16)
-        r.w[UP][:, :, :, at] = term.reshape(2, 4, 80, 512)
-        if number == 1:
-            halves[GATE_ONE] = send_half(r, GATE_ONE)
-            halves[UP_ONE] = send_half(r, UP_ONE)
-    for piece in (DOWN_ONE, DOWN_TWO, GATE_TWO, UP_TWO):
-        halves[piece] = send_half(r, piece)
+        if number % 2:
+            lanes = pl.ds(512 * number - 512, 1024)
+            for both in (r.both_gate, r.both_up):
+                grads_shared.append(
+                    r.links.across(
+                        both.at[core, :, lanes],
+                        lambda core, both=both, lanes=lanes: both.at[core, :, lanes],
+                        both.at[core, :, lanes],
+                    )
+                )
+    shared[DOWN].wait()
+    low_shared.wait()
+    term = dot_tn(pair(r.both_hidden), pair(r.both_low)).astype(BF16)
+    r.w[DOWN][core] = term.reshape(4, 4, 4, 16, 640)
+    start(DOWN_ONE, DOWN_TWO)
+    shared[GATE].wait()
+    shared[UP].wait()
+
+    def columns_of_both(first):
+        for number, ins, both, wait in (
+            (GATE, r.both_in, r.both_gate, grads_shared[first // 512]),
+            (UP, r.both_in_b, r.both_up, grads_shared[first // 512 + 1]),
+        ):
+            wait.wait()
+            for at in (first, first + 512):
+                lanes = slice(at, at + 512)
+                term = dot_tn(pair(ins), both[:, :, lanes].reshape(256, 512))[:320].astype(BF16)
+                r.w[number][core, :, :, lanes] = term.reshape(4, 80, 512)
+
+    columns_of_both(0)
+    start(GATE_ONE, UP_ONE)
     grad_in = grad_in + unturned(r, grad_in_b)
     back, term = norm_back(r.mid[...], gain(r, G_FFN), grad_in)
     note_gain(r, G_FFN, term)
@@ -1051,10 +1153,9 @@
     back, term = norm_back(r.proj[...], gain(r, G_POST_ATTN), grad_mid)
     note_gain(r, G_POST_ATTN, term)
     proj_low = back.astype(BF16)
+    r.both_proj[core] = proj_low
+    proj_shared = share(r, r.both_proj, r.both_proj.at[core])
     grad_attn = dot_nt(proj_low, r.w[OUTPUT][...].reshape(1024, 640)).astype(BF16)
-    term = dot_tn(r.attn_low[...], proj_low).astype(BF16)
-    r.w[OUTPUT][...] = term.reshape(2, 4, 128, 640)
-    halves[OUT] = send_half(r, OUT)
     for block in range(2):
         for head in range(HEADS):
             r.grad_attn[head_rows(block, head)] = grad_attn[
@@ -1062,10 +1163,19 @@
             ]
     dots = jnp.sum(r.grad_attn[...].astype(F32) * r.attn[...], axis=1, keepdims=True)
     r.dots[...] = jnp.broadcast_to(dots, (512, 128))
-    return halves
-
-
-def queries_back(r, spreads):
+
+    def rest_back():
+        columns_of_both(1024)
+        shared[OUTPUT].wait()
+        proj_shared.wait()
+        term = dot_tn(pair(r.both_attn), pair(r.both_proj)).astype(BF16)
+        r.w[OUTPUT][core] = term.reshape(4, 128, 640)
+
+    return rest_back
+
+
+def queries_back(r, spreads, shared):
+    core = lax.axis_index("dp")
     total = jnp.zeros((1, HEAD), F32)
     for head in range(HEADS):
         at = slice(HEAD * head, HEAD * head + HEAD)
@@ -1074,19 +1184,17 @@
             r.query_raw[:, at], gain(r, G_QUERY), rope_back(r, grad * QUARTER)
         )
         total += term
-        r.query_low[:, at] = back.astype(BF16)
+        r.both_query[core, :, at] = back.astype(BF16)
     note_gain(r, G_QUERY, total)
-    r.grad_normed[...] = unturned(r, dot_nt(r.query_low[...], r.w[QUERY][...].reshape(640, 1024)))
+    query_shared = share(r, r.both_query, r.both_query.at[core])
+    r.grad_normed[...] = unturned(
+        r, dot_nt(r.both_query[core], r.w[QUERY][...].reshape(640, 1024))
+    )
     spreads[ASK].free()
-    term = dot_tn(r.normed_b[...], r.query_low[...]).astype(BF16)
-    r.w[QUERY][...] = term.reshape(2, 4, 80, 1024)
-    return send_half(r, ASK)
-
-
-def send_half(r, piece):
-    number = PIECES[piece][0]
-    grad, half = piece_of(piece, r.w[number]), piece_of(piece, r.half[number])
-    return r.links.across(grad.at[1 - lax.axis_index("dp")], lambda at: half, half)
+    shared[QUERY].wait()
+    query_shared.wait()
+    term = dot_tn(pair(r.both_normed), pair(r.both_query))[:320].astype(BF16)
+    r.w[QUERY][core] = term.reshape(4, 80, 1024)
 
 
 def add_rows(count, to, value):
@@ -1110,12 +1218,10 @@
 
 
 class Gather:
-    def __init__(self, r, piece, over):
+    def __init__(self, r, piece):
         self.piece, axis = piece, piece_axis(piece)
         core, mine = lax.axis_index("dp"), place()[axis]
         number = PIECES[piece][0]
-        over.wait()
-        add_into(piece_of(piece, r.w[number]).at[core], piece_of(piece, r.half[number]))
         self.land = piece_of(piece, r.landed[number], 3)
         self.at = lambda step: piece_plane(r, piece, core, shifted(mine, step))
         sends = r.links.sends(self.land)
@@ -1149,7 +1255,7 @@
 
 
 def repack(r, number, *gathers):
-    part, first, rows, by_chip = WEIGHTS[number]
+    _, rows, by_chip = WEIGHTS[number]
     count, tiles = plane_tiles(number)
     own, land = own_plane(r, number), r.landed[number]
     for gather in gathers:
@@ -1161,44 +1267,44 @@
         r.stage[pl.ds(tile, count, stride=tiles)] = total.reshape(count, 128)
 
     def one(chip):
-        r.p[part][chip // 4, chip % 4, first : first + rows] = r.stage[
+        r.p[number][chip // 4, chip % 4, :rows] = r.stage[
             pl.ds(pl.multiple_of(chip * rows, 8), rows)
         ].astype(BF16)
 
     loop(16, one)
 
 
-def late_second(r, part):
-    second = ORDERS[part][1]
+def late_second(r, number):
+    second = weight_order(number)[1]
     mine = place()[second]
     return r.links.ring(
         second,
-        lambda step: r.p[part].at[shifted(mine, step)],
-        lambda step, at: r.second[part].at[step - 1],
-        r.second[part],
+        lambda step: r.p[number].at[shifted(mine, step)],
+        lambda step, at: r.second[number].at[step - 1],
+        r.second[number],
     )
 
 
-def late_first(r, part, ring):
-    first, second, _ = ORDERS[part]
+def late_first(r, number, ring):
+    first, second, _ = weight_order(number)
     mine, own = place()[first], place()[second]
     ring.wait_all()
     for at in range(4):
-        r.line[part][at] = add_all(
-            [r.p[part][own, at]] + [r.second[part][step, at] for step in range(3)]
+        r.line[number][at] = add_all(
+            [r.p[number][own, at]] + [r.second[number][step, at] for step in range(3)]
         ).astype(BF16)
     return r.links.ring(
         first,
-        lambda step: r.line[part].at[shifted(mine, step)],
-        lambda step, at: r.first[part].at[step - 1],
-        r.first[part],
+        lambda step: r.line[number].at[shifted(mine, step)],
+        lambda step, at: r.first[number].at[step - 1],
+        r.first[number],
     )
 
 
-def late_end(r, part, ring, out):
-    mine = place()[ORDERS[part][0]]
+def late_end(r, number, ring, out):
+    mine = place()[weight_order(number)[0]]
     ring.wait_all()
-    out[...] = add_all([r.line[part][mine]] + [r.first[part][step] for step in range(3)])
+    out[...] = add_all([r.line[number][mine]] + [r.first[number][step] for step in range(3)])
 
 
 def scatter_third(r):
@@ -1313,7 +1419,7 @@
             )
 
 
-def keys_values_back(r):
+def keys_values_back(r, split_shared):
     lanes = []
     for lane in range(4):
         pieces = [
@@ -1325,47 +1431,51 @@
     back, term = norm_back(r.key_raw[...], gain(r, G_KEY), rope_back(r, grad_keys))
     note_gain(r, G_KEY, term)
     kv_low = jnp.concatenate([back, grad_values], axis=1).astype(BF16)
-    terms = dot_tn(r.normed_split[...], kv_low)
-    r.stage[SMALL : 2 * SMALL] = jnp.zeros((SMALL, 128), F32)
-    for tile in range(4):
-        lanes = slice(128 * tile, 128 * tile + 128)
-        r.stage[pl.ds(tile, 512, stride=4)] = terms[:512, lanes]
-        r.stage[pl.ds(SMALL + tile, 128, stride=16)] = terms[512:, lanes]
+    core = lax.axis_index("dp")
+    r.both_kv[core] = kv_low
+    kv_shared = share(r, r.both_kv, r.both_kv.at[core])
     grad_split = dot_nt(kv_low, r.w_kv[...]).astype(BF16)
     grad_normed = dot_nt(grad_split, r.splitting[...]) + r.grad_normed[...]
     back, term = norm_back(r.x[...], gain(r, G_ATTN), grad_normed)
     note_gain(r, G_ATTN, term)
+    gains_back(r, G_KEY, G_ATTN)
+    low, high = r.held[:64], r.held[64:]
+    r.both_held[core] = jnp.where(core == 0, low, high)
+    r.out_held[...] = jnp.where(core == 0, high, low)
+    held_shared = share(r, r.both_held, r.out_held)
     r.tokens_grad[...] = low_first(r, (r.grad_mid[...] + back).astype(BF16))
-    held = jnp.zeros((128, 128), F32)
-    for number, (at, count, _, _) in enumerate(GAINS):
+    r.stage[SMALL : SMALL + 1024] = jnp.zeros((1024, 128), F32)
+    split_shared.wait()
+    kv_shared.wait()
+    terms = dot_tn(pair(r.both_split), pair(r.both_kv))
+    for tile in range(4):
+        lanes = slice(128 * tile, 128 * tile + 128)
+        r.stage[pl.ds(tile, 256, stride=4)] = terms[:256, lanes]
+        r.stage[pl.ds(SMALL + tile, 64, stride=16)] = terms[256:320, lanes]
+    held_shared.wait()
+    r.stage[pl.ds(SMALL + 4, 64, stride=16)] = r.both_held[0] + r.both_held[1]
+    for unit in range(2):
+        for plane in range(4):
+            row = SMALL * unit + 256 * plane
+            r.u[unit][core, plane] = r.stage[row : row + 256].astype(BF16).reshape(4, 4, 16, 128)
+
+
+def gains_back(r, *numbers):
+    for number in numbers:
+        at, count, _, _ = GAINS[number]
         lanes, owners = gain_maps(r, number)
         term = jnp.where(owners, r.gain_sums[0:1, at : at + count], 0.0).astype(BF16)
-        held += dot_nt(term, lanes)
-    r.stage[pl.ds(SMALL + 4, 128, stride=16)] = held
-    for unit in range(2):
-        for core in range(2):
-            for plane in range(4):
-                row = SMALL * unit + 1024 * core + 256 * plane
-                r.u[unit][core, plane] = r.stage[row : row + 256].astype(BF16).reshape(4, 4, 16, 128)
+        r.held[...] += dot_nt(term, lanes)
 
 
 def small_sums(r, between):
     links = r.links
     core = lax.axis_index("dp")
     spot = place()
-    overs = [links.across(ref.at[1 - core], lambda at, to=to: to, to) for ref, to in zip(r.u, r.vh)]
     axes = ((X, Y, Z), (Y, Z, X))
     rings = []
     for unit, order in enumerate(axes):
-        half, own, land = r.vh[unit], r.u[unit], r.land3[unit]
-        overs[unit].wait()
-
-        def join(number, half=half, own=own):
-            at = (number // 4, number % 4)
-            index = (core, *at)
-            own[index] = (own[index].astype(F32) + half[at].astype(F32)).astype(BF16)
-
-        loop(16, join)
+        own, land = r.u[unit], r.land3[unit]
         axis = order[0]
         rings.append(
             links.ring(
@@ -1422,12 +1532,15 @@
 
 def layer(r):
     greet()
+    for copy in r.fetches.values():
+        copy.wait()
     pack(r)
     greeted()
     early_rings, early_held, spreads = early(r)
     unpack_small(r)
     keys_values(r)
     firsts = gather_first(r)
+    split_shared = share(r, r.both_split, r.out_split)
     seconds = gather_second(r, firsts)
     early_pieces = (ASK, OUT, GATE_ONE, UP_ONE, DOWN_ONE)
     for piece in early_pieces:
@@ -1441,7 +1554,7 @@
     for piece in LATE_PIECES:
         spreads[piece].forward()
     spreads[ASK].finish()
-    queries(r)
+    query_shared = queries(r)
 
     def pass_on(number):
         if number == 0:
@@ -1451,64 +1564,79 @@
                 spreads[piece].pass_on()
 
     attention(r, thirds, specials, pass_on)
-    feed_forward(r, spreads)
+    shared = feed_forward(r, spreads)
+    shared[QUERY] = query_shared
     before = tuple(r.links.open)
-    halves = feed_forward_back(r, spreads)
     sums = {}
 
-    def start_sums(*pieces):
+    def start(*pieces):
         for piece in pieces:
-            sums[piece] = Gather(r, piece, halves[piece])
+            sums[piece] = Gather(r, piece)
 
     def relay(*pieces):
         for piece in pieces:
             sums[piece].relay()
 
-    def between(number):
-        pass
-
-    thirds, third_specials = attention_back(r, between)
-    halves[ASK] = queries_back(r, spreads)
+    late = {}
+
+    def send_late(*numbers):
+        pieces = {
+            GATE: (GATE_ONE, GATE_TWO),
+            OUTPUT: (OUT,),
+            UP: (UP_ONE, UP_TWO),
+            QUERY: (ASK,),
+            DOWN: (DOWN_ONE, DOWN_TWO),
+        }
+        for number in numbers:
+            repack(r, number, *(sums[piece] for piece in pieces[number]))
+            late[number] = late_second(r, number)
+
+    def go_on(*numbers):
+        for number in numbers:
+            late[number] = late_first(r, number, late[number])
+
+    def finish(*numbers):
+        outs = (r.fgate, r.foutput, r.fup, r.fquery, r.fdown)
+        for number in numbers:
+            late_end(r, number, late[number], outs[number])
+
+    rest_back = feed_forward_back(r, spreads, shared, start)
+    thirds, third_specials = attention_back(r, lambda number: None)
+    queries_back(r, spreads, shared)
+    rest_back()
+    start(GATE_TWO, UP_TWO, OUT, ASK)
     for ring in early_rings:
         ring.sent()
     for ring in seconds:
         ring.sent()
     r.links.settle(before)
     before = tuple(r.links.open)
-    start_sums(GATE_ONE, UP_ONE, DOWN_ONE, GATE_TWO, UP_TWO, DOWN_TWO, OUT, ASK)
+    r.held[...] = jnp.zeros_like(r.held)
+    gains_back(r, G_POST_ATTN, G_FFN, G_POST_FFN, G_QUERY)
     seconds = scatter_second(r, thirds, third_specials)
-    relay(GATE_ONE, UP_ONE, DOWN_ONE, OUT)
+    relay(DOWN_ONE, GATE_ONE, UP_ONE)
     firsts = scatter_first(r, seconds)
-    relay(GATE_TWO, UP_TWO, DOWN_TWO, ASK)
+    relay(DOWN_TWO, GATE_TWO, UP_TWO)
     scatter_end(r, firsts)
+    relay(OUT, ASK)
     for copy in early_held:
         copy.sent()
-    keys_values_back(r)
-    late = {}
-
-    def begin_late():
+    keys_values_back(r, split_shared)
+
+    def one():
         r.links.settle(before)
-        repack(r, DOWN, sums[DOWN_ONE], sums[DOWN_TWO])
-        late[2] = late_second(r, 2)
-        repack(r, GATE, sums[GATE_ONE], sums[GATE_TWO])
-        repack(r, OUTPUT, sums[OUT])
-        late[0] = late_second(r, 0)
-        repack(r, UP, sums[UP_ONE], sums[UP_TWO])
-        repack(r, QUERY, sums[ASK])
-        late[1] = late_second(r, 1)
-
-    def go_on_late():
-        r.links.settle(tuple(r.links.open)[:-10])
-        for part in (2, 0, 1):
-            late[part] = late_first(r, part, late[part])
-
-    def finish_late():
-        for part, out in enumerate((r.fa, r.fb, r.fc)):
-            late_end(r, part, late[part], out)
-
-    small_sums(r, (begin_late, go_on_late, finish_late))
+        send_late(DOWN, GATE, UP)
+
+    def two():
+        send_late(OUTPUT, QUERY)
+
+    def three():
+        go_on(DOWN, GATE, UP, OUTPUT, QUERY)
+
+    small_sums(r, (one, two, three))
+    finish(DOWN, GATE, UP, OUTPUT, QUERY)
     r.links.settle()
-    assert (r.links.sending, r.links.receiving) <= COPIES and r.links.receiving <= COPIES[1]
+    assert r.links.sending <= COPIES[0] and r.links.receiving <= COPIES[1]
 
 
 def end(r):
@@ -1517,11 +1645,11 @@
         for tile in range(tiles):
             out[:, 128 * tile : 128 * tile + 128] = columns_of(r, base, count, tiles, tile)
 
-    rows(r.gate_grad, r.fa[0:80], 0, 5, 16)
-    rows(r.output_grad, r.fa[80:120], 80, 8, 5)
-    rows(r.up_grad, r.fb[0:80], 128, 5, 16)
-    rows(r.query_grad, r.fb[80:120], 208, 5, 8)
-    rows(r.down_grad, r.fc[...], 256, 16, 5)
+    rows(r.gate_grad, r.fgate[...], 0, 5, 16)
+    rows(r.output_grad, r.foutput[0:40], 80, 8, 5)
+    rows(r.up_grad, r.fup[...], 128, 5, 16)
+    rows(r.query_grad, r.fquery[0:40], 208, 5, 8)
+    rows(r.down_grad, r.fdown[...], 256, 16, 5)
     r.stage[336:368] = r.fk[...]
     for tile in range(4):
         out = (r.key_grad, r.value_grad)[tile // 2]
@@ -1537,7 +1665,7 @@
     r.final_grad[0] = r.tokens_grad[...]
 
 
-COPIES = (96, 160)
+COPIES = (97, 159)
 
 
 def by_part(*dims):
@@ -1545,7 +1673,7 @@
 
 
 def by_flat(*dims):
-    return [hold(BF16, *dims, rows, 128) for rows in (128, 128, 80)]
+    return [hold(BF16, *dims, rows, 128) for rows in (80, 48, 80, 48, 80)]
 
 
 def by_unit(*dims):
@@ -1579,7 +1707,12 @@
         line=by_flat(4),
         first=by_flat(3),
         u=by_unit(2, 4, 4, 4),
-        vh=by_unit(4, 4, 4),
+        both_split=hold(BF16, 2, 128, 384),
+        both_kv=hold(BF16, 2, 128, 512),
+        both_held=hold(F32, 2, 64, 128),
+        out_held=hold(F32, 64, 128),
+        out_split=hold(BF16, 128, 384),
+        held=hold(F32, 128, 128),
         land3=by_unit(3, 4, 4),
         sum2=by_unit(4, 4),
         land2=by_unit(3, 4),
@@ -1587,7 +1720,19 @@
         land1=by_unit(3),
         w_kv=hold(BF16, 640, 512),
         w=by_weight((4,), (2,)),
-        half=by_weight((4,), ()),
+        both_hidden=hold(BF16, 2, 128, 1024),
+        both_low=hold(BF16, 2, 128, 640),
+        both_gate=hold(BF16, 2, 128, 2048),
+        both_up=hold(BF16, 2, 128, 2048),
+        both_in=hold(BF16, 2, 128, 384),
+        both_in_b=hold(BF16, 2, 128, 384),
+        both_attn=hold(BF16, 2, 128, 512),
+        both_proj=hold(BF16, 2, 128, 640),
+        both_normed=hold(BF16, 2, 128, 384),
+        both_query=hold(BF16, 2, 128, 1024),
+        out_in=hold(BF16, 128, 384),
+        out_in_b=hold(BF16, 128, 384),
+        out_normed=hold(BF16, 128, 384),
         landed=[
             hold(BF16, 3, 80, 2048),
             hold(BF16, 3, 128, 640),
@@ -1627,11 +1772,9 @@
         up=hold(F32, 128, 2048),
         hidden=hold(BF16, 128, 2048),
         ffn_out=hold(F32, 128, 640),
-        low_grad=hold(BF16, 128, 640),
         grad_mid=hold(F32, 128, 640),
         grad_attn=hold(BF16, 512, 256),
         grad_query=hold(F32, 512, 256),
-        query_low=hold(BF16, 128, 1024),
         grad_normed=hold(F32, 128, 640),
     )
 
@@ -1658,17 +1801,21 @@
     made = run(
         layer,
         dict(block_order=block_order, doc_lengths=doc_lengths),
+        {},
         dict(
-            tokens=tokens,
-            out_cot=out_cot,
-            attn_norm=attn_norm[None],
-            attn_post_norm=attn_post_norm[None],
-            ffn_norm=ffn_norm[None],
-            ffn_post_norm=ffn_post_norm[None],
-            query_gain=query_gain[None],
-            key_gain=key_gain[None],
-            table=jnp.asarray(number_table()),
-            frequency=jnp.asarray(ROPE_BASE ** (-2.0 * np.arange(128) / 256), F32)[None],
+            block_out=hold(BF16, 128, 640),
+            tokens_grad=hold(BF16, 128, 640),
+            fgate=hold(F32, 80, 128),
+            foutput=hold(F32, 48, 128),
+            fup=hold(F32, 80, 128),
+            fquery=hold(F32, 48, 128),
+            fdown=hold(F32, 80, 128),
+            fk=hold(F32, 32, 128),
+        ),
+        buffers(),
+        number=1,
+        copies=COPIES,
+        fetched=dict(
             gate_weight=gate_weight,
             output_weight=output_weight,
             up_weight=up_weight,
@@ -1676,18 +1823,17 @@
             down_weight=down_weight,
             key_weight=key_weight,
             value_weight=value_weight,
+            attn_norm=attn_norm[None],
+            attn_post_norm=attn_post_norm[None],
+            ffn_norm=ffn_norm[None],
+            ffn_post_norm=ffn_post_norm[None],
+            query_gain=query_gain[None],
+            key_gain=key_gain[None],
+            tokens=tokens,
+            table=jnp.asarray(number_table()),
+            frequency=jnp.asarray(ROPE_BASE ** (-2.0 * np.arange(128) / 256), F32)[None],
+            out_cot=out_cot,
         ),
-        dict(
-            block_out=hold(BF16, 128, 640),
-            tokens_grad=hold(BF16, 128, 640),
-            fa=hold(F32, 128, 128),
-            fb=hold(F32, 128, 128),
-            fc=hold(F32, 80, 128),
-            fk=hold(F32, 32, 128),
-        ),
-        buffers(),
-        number=1,
-        copies=COPIES,
     )
     results = run(
         end,

time: 147 us -> 144 us (0.980)
    pallas_call x2, Pallas kernels: 144 us -> 143 us  [run(): pl.pallas_call(kernel, out_shape=[jax.ShapeDtypeStruct(out.shape, out.dty...]
where the time goes in v4:
time: 144 us
  Pallas kernels  143 us (99%)
    pallas_call x2, Pallas kernels, run(): pl.pallas_call(kernel, out_shape=[jax.ShapeDtypeStruct(out.shape, out.dty...  143 us

profile of v4, /device:TPU:0, one launch (start us, length us, event | category | flops | bytes accessed | tf_op | source)
XLA Modules:
  0.0 143.6 jit_solution(12169074715845765889)
XLA Ops:
  0.7 140.9 %shard_map.298 = (bf16[128,640]{1,0:T(8,128)(2,1)}, bf16[128,640]{1,0:T(8,128)(2,1)}, f32[80,128]{1,0:T(8,128)}, f32[48,128]{1,0:T(8,128)}, f32[80,128]{1,0:T(8,...) custom-call(s32[128]{0:T(128)} %refs_0_.1, s32[1,8]{1,0:T(1,128)} %refs_1_.1, ...), custom_call_target="tpu_custom_call" | custom-call | tf_op jit(solution)/shard_map/pallas_call | solution.py:200
  141.6 1.9 %shard_map.299 = (bf16[1,128,640]{2,1,0:T(8,128)(2,1)}, bf16[1,128,640]{2,1,0:T(8,128)(2,1)}, f32[1,5]{1,0:T(1,128)}, f32[5,1024]{1,0:T(8,128)}, f32[5,256]{1,0:...) custom-call(bf16[128,640]{1,0:T(8,128)(2,1)} %get-tuple-element.38.r, ...), custom_call_target="tpu_custom_call" | custom-call | tf_op jit(solution)/shard_map/pallas_call | solution.py:200

commit v5 on v4

--- a/solution.py
+++ b/solution.py
@@ -627,8 +627,8 @@
     (DOWN, 2, 2),
 )
 GATE_ONE, GATE_TWO, OUT, UP_ONE, UP_TWO, ASK, DOWN_ONE, DOWN_TWO = range(8)
-EARLY_PIECES = ((GATE_ONE,), (OUT,), (UP_ONE,), (ASK,), (DOWN_ONE,))
-LATE_PIECES = (GATE_TWO, UP_TWO, DOWN_TWO)
+EARLY_PIECES = ((GATE_ONE, GATE_TWO), (OUT,), (UP_ONE, UP_TWO), (ASK,), (DOWN_ONE, DOWN_TWO))
+LATE_PIECES = (GATE_TWO, UP_TWO)
 
 
 def window(ref, dim, first, count):
@@ -1124,14 +1124,6 @@
                         both.at[core, :, lanes],
                     )
                 )
-    shared[DOWN].wait()
-    low_shared.wait()
-    term = dot_tn(pair(r.both_hidden), pair(r.both_low)).astype(BF16)
-    r.w[DOWN][core] = term.reshape(4, 4, 4, 16, 640)
-    start(DOWN_ONE, DOWN_TWO)
-    shared[GATE].wait()
-    shared[UP].wait()
-
     def columns_of_both(first):
         for number, ins, both, wait in (
             (GATE, r.both_in, r.both_gate, grads_shared[first // 512]),
@@ -1143,8 +1135,6 @@
                 term = dot_tn(pair(ins), both[:, :, lanes].reshape(256, 512))[:320].astype(BF16)
                 r.w[number][core, :, :, lanes] = term.reshape(4, 80, 512)
 
-    columns_of_both(0)
-    start(GATE_ONE, UP_ONE)
     grad_in = grad_in + unturned(r, grad_in_b)
     back, term = norm_back(r.mid[...], gain(r, G_FFN), grad_in)
     note_gain(r, G_FFN, term)
@@ -1165,6 +1155,15 @@
     r.dots[...] = jnp.broadcast_to(dots, (512, 128))
 
     def rest_back():
+        shared[DOWN].wait()
+        low_shared.wait()
+        term = dot_tn(pair(r.both_hidden), pair(r.both_low)).astype(BF16)
+        r.w[DOWN][core] = term.reshape(4, 4, 4, 16, 640)
+        start(DOWN_ONE, DOWN_TWO)
+        shared[GATE].wait()
+        shared[UP].wait()
+        columns_of_both(0)
+        start(GATE_ONE, UP_ONE)
         columns_of_both(1024)
         shared[OUTPUT].wait()
         proj_shared.wait()
@@ -1190,11 +1189,15 @@
     r.grad_normed[...] = unturned(
         r, dot_nt(r.both_query[core], r.w[QUERY][...].reshape(640, 1024))
     )
-    spreads[ASK].free()
-    shared[QUERY].wait()
-    query_shared.wait()
-    term = dot_tn(pair(r.both_normed), pair(r.both_query))[:320].astype(BF16)
-    r.w[QUERY][core] = term.reshape(4, 80, 1024)
+
+    def rest_back():
+        spreads[ASK].free()
+        shared[QUERY].wait()
+        query_shared.wait()
+        term = dot_tn(pair(r.both_normed), pair(r.both_query))[:320].astype(BF16)
+        r.w[QUERY][core] = term.reshape(4, 80, 1024)
+
+    return rest_back
 
 
 def add_rows(count, to, value):
@@ -1282,23 +1285,29 @@
         lambda step: r.p[number].at[shifted(mine, step)],
         lambda step, at: r.second[number].at[step - 1],
         r.second[number],
+        begin=False,
     )
 
 
-def late_first(r, number, ring):
-    first, second, _ = weight_order(number)
-    mine, own = place()[first], place()[second]
+def late_first(r, number):
+    first = weight_order(number)[0]
+    mine = place()[first]
+    return r.links.ring(
+        first,
+        lambda step: r.line[number].at[shifted(mine, step)],
+        lambda step, at: r.first[number].at[step - 1],
+        r.first[number],
+        begin=False,
+    )
+
+
+def late_line(r, number, ring):
+    own = place()[weight_order(number)[1]]
     ring.wait_all()
     for at in range(4):
         r.line[number][at] = add_all(
             [r.p[number][own, at]] + [r.second[number][step, at] for step in range(3)]
         ).astype(BF16)
-    return r.links.ring(
-        first,
-        lambda step: r.line[number].at[shifted(mine, step)],
-        lambda step, at: r.first[number].at[step - 1],
-        r.first[number],
-    )
 
 
 def late_end(r, number, ring, out):
@@ -1419,7 +1428,7 @@
             )
 
 
-def keys_values_back(r, split_shared):
+def keys_values_back(r, split_shared, between):
     lanes = []
     for lane in range(4):
         pieces = [
@@ -1444,6 +1453,7 @@
     r.out_held[...] = jnp.where(core == 0, high, low)
     held_shared = share(r, r.both_held, r.out_held)
     r.tokens_grad[...] = low_first(r, (r.grad_mid[...] + back).astype(BF16))
+    between()
     r.stage[SMALL : SMALL + 1024] = jnp.zeros((1024, 128), F32)
     split_shared.wait()
     kv_shared.wait()
@@ -1542,26 +1552,23 @@
     firsts = gather_first(r)
     split_shared = share(r, r.both_split, r.out_split)
     seconds = gather_second(r, firsts)
-    early_pieces = (ASK, OUT, GATE_ONE, UP_ONE, DOWN_ONE)
+    early_pieces = (ASK, OUT, GATE_ONE, UP_ONE, DOWN_ONE, DOWN_TWO)
     for piece in early_pieces:
         spreads[piece].forward()
+    for piece in LATE_PIECES:
+        spreads[piece].forward()
     before = tuple(r.links.open)
-    for piece in LATE_PIECES:
-        spreads[piece] = Spread(r, piece)
     thirds, specials = gather_third(r, seconds)
     for piece in early_pieces:
         spreads[piece].pass_on()
     for piece in LATE_PIECES:
-        spreads[piece].forward()
+        spreads[piece].pass_on()
     spreads[ASK].finish()
     query_shared = queries(r)
 
     def pass_on(number):
         if number == 0:
             r.links.settle(before)
-        if number == 2:
-            for piece in LATE_PIECES:
-                spreads[piece].pass_on()
 
     attention(r, thirds, specials, pass_on)
     shared = feed_forward(r, spreads)
@@ -1577,33 +1584,42 @@
         for piece in pieces:
             sums[piece].relay()
 
-    late = {}
+    pieces = {
+        GATE: (GATE_ONE, GATE_TWO),
+        OUTPUT: (OUT,),
+        UP: (UP_ONE, UP_TWO),
+        QUERY: (ASK,),
+        DOWN: (DOWN_ONE, DOWN_TWO),
+    }
+    second_rings, first_rings = {}, {}
+
+    def prepare_late():
+        for number in pieces:
+            second_rings[number] = late_second(r, number)
+            first_rings[number] = late_first(r, number)
 
     def send_late(*numbers):
-        pieces = {
-            GATE: (GATE_ONE, GATE_TWO),
-            OUTPUT: (OUT,),
-            UP: (UP_ONE, UP_TWO),
-            QUERY: (ASK,),
-            DOWN: (DOWN_ONE, DOWN_TWO),
-        }
         for number in numbers:
             repack(r, number, *(sums[piece] for piece in pieces[number]))
-            late[number] = late_second(r, number)
+            for step in (1, 2, 3):
+                second_rings[number].start(step)
 
     def go_on(*numbers):
         for number in numbers:
-            late[number] = late_first(r, number, late[number])
+            late_line(r, number, second_rings[number])
+            for step in (1, 2, 3):
+                first_rings[number].start(step)
 
     def finish(*numbers):
         outs = (r.fgate, r.foutput, r.fup, r.fquery, r.fdown)
         for number in numbers:
-            late_end(r, number, late[number], outs[number])
+            late_end(r, number, first_rings[number], outs[number])
 
     rest_back = feed_forward_back(r, spreads, shared, start)
     thirds, third_specials = attention_back(r, lambda number: None)
-    queries_back(r, spreads, shared)
+    query_back = queries_back(r, spreads, shared)
     rest_back()
+    query_back()
     start(GATE_TWO, UP_TWO, OUT, ASK)
     for ring in early_rings:
         ring.sent()
@@ -1621,17 +1637,24 @@
     relay(OUT, ASK)
     for copy in early_held:
         copy.sent()
-    keys_values_back(r, split_shared)
+    prepare_late()
+    core = lax.axis_index("dp")
+
+    def on(which, action, *numbers):
+        pl.when(core == which)(lambda: action(*numbers))
+
+    keys_values_back(r, split_shared, lambda: on(1, send_late, DOWN, GATE, UP, OUTPUT, QUERY))
 
     def one():
         r.links.settle(before)
-        send_late(DOWN, GATE, UP)
+        on(0, send_late, DOWN, GATE, UP)
 
     def two():
-        send_late(OUTPUT, QUERY)
+        on(0, send_late, OUTPUT, QUERY)
+        on(1, go_on, DOWN, GATE, UP, OUTPUT, QUERY)
 
     def three():
-        go_on(DOWN, GATE, UP, OUTPUT, QUERY)
+        on(0, go_on, DOWN, GATE, UP, OUTPUT, QUERY)
 
     small_sums(r, (one, two, three))
     finish(DOWN, GATE, UP, OUTPUT, QUERY)

time: 144 us -> 139 us (0.965)
  Pallas kernels: 143 us -> 138 us
    pallas_call x2, Pallas kernels: 143 us -> 138 us  [run(): pl.pallas_call(kernel, out_shape=[jax.ShapeDtypeStruct(out.shape, out.dty...]
where the time goes in v5:
time: 139 us
  Pallas kernels  138 us (99%)
    pallas_call x2, Pallas kernels, run(): pl.pallas_call(kernel, out_shape=[jax.ShapeDtypeStruct(out.shape, out.dty...  138 us

profile of v5, /device:TPU:0, one launch (start us, length us, event | category | flops | bytes accessed | tf_op | source)
XLA Modules:
  0.0 138.9 jit_solution(18084861851091563366)
XLA Ops:
  0.7 136.1 %shard_map.298 = (bf16[128,640]{1,0:T(8,128)(2,1)}, bf16[128,640]{1,0:T(8,128)(2,1)}, f32[80,128]{1,0:T(8,128)}, f32[48,128]{1,0:T(8,128)}, f32[80,128]{1,0:T(8,...) custom-call(s32[128]{0:T(128)} %refs_0_.1, s32[1,8]{1,0:T(1,128)} %refs_1_.1, ...), custom_call_target="tpu_custom_call" | custom-call | tf_op jit(solution)/shard_map/pallas_call | solution.py:200
  136.8 1.9 %shard_map.299 = (bf16[1,128,640]{2,1,0:T(8,128)(2,1)}, bf16[1,128,640]{2,1,0:T(8,128)(2,1)}, f32[1,5]{1,0:T(1,128)}, f32[5,1024]{1,0:T(8,128)}, f32[5,256]{1,0:...) custom-call(bf16[128,640]{1,0:T(8,128)(2,1)} %get-tuple-element.38.r, ...), custom_call_target="tpu_custom_call" | custom-call | tf_op jit(solution)/shard_map/pallas_call | solution.py:200

commit v6 on v5

--- a/solution.py
+++ b/solution.py
@@ -1632,9 +1632,8 @@
     seconds = scatter_second(r, thirds, third_specials)
     relay(DOWN_ONE, GATE_ONE, UP_ONE)
     firsts = scatter_first(r, seconds)
-    relay(DOWN_TWO, GATE_TWO, UP_TWO)
+    relay(DOWN_TWO, GATE_TWO, UP_TWO, OUT, ASK)
     scatter_end(r, firsts)
-    relay(OUT, ASK)
     for copy in early_held:
         copy.sent()
     prepare_late()
@@ -1647,14 +1646,14 @@
 
     def one():
         r.links.settle(before)
-        on(0, send_late, DOWN, GATE, UP)
+        on(0, send_late, DOWN, GATE, UP, OUTPUT, QUERY)
+        on(1, go_on, DOWN, GATE, UP, OUTPUT, QUERY)
 
     def two():
-        on(0, send_late, OUTPUT, QUERY)
-        on(1, go_on, DOWN, GATE, UP, OUTPUT, QUERY)
+        on(0, go_on, DOWN, GATE, UP)
 
     def three():
-        on(0, go_on, DOWN, GATE, UP, OUTPUT, QUERY)
+        on(0, go_on, OUTPUT, QUERY)
 
     small_sums(r, (one, two, three))
     finish(DOWN, GATE, UP, OUTPUT, QUERY)

time: 139 us -> 138 us (level)
  no operation moved by 1% of the time
where the time goes in v6:
time: 138 us
  Pallas kernels  137 us (99%)
    pallas_call x2, Pallas kernels, run(): pl.pallas_call(kernel, out_shape=[jax.ShapeDtypeStruct(out.shape, out.dty...  137 us

profile of v6, /device:TPU:0, one launch (start us, length us, event | category | flops | bytes accessed | tf_op | source)
XLA Modules:
  0.0 137.6 jit_solution(14726939003769751532)
XLA Ops:
  0.7 134.9 %shard_map.298 = (bf16[128,640]{1,0:T(8,128)(2,1)}, bf16[128,640]{1,0:T(8,128)(2,1)}, f32[80,128]{1,0:T(8,128)}, f32[48,128]{1,0:T(8,128)}, f32[80,128]{1,0:T(8,...) custom-call(s32[128]{0:T(128)} %refs_0_.1, s32[1,8]{1,0:T(1,128)} %refs_1_.1, ...), custom_call_target="tpu_custom_call" | custom-call | tf_op jit(solution)/shard_map/pallas_call | solution.py:200
  135.6 1.9 %shard_map.299 = (bf16[1,128,640]{2,1,0:T(8,128)(2,1)}, bf16[1,128,640]{2,1,0:T(8,128)(2,1)}, f32[1,5]{1,0:T(1,128)}, f32[5,1024]{1,0:T(8,128)}, f32[5,256]{1,0:...) custom-call(bf16[128,640]{1,0:T(8,128)(2,1)} %get-tuple-element.38.r, ...), custom_call_target="tpu_custom_call" | custom-call | tf_op jit(solution)/shard_map/pallas_call | solution.py:200

commit v7 on v6

--- a/solution.py
+++ b/solution.py
@@ -1645,9 +1645,9 @@
     keys_values_back(r, split_shared, lambda: on(1, send_late, DOWN, GATE, UP, OUTPUT, QUERY))
 
     def one():
-        r.links.settle(before)
         on(0, send_late, DOWN, GATE, UP, OUTPUT, QUERY)
         on(1, go_on, DOWN, GATE, UP, OUTPUT, QUERY)
+        r.links.settle(before)
 
     def two():
         on(0, go_on, DOWN, GATE, UP)

time: 138 us -> 138 us (level)
  no operation moved by 1% of the time
where the time goes in v7:
time: 138 us
  Pallas kernels  137 us (99%)
    pallas_call x2, Pallas kernels, run(): pl.pallas_call(kernel, out_shape=[jax.ShapeDtypeStruct(out.shape, out.dty...  137 us

profile of v7, /device:TPU:0, one launch (start us, length us, event | category | flops | bytes accessed | tf_op | source)
XLA Modules:
  0.0 137.7 jit_solution(3713015098126525588)
XLA Ops:
  0.7 135.0 %shard_map.298 = (bf16[128,640]{1,0:T(8,128)(2,1)}, bf16[128,640]{1,0:T(8,128)(2,1)}, f32[80,128]{1,0:T(8,128)}, f32[48,128]{1,0:T(8,128)}, f32[80,128]{1,0:T(8,...) custom-call(s32[128]{0:T(128)} %refs_0_.1, s32[1,8]{1,0:T(1,128)} %refs_1_.1, ...), custom_call_target="tpu_custom_call" | custom-call | tf_op jit(solution)/shard_map/pallas_call | solution.py:200
  135.6 1.9 %shard_map.299 = (bf16[1,128,640]{2,1,0:T(8,128)(2,1)}, bf16[1,128,640]{2,1,0:T(8,128)(2,1)}, f32[1,5]{1,0:T(1,128)}, f32[5,1024]{1,0:T(8,128)}, f32[5,256]{1,0:...) custom-call(bf16[128,640]{1,0:T(8,128)(2,1)} %get-tuple-element.38.r, ...), custom_call_target="tpu_custom_call" | custom-call | tf_op jit(solution)/shard_map/pallas_call | solution.py:200
